TPU v7x, 256 devices: a whole 4x4x8 slice. The times are simulated.
256 devices in a mesh: energy: 8 (over y, core), rows: 32 (over z, x).
Axes of the slice: x: 4, y: 4, z: 8, core: 2. Of those that a mesh axis runs over, the one named last changes fastest.
Arguments:
- panels: bfloat16 [8, 256, 2, 128, 256], P('energy', 'rows'), may hold values from -0.029907227 to 0.029907227
- energy_weight: float32 [8], P('energy'), may hold values from 0.1 to 1
- block_orbitals: int32 [256], replicated, may hold values from 40 to 64, as said below
- pattern_columns: int32 [256, 6], P('rows'), may hold values from 0 to 255, as said below
- request_source: int32 [4096, 1], replicated, may hold values from 0 to 31; in each aligned block of 16 rows (0 to 15, 16 to 31, ...) at most 2 rows name the same one
- request_local: int32 [4096], replicated, may hold values from 0 to 7
- orbital_values: bfloat16 [4096, 384, 128], P(('energy', 'rows')), may hold values from -6 to 6
Outputs:
- density: float32 [4, 32768], P(None, ('energy', 'rows'))
Inputs may be any that keep to these rules, and one draw needn't show every extreme that they name: `block_orbitals`: some block has exactly 64 live orbitals. `pattern_columns`: row i lists block i first, then 6 - 1 distinct other blocks, each within 8 blocks of i. `request_source`: among the 16 requests of one device no rows index appears more than 2 times, and some device has a rows index exactly 2 times.
All inputs are finite; a program needn't handle non-finite values.
Results may differ from a plain program's by a relative error of at most 0.0045.
Values may be sent and summed in bfloat16 or wider, within the bound.
No kernel may reach another device: no remote copies, remote signals or barrier semaphores. Data moves between devices by JAX's collectives and lax.ppermute only.
A program may use at most 128 MiB of HBM per device.

v0:
```python
import jax
import jax.numpy as jnp
from jax import lax
from jax.sharding import PartitionSpec as P


def with_halo(block, sides, width):
    for axis, dim in sides:
        count = lax.axis_size(axis)
        forward = [(i, i + 1) for i in range(count - 1)]
        backward = [(target, source) for source, target in forward]
        low = lax.ppermute(
            lax.slice_in_dim(block, block.shape[dim] - width, None, axis=dim), axis, forward
        )
        high = lax.ppermute(lax.slice_in_dim(block, 0, width, axis=dim), axis, backward)
        block = jnp.concatenate([low, block, high], axis=dim)
    return block


def spin_parts(real_part, imag_part):
    block_width = real_part.shape[-1] // 2
    new_shape = real_part.shape[:-3] + (2, block_width, real_part.shape[-2], 2, block_width)
    real_view = real_part.reshape(new_shape)
    imag_view = imag_part.reshape(new_shape)
    charge = real_view[..., 0, :, :, 0, :] + real_view[..., 1, :, :, 1, :]
    moment_first = real_view[..., 0, :, :, 1, :] + real_view[..., 1, :, :, 0, :]
    moment_second = imag_view[..., 1, :, :, 0, :] - imag_view[..., 0, :, :, 1, :]
    moment_third = real_view[..., 0, :, :, 0, :] - real_view[..., 1, :, :, 1, :]
    return jnp.stack([charge, moment_first, moment_second, moment_third], axis=-4)


def local(
    panels,
    energy_weight,
    block_orbitals,
    pattern_columns,
    request_source,
    request_local,
    orbital_values,
):
    block_width = panels.shape[3] // 2
    own_blocks = panels.shape[1]
    pattern_width = pattern_columns.shape[1]
    request_count = orbital_values.shape[0]
    rows_count = lax.axis_size("rows")
    rows_index = lax.axis_index("rows")
    energy_index = lax.axis_index("energy")
    first_block = rows_index * own_blocks
    own_counts = lax.dynamic_slice_in_dim(block_orbitals, first_block, own_blocks)
    orbital_index = jnp.arange(2 * block_width) % block_width
    kept_mask = (orbital_index[None, :] < own_counts[:, None]).astype(panels.dtype)
    masked = panels * kept_mask[None, :, None, :, None]
    extended = with_halo(masked, (("rows", 1),), own_blocks)
    offsets = (pattern_columns - first_block + own_blocks).reshape(-1)
    column_panel = jnp.take(extended[0], offsets, axis=0).reshape(
        (own_blocks, pattern_width) + panels.shape[2:]
    )
    row_panel = masked[0]
    left_side = jnp.stack(
        [
            jnp.concatenate([row_panel[:, 0], row_panel[:, 1]], axis=-1),
            jnp.concatenate([row_panel[:, 1], -row_panel[:, 0]], axis=-1),
        ],
        axis=1,
    )
    right_side = jnp.concatenate([column_panel[:, :, 0], column_panel[:, :, 1]], axis=-1)
    product = jnp.einsum(
        "icak,inbk->icanb", left_side, right_side, preferred_element_type=jnp.float32
    )
    spin_blocks = spin_parts(product[:, 0], product[:, 1])
    partial_value = (energy_weight[0] * spin_blocks).astype(jnp.bfloat16)
    partial_value = lax.optimization_barrier(partial_value).astype(jnp.float32)
    summed = lax.psum(partial_value.astype(jnp.bfloat16), "energy")
    density_rows = summed.reshape(own_blocks, 4 * block_width, pattern_width * block_width)
    row_shape = density_rows.shape[1:]
    capacity = max(2, 2 * request_count // rows_count)
    device_table = request_source[:, 0].reshape(-1, request_count)
    local_table = request_local.reshape(-1, request_count)
    own_device = energy_index * rows_count + rows_index
    my_sources = lax.dynamic_index_in_dim(device_table, own_device, 0, keepdims=False)
    request_ids = jnp.arange(request_count)
    same_source = my_sources[:, None] == my_sources[None, :]
    my_ranks = jnp.sum(same_source & (request_ids[None, :] < request_ids[:, None]), axis=1)
    slot_ids = jnp.arange(capacity)
    orbital_rows = orbital_values[:, :block_width].astype(jnp.float32)
    group_sources = lax.dynamic_slice_in_dim(device_table, energy_index * rows_count, rows_count, 0)
    group_locals = lax.dynamic_slice_in_dim(local_table, energy_index * rows_count, rows_count, 0)
    mine_flag = group_sources == rows_index
    group_ranks = jnp.cumsum(mine_flag.astype(jnp.int32), axis=1) - 1
    matched = mine_flag[:, :, None] & (group_ranks[:, :, None] == slot_ids[None, None, :])
    send_local = jnp.sum(jnp.where(matched, group_locals[:, :, None], 0), axis=1)
    send_valid = jnp.any(matched, axis=1)
    outgoing = jnp.take(density_rows, send_local.reshape(-1), axis=0).reshape(
        (rows_count, capacity) + row_shape
    )
    outgoing = outgoing * send_valid[:, :, None, None].astype(outgoing.dtype)
    incoming = lax.all_to_all(outgoing, "rows", split_axis=0, concat_axis=0, tiled=True)
    wanted_rows = jnp.take(
        incoming.reshape((rows_count * capacity,) + row_shape),
        my_sources * capacity + my_ranks,
        axis=0,
    )
    applied = jnp.einsum(
        "rab,rbp->rap", wanted_rows, orbital_values, preferred_element_type=jnp.float32
    )
    applied = applied.reshape(request_count, 4, block_width, -1)
    density = jnp.sum(orbital_rows[:, None] * applied, axis=(0, 2))
    return density


def solution(mesh):
    in_specs = (
        P("energy", "rows", None, None, None),
        P("energy"),
        P(),
        P("rows", None),
        P(),
        P(),
        P(("energy", "rows"), None, None),
    )
    out_specs = P(None, ("energy", "rows"))
    return jax.shard_map(local, mesh=mesh, in_specs=in_specs, out_specs=out_specs, check_vma=False)
```

profile of v0, /device:TPU:127, one launch (start us, length us, event | category | flops | bytes accessed | tf_op | source)
XLA Modules:
  0.0 559.6 jit_solution(14559058766305022216)
XLA Ops:
  6.6 0.8 dynamic_slice.16
  7.4 1.4 copy_multiply_fusion
  8.9 4.7 collective-permute-start
  13.5 1.9 collective-permute-start.1
  15.5 1.4 fusion.29
  17.0 0.5 broadcast.186
  17.5 0.7 reduce.5
  19.5 1.5 maximum_bitcast_fusion.5
  21.0 14.3 %collective-permute-done = bf16[1,8,2,128,256]{4,3,1,2,0:T(8,128)(2,1)S(1)} collective-permute-done((bf16[1,8,2,128,256]{4,3,1,2,0:T(8,128)(2,1)S(1)}, bf16[1,8,2,128,256]{4,3,1,2,0:T(8,128)(2,1)S(1)}, u32[]{:S(2)}, u32[]{:S(2)}) %collective-permute-start) | collective-permute-done | bytes 1048608 | tf_op jit(solution)/shard_map/ppermute | solution.py:12
  35.3 1.0 copy-done.10
  36.3 6.2 %collective-permute-done.1 = bf16[1,8,2,128,256]{4,3,1,2,0:T(8,128)(2,1)} collective-permute-done((bf16[1,8,2,128,256]{4,3,1,2,0:T(8,128)(2,1)S(1)}, bf16[1,8,2,128,256]{4,3,1,2,0:T(8,128)(2,1)}, u32[]{:S(2)}, u32[]{:S(2)}) %collective-permute-start.1) | collective-permute-done | bytes 1048608 | tf_op jit(solution)/shard_map/ppermute | solution.py:15
  42.6 2.0 maximum_bitcast_fusion.2
  44.6 5.0 gather_fusion
  49.5 3.2 copy.42
  52.8 0.7 broadcast_select_fusion
  53.5 0.8 slice_bitcast_fusion.1
  54.3 0.4 copy-done.8
  54.7 0.3 copy-done.9
  55.0 1.8 fusion
  56.9 2.3 fusion.26
  59.2 7.1 %reshape_squeeze.10 = f32[8,2,64,6,2,64]{5,4,2,1,3,0:T(2,128)} reshape(f32[8,1,128,6,128]{4,2,3,1,0:T(8,128)} %get-tuple-element.14) | data formatting | bytes 6291456 | tf_op jit(solution)/shard_map/reshape;squeeze | solution.py:23
  66.3 11.5 %fusion.24 = (f32[8,1,64,6,1,64]{5,4,2,1,3,0:T(1,128)}, f32[8,1,64,6,1,64]{5,4,2,1,3,0:T(1,128)}, f32[8,1,64,6,1,64]{5,4,2,1,3,0:T(1,128)}, f32[8,1,64,6,1,64]{5,4,2,1,3,0:T(1,128)}) fusion(f32[8,2,64,6,2,64]{5,4,2,1,3,0:T(2,128)} %reshape_squeeze.10), kind=kLoop, calls=%fused_computation.65 | loop fusion | bytes 6291456 | tf_op jit(solution)/shard_map/slice | solution.py:26
  77.8 4.9 copy.57
  82.6 4.9 copy.58
  87.5 5.0 reshape_squeeze.11
  92.5 7.3 %fusion.25 = (f32[8,1,64,6,1,64]{5,4,2,1,3,0:T(1,128)}, f32[8,1,64,6,1,64]{5,4,2,1,3,0:T(1,128)S(1)}) fusion(f32[8,2,64,6,2,64]{5,4,2,1,3,0:T(2,128)} %reshape_squeeze.11), kind=kLoop, calls=%fused_computation.66 | loop fusion | bytes 3145728 | tf_op jit(solution)/shard_map/slice | solution.py:27
  99.8 2.8 copy.59
  102.6 4.9 copy.60
  107.5 2.7 copy.55
  110.3 2.7 copy.56
  113.0 1.8 add.155
  114.9 0.5 copy-done.5
  115.4 0.3 sub.39
  115.7 1.1 copy-done.4
  116.8 0.5 copy-done.6
  117.2 0.6 fusion.27
  117.8 7.8 %fusion.3 = bf16[8,4,64,6,64]{2,1,4,3,0:T(4,128)(2,1)S(1)} fusion(f32[8,1,64,6,64]{2,1,4,3,0:T(1,128)S(1)} %bitcast.80, f32[8,1,64,6,64]{2,1,4,3,0:T(1,128)S(1)} %bitcast.78, f32[8,1,64,6,64]{2,1,4,3,0:T(1,128)S(1)} %bitcast.77, f32[8,1,64,6,64]{2,1,4,3,0:T(1,128)S(1)} %bitcast.79, f32[]{:T(128)} %bitcast.74), kind=kLoop, calls=%fused_computation.9 | loop fusion | flops 3932160 | bytes 4718596 | tf_op jit(solution)/shard_map/convert_element_type | solution.py:71
  125.6 3.0 reshape.258
  129.2 67.5 %all-reduce.2.cloned.1.call-done = bf16[8,256,384]{1,2,0:T(8,128)(2,1)} async-done(((bf16[8,256,384]{1,2,0:T(8,128)(2,1)}), bf16[8,256,384]{1,2,0:T(8,128)(2,1)}) %all-reduce.2.cloned.1.call-update) | async-done | bytes 1572880 | tf_op jit(solution)/shard_map/psum | solution.py:73
  196.7 8.3 %gather_fusion.1 = bf16[64,256,384]{1,2,0:T(8,128)(2,1)} fusion(bf16[8,256,384]{1,2,0:T(8,128)(2,1)} %all-reduce.2.cloned.1.call-done, s32[1024]{0:T(1024)S(1)} %pad_clamp_fusion.1), kind=kCustom, calls=%fused_computation.1 | custom fusion | bytes 25166080 | tf_op jit(solution)/shard_map/jit(_take)/gather | solution.py:93
  205.1 16.6 %copy.51 = bf16[32,2,256,384]{3,2,1,0:T(8,128)(2,1)} copy(bf16[32,2,256,384]{2,3,1,0:T(8,128)(2,1)} %bitcast.75) | data formatting | bytes 25165824 | tf_op jit(solution)/shard_map/jit(_take)/gather | solution.py:93
  221.7 10.9 %select_multiply_fusion = bf16[32,2,256,384]{3,2,1,0:T(8,128)(2,1)} fusion(bf16[32,2,256,384]{3,2,1,0:T(8,128)(2,1)} %copy.51, pred[32,2]{1,0:T(8,128)(4,1)S(1)} %copy.39, bf16[32,2]{1,0:T(8,128)(2,1)S(1)} %copy.52), kind=kLoop, calls=%fused_computation.3 | loop fusion | flops 12582912 | bytes 25166016 | tf_op jit(solution)/shard_map/mul | solution.py:96
  232.6 9.4 %all-to-all-start = ((bf16[32,2,256,384]{3,2,1,0:T(8,128)(2,1)}), bf16[32,2,256,384]{3,2,1,0:T(8,128)(2,1)}, u32[]{:S(2)}, u32[]{:S(2)}) async-start(bf16[32,2,256,384]{3,2,1,0:T(8,128)(2,1)} %select_multiply_fusion), calls=%async_computation | async-start | bytes 25165824 | tf_op jit(solution)/shard_map/all_to_all | solution.py:97
  242.3 1.8 slice_convert_fusion
  244.1 299.7 %all-to-all-done = bf16[32,2,256,384]{3,2,1,0:T(8,128)(2,1)} async-done(((bf16[32,2,256,384]{3,2,1,0:T(8,128)(2,1)}), bf16[32,2,256,384]{3,2,1,0:T(8,128)(2,1)}, u32[]{:S(2)}, u32[]{:S(2)}) %all-to-all-start) | async-done | bytes 12582944 | tf_op jit(solution)/shard_map/all_to_all | solution.py:97
  543.8 5.8 %gather_fusion.2 = bf16[16,256,384]{2,1,0:T(8,128)(2,1)S(1)} fusion(bf16[64,256,384]{2,1,0:T(8,128)(2,1)} %bitcast.25, s32[1024]{0:T(1024)S(1)} %pad_clamp_fusion), kind=kCustom, calls=%fused_computation.2 | custom fusion | bytes 6291520 | tf_op jit(solution)/shard_map/jit(_take)/gather | solution.py:98
  549.6 2.6 fusion.9
  552.2 0.6 bitcast_reduce_fusion
  (57 shorter events, 1.7 us)
Async XLA Ops:
  6.5 10.4 %copy-start.13 = (s32[8,6]{1,0:T(8,128)S(1)}, s32[8,6]{1,0:T(8,128)}, u32[]{:S(2)}) copy-start(s32[8,6]{1,0:T(8,128)} %param.10) | copy-start | bytes 580
  6.5 11.0 %copy-start.12 = (s32[4096,1]{0,1:T(1,128)S(1)}, s32[4096,1]{0,1:T(1,128)}, u32[]{:S(2)}) copy-start(s32[4096,1]{0,1:T(1,128)} %param.11) | copy-start | bytes 49156
  6.5 12.7 %copy-start.11 = (s32[4096]{0:T(1024)S(1)}, s32[4096]{0:T(1024)}, u32[]{:S(2)}) copy-start(s32[4096]{0:T(1024)} %param.12) | copy-start | bytes 49156
  6.5 190.2 %all-reduce.2.cloned.1.call-start = ((), (), s32[]{:S(2)}) async-start(), calls=%async_computation.1 | async-start | bytes 3145728 | tf_op jit(solution)/shard_map/psum | solution.py:73
  8.8 12.2 %copy-start.7 = (bf16[1,8,2,128,256]{4,3,1,2,0:T(8,128)(2,1)}, bf16[1,8,2,128,256]{4,3,1,2,0:T(8,128)(2,1)S(1)}, u32[]{:S(2)}) copy-start(bf16[1,8,2,128,256]{4,3,1,2,0:T(8,128)(2,1)S(1)} %copy_multiply_fusion) | copy-start | bytes 3145732
  8.9 26.5 %collective-permute-start = (bf16[1,8,2,128,256]{4,3,1,2,0:T(8,128)(2,1)S(1)}, bf16[1,8,2,128,256]{4,3,1,2,0:T(8,128)(2,1)S(1)}, u32[]{:S(2)}, u32[]{:S(2)}) collective-permute-start(bf16[1,8,2,128,256]{4,3,1,2,0:T(8,128)(2,1)S(1)} %copy_multiply_fusion), channel_id=1, source_target_pairs={{0,1},{1,2},{2,3},{3,4},{4,5},{5,6},{6,7},{7,8},{8,9},{9,10},{10,1... | collective-permute-start | bytes 3145736 | tf_op jit(solution)/shard_map/ppermute | solution.py:12
  13.5 29.0 %collective-permute-start.1 = (bf16[1,8,2,128,256]{4,3,1,2,0:T(8,128)(2,1)S(1)}, bf16[1,8,2,128,256]{4,3,1,2,0:T(8,128)(2,1)}, u32[]{:S(2)}, u32[]{:S(2)}) collective-permute-start(bf16[1,8,2,128,256]{4,3,1,2,0:T(8,128)(2,1)S(1)} %copy_multiply_fusion), channel_id=1, source_target_pairs={{1,0},{2,1},{3,2},{4,3},{5,4},{6,5},{7,6},{8,7},{9,8},{10,9},{11,1... | collective-permute-start | bytes 3145736 | tf_op jit(solution)/shard_map/ppermute | solution.py:15
  35.3 1.0 copy-start.10
  53.5 1.2 copy-start.8
  53.5 1.5 copy-start.9
  99.8 7.7 %copy-start.1 = (f32[8,1,64,6,1,64]{5,4,2,1,3,0:T(1,128)S(1)}, f32[8,1,64,6,1,64]{5,4,2,1,3,0:T(1,128)}, u32[]{:S(2)}) copy-start(f32[8,1,64,6,1,64]{5,4,2,1,3,0:T(1,128)} %get-tuple-element.10) | copy-start | bytes 2359300
  102.6 7.7 %copy-start = (f32[8,1,64,6,1,64]{5,4,2,1,3,0:T(1,128)S(1)}, f32[8,1,64,6,1,64]{5,4,2,1,3,0:T(1,128)}, u32[]{:S(2)}) copy-start(f32[8,1,64,6,1,64]{5,4,2,1,3,0:T(1,128)} %get-tuple-element.9) | copy-start | bytes 2359300
  110.3 2.7 copy-start.2
  113.0 1.9 copy-start.3
  113.0 2.4 copy-start.5
  115.4 1.4 copy-start.4
  115.4 1.9 copy-start.6
  232.6 311.1 %all-to-all-start = ((bf16[32,2,256,384]{3,2,1,0:T(8,128)(2,1)}), bf16[32,2,256,384]{3,2,1,0:T(8,128)(2,1)}, u32[]{:S(2)}, u32[]{:S(2)}) async-start(bf16[32,2,256,384]{3,2,1,0:T(8,128)(2,1)} %select_multiply_fusion), calls=%async_computation | async-start | bytes 25165824 | tf_op jit(solution)/shard_map/all_to_all | solution.py:97
Sparse Core Ops, SparseCore 0:
  128.7 67.9 all-reduce.1
where the time goes:
time: 561 us; the launch traced here: 560 us
  waiting for transfers between devices  388 us (69%)
  local copies, waits for them, and re-layouts  105 us (19%)
  other arithmetic  32.3 us (6%)
  starting transfers between devices  16 us (3%)
  between operations  14.4 us (3%)
    all_to_all x1, waiting for transfers between devices, local(): lax.all_to_all(outgoing, 'rows', split_axis=0, concat_axis=0, tiled=True)  300 us
    psum x1, waiting for transfers between devices, local(): summed = lax.psum(partial_value.astype(jnp.bfloat16), 'energy')  67.5 us
    unnamed x35, local copies, waits for them, and re-layouts  27.2 us
    gather x2, local copies, waits for them, and re-layouts, local(): jnp.take(density_rows, send_local.reshape(-1), axis=0)  25 us
    ppermute x1, waiting for transfers between devices, with_halo(): lax.ppermute(lax.slice_in_dim(block, block.shape[dim] - width, None, axis...  14.3 us
    slice x1, local copies, waits for them, and re-layouts, spin_parts(): moment_first = real_view[..., 0, :, :, 1, :] + real_view[..., 1, :, :, 0, :]  11.5 us
  transfers between devices with their start and end apart: 4, of which 4 were waited for; matrix products, arithmetic and copies ran while one was open for 1% of the time, Pallas kernels for 0%

commit v1 on v0

v1 whole, which is shorter than its diff:
```python
import functools

import jax
import jax.numpy as jnp
from jax import lax
from jax.experimental import pallas as pl
from jax.experimental.pallas import tpu as pltpu
from jax.sharding import Mesh, PartitionSpec as P

NT = (((1,), (1,)), ((), ()))
TN = (((0,), (0,)), ((), ()))
VMEM_LIMIT = 56 * 1024 * 1024


def product_kernel(place, pattern, live, weight, own, prev, nxt, mine, theirs, ext, sems):
    copies = [
        pltpu.make_async_copy(src, ext.at[pl.ds(8 * n, 8)], sems.at[n])
        for n, src in enumerate((prev, own, nxt))
    ]
    for copy in copies:
        copy.start()
    for copy in copies:
        copy.wait()
    first = place[0]
    core = place[1]
    scale = weight[0]
    lane = lax.broadcasted_iota(jnp.int32, (64, 256), 1)
    row = lax.broadcasted_iota(jnp.int32, (64, 256), 0)
    half = jnp.where(lane < 128, core, 1 - core)
    orbital = half * 32 + lane % 32
    starts = (core * 32, (1 - core) * 32)

    def one(i, carry):
        def piece(part, spin, t):
            at = pl.multiple_of(spin * 64 + starts[t], 32)
            return ext[8 + i, part, pl.ds(at, 32), :]

        def stack(parts):
            return jnp.concatenate(
                [piece(part, spin, t) * sign for t in range(2) for part, spin, sign in parts], axis=0
            )

        one_ = jnp.asarray(1, jnp.bfloat16)
        neg = jnp.asarray(-1, jnp.bfloat16)
        sides = {
            (0, 0): stack([(0, 0, one_), (0, 1, one_), (0, 0, one_), (1, 1, one_)]),
            (0, 1): stack([(1, 0, one_), (1, 1, one_), (1, 0, one_), (0, 1, neg)]),
            (1, 0): stack([(0, 1, one_), (0, 0, one_), (0, 1, neg), (1, 0, neg)]),
            (1, 1): stack([(1, 1, one_), (1, 0, one_), (1, 1, neg), (0, 0, one_)]),
        }
        columns = [pattern[i, k] for k in range(6)]
        total = None
        for (spin, part), side in sides.items():
            left = jnp.concatenate(
                [ext[c - first + 8, part, pl.ds(spin * 64, 64), :] for c in columns], axis=0
            )
            term = lax.dot_general(left, side, NT, preferred_element_type=jnp.float32)
            total = term if total is None else total + term
        kept_row = orbital < live[first + i]
        pieces = []
        for k, c in enumerate(columns):
            kept = kept_row & (row < live[c])
            pieces.append(jnp.where(kept, total[64 * k : 64 * k + 64] * scale, 0.0))
        rounded = jnp.concatenate(pieces, axis=0).astype(jnp.bfloat16)
        for ref, at in ((mine, 0), (theirs, 128)):
            ref[i // 2, :, i % 2] = rounded[:, at : at + 128].reshape(8, 48, 128)
        return carry

    lax.fori_loop(0, 8, one, 0)


def products(place, pattern, live, weight, own, prev, nxt):
    smem = pl.BlockSpec(memory_space=pltpu.SMEM)
    hbm = pl.BlockSpec(memory_space=pl.ANY)
    shape = jax.ShapeDtypeStruct((4, 8, 2, 48, 128), jnp.bfloat16)
    return pl.pallas_call(
        product_kernel,
        out_shape=(shape, shape),
        in_specs=[smem] * 4 + [hbm] * 3,
        out_specs=(pl.BlockSpec(memory_space=pltpu.VMEM),) * 2,
        scratch_shapes=[
            pltpu.VMEM((24, 2, 128, 256), jnp.bfloat16),
            pltpu.SemaphoreType.DMA((3,)),
        ],
        compiler_params=pltpu.CompilerParams(vmem_limit_bytes=VMEM_LIMIT),
        cost_estimate=pl.CostEstimate(flops=1_600_000_000, bytes_accessed=5_000_000, transcendentals=0),
        name="products",
    )(place, pattern, live, weight, own, prev, nxt)


def apply_kernel(place, source, local, own_q, other_q, vals_o, *rest):
    shards, out, rows, sems = rest[:8], rest[8], rest[9], rest[10]
    z = pl.program_id(0)
    core, y_at, x_at = place[1], place[2], place[3]

    @pl.when(z == 0)
    def _():
        copies = [
            pltpu.make_async_copy(shard, rows.at[n], sems.at[n]) for n, shard in enumerate(shards)
        ]
        for copy in copies:
            copy.start()
        for copy in copies:
            copy.wait()

    for t in range(2):
        owner = jnp.where(core == 0, t, 1 - t)
        device = (2 * y_at + owner) * 32 + 4 * z + x_at
        vals_q = own_q if t == 0 else other_q

        total = jnp.zeros((4, 32, 128), jnp.float32)
        for r in range(16):
            request = device * 16 + r
            src = source[request]
            loc = local[request]
            dx = (x_at - src % 4) & 3
            dy = (y_at - loc // 2) & 3
            odd = loc % 2
            outer = jnp.where(odd == 0, dy, 4 + dx)
            inner = jnp.where(odd == 0, dx, dy)
            side = rows[outer, inner, src // 4]
            applied = lax.dot_general(side, vals_q[0, r], TN, preferred_element_type=jnp.float32)
            weights = vals_o[0, t, r].astype(jnp.float32)
            total = total + applied.reshape(4, 32, 128) * weights[None]
        sums = jnp.sum(total, axis=1)
        for at, c in enumerate((0, 1, 3, 2)):
            out[0, t, pl.ds(c, 1)] = sums[at : at + 1]


def applied_sums(place, source, local, own_q, other_q, vals_o, shards):
    smem = pl.BlockSpec(memory_space=pltpu.SMEM)
    hbm = pl.BlockSpec(memory_space=pl.ANY)
    by_z = pl.BlockSpec((1, 16, 48, 128), lambda z: (z, 0, 0, 0))
    return pl.pallas_call(
        apply_kernel,
        grid=(8,),
        out_shape=jax.ShapeDtypeStruct((8, 2, 4, 128), jnp.float32),
        in_specs=[smem] * 3
        + [by_z, by_z, pl.BlockSpec((1, 2, 16, 32, 128), lambda z: (z, 0, 0, 0, 0))]
        + [hbm] * 8,
        out_specs=pl.BlockSpec((1, 2, 4, 128), lambda z: (z, 0, 0, 0)),
        scratch_shapes=[
            pltpu.VMEM((8, 4, 8, 48, 128), jnp.bfloat16),
            pltpu.SemaphoreType.DMA((8,)),
        ],
        compiler_params=pltpu.CompilerParams(vmem_limit_bytes=VMEM_LIMIT),
        cost_estimate=pl.CostEstimate(flops=400_000_000, bytes_accessed=8_000_000, transcendentals=0),
        name="applied_sums",
    )(place, source, local, own_q, other_q, vals_o, *shards)


def shifted(value, axis, by):
    count = lax.axis_size(axis)
    return lax.ppermute(value, axis, [(n, (n + by) % count) for n in range(count)])


def gathered(value, axis):
    return [value] + [shifted(value, axis, d) for d in (1, 2, 3)]


def local_program(panels, energy_weight, block_orbitals, pattern_columns, request_source, request_local, orbital_values):
    core = lax.axis_index("core")
    y_at, z_at, x_at = lax.axis_index("y"), lax.axis_index("z"), lax.axis_index("x")
    place = jnp.stack([(z_at * 4 + x_at) * 8, core, y_at, x_at]).astype(jnp.int32)
    own = panels[0]
    forward = [(n, n + 1) for n in range(31)]
    backward = [(n + 1, n) for n in range(31)]
    swap = [(0, 1), (1, 0)]
    prev = lax.ppermute(own, ("z", "x"), forward)
    nxt = lax.ppermute(own, ("z", "x"), backward)

    values_o = orbital_values[:, :64].reshape(16, 2, 32, 128)
    keep_o = lax.dynamic_index_in_dim(values_o, core, 1, keepdims=False)
    send_o = lax.dynamic_index_in_dim(values_o, 1 - core, 1, keepdims=False)
    pair_o = jnp.stack([keep_o, lax.ppermute(send_o, "core", swap)])
    vals_o = lax.all_gather(pair_o, "z")
    chunks = orbital_values.reshape(16, 8, 48, 128).swapaxes(0, 1)
    own_q = lax.all_to_all(chunks, "z", 0, 0, tiled=True)
    other_q = lax.ppermute(own_q, "core", swap)

    mine, theirs = products(place, pattern_columns, block_orbitals, energy_weight, own, prev, nxt)
    got = lax.ppermute(theirs, "core", swap)
    pair = (mine.astype(jnp.float32) + got.astype(jnp.float32)).astype(jnp.bfloat16)
    parts = lax.all_to_all(pair.reshape(32, 2, 48, 128), ("y", "z"), 0, 0, tiled=True)
    rows = jnp.sum(parts.reshape(4, 8, 2, 48, 128).astype(jnp.float32), axis=0).astype(jnp.bfloat16)
    even = jnp.stack(gathered(rows[:, 0], "x"))
    odd = jnp.stack(gathered(rows[:, 1], "y"))
    shards = gathered(even, "y") + gathered(odd, "x")

    sums = applied_sums(place, request_source.reshape(-1), request_local, own_q, other_q, vals_o, shards)
    back = lax.ppermute(sums[:, 1], "core", swap)
    total = sums[:, 0] + back
    landed = lax.all_to_all(total, "z", 0, 0, tiled=True)
    return jnp.sum(landed, axis=0)


def solution(mesh):
    fine = Mesh(mesh.devices.reshape(4, 2, 8, 4), ("y", "core", "z", "x"))
    energy, rows = ("y", "core"), ("z", "x")
    in_specs = (
        P(energy, rows, None, None, None),
        P(energy),
        P(),
        P(rows, None),
        P(),
        P(),
        P(energy + rows, None, None),
    )
    return jax.shard_map(
        local_program, mesh=fine, in_specs=in_specs, out_specs=P(None, energy + rows), check_vma=False
    )
```

time: 561 us -> 217 us (0.39)
  the two profiles are of different devices: /device:TPU:127 before, /device:TPU:1 now
where the time goes in v1:
time: 217 us; the launch traced here: 216 us
  waiting for transfers between devices  82.1 us (38%)
  starting transfers between devices  77.7 us (36%)
  Pallas kernels  18.1 us (8%)
  blocking collectives  14.8 us (7%)
  between operations  14.2 us (7%)
  other arithmetic  5.07 us (2%)
  local copies, waits for them, and re-layouts  4.44 us (2%)
    all_to_all x1, starting transfers between devices, local_program(): lax.all_to_all(pair.reshape(32, 2, 48, 128), ('y', 'z'), 0, 0, tiled=True)  41.3 us
    ppermute x12, waiting for transfers between devices, shifted(): lax.ppermute(value, axis, [(n, (n + by) % count) for n in range(count)])  37.1 us
    all_to_all x1, waiting for transfers between devices, local_program(): lax.all_to_all(pair.reshape(32, 2, 48, 128), ('y', 'z'), 0, 0, tiled=True)  26.2 us
    ppermute x1, waiting for transfers between devices, local_program(): nxt = lax.ppermute(own, ('z', 'x'), backward)  15.8 us
    all_to_all x1, blocking collectives, local_program(): landed = lax.all_to_all(total, 'z', 0, 0, tiled=True)  14.8 us
    ppermute x12, starting transfers between devices, shifted(): lax.ppermute(value, axis, [(n, (n + by) % count) for n in range(count)])  12.1 us
    pallas_call x1, Pallas kernels, applied_sums(): pl.pallas_call(apply_kernel, grid=(8,), out_shape=jax.ShapeDtypeStruct((8...  11 us
    all_to_all x1, starting transfers between devices, local_program(): own_q = lax.all_to_all(chunks, 'z', 0, 0, tiled=True)  9.01 us
  transfers between devices with their start and end apart: 21, of which 14 were waited for; matrix products, arithmetic and copies ran while one was open for 2% of the time, Pallas kernels for 3%

profile of v1, /device:TPU:1, one launch (start us, length us, event | category | flops | bytes accessed | tf_op | source)
XLA Modules:
  0.0 216.4 jit_solution(521768343821952630)
XLA Ops:
  6.5 2.6 %copy.23 = bf16[16,8,48,128]{3,2,0,1:T(8,128)(2,1)} copy(bf16[16,8,48,128]{3,2,1,0:T(8,128)(2,1)} %bitcast.52) | data formatting | bytes 3145728 | tf_op jit(solution)/shard_map/reshape | solution.py:177
  9.2 9.0 %all-to-all-start = ((bf16[8,16,48,128]{3,2,1,0:T(8,128)(2,1)}), bf16[8,16,48,128]{3,2,1,0:T(8,128)(2,1)S(1)}, u32[]{:S(2)}, u32[]{:S(2)}) async-start(bf16[8,16,48,128]{3,2,1,0:T(8,128)(2,1)} %bitcast.50), calls=%async_computation | async-start | bytes 3145728 | tf_op jit(solution)/shard_map/all_to_all | solution.py:178
  18.2 0.0 all-gather.3.cloned.1.call-start
  18.2 1.3 collective-permute-start.3
  19.5 5.0 %collective-permute-start.2 = (bf16[8,2,128,256]{3,2,1,0:T(8,128)(2,1)}, bf16[8,2,128,256]{3,2,1,0:T(8,128)(2,1)}, u32[]{:S(2)}, u32[]{:S(2)}) collective-permute-start(bf16[8,2,128,256]{3,2,1,0:T(8,128)(2,1)} %bitcast.12.own), channel_id=1, source_target_pairs={{0,1},{1,2},{2,3},{3,4},{4,5},{5,6},{6,7},{7,8},{8,9},{9,10},{10,1... | collective-permute-start | bytes 3145736 | tf_op jit(solution)/shard_map/ppermute | solution.py:169
  24.6 1.0 slice.15
  25.6 1.6 collective-permute-start.1
  27.8 0.6 pad_add_fusion.place
  28.4 15.8 %collective-permute-done.3.nxt = bf16[8,2,128,256]{3,2,1,0:T(8,128)(2,1)} collective-permute-done((bf16[8,2,128,256]{3,2,1,0:T(8,128)(2,1)}, bf16[8,2,128,256]{3,2,1,0:T(8,128)(2,1)}, u32[]{:S(2)}, u32[]{:S(2)}) %collective-permute-start.3) | collective-permute-done | bytes 1048608 | tf_op jit(solution)/shard_map/ppermute | solution.py:170
  44.2 0.9 collective-permute-done.2.prev
  45.1 7.1 %products.1 = (bf16[4,8,2,48,128]{4,3,2,1,0:T(8,128)(2,1)}, bf16[4,8,2,48,128]{4,3,2,1,0:T(8,128)(2,1)}) custom-call(s32[4]{0:T(128)} %pad_add_fusion.place, s32[8,6]{1,0:T(8,128)} %pattern.1, s32[256]{0:T(256)} %live.1, f32[1]{0:T(128)S(6)} %copy.24.weight, bf16[8,2,128,256]{3,2,1,0:T(8,128)(2,1)} %bitcast.12.own, ...), custom_call_target="tpu_custom_call" | custom-call | flops 1600000000 | bytes 5000000 | tf_op jit(solution)/shard_map/products/pallas_call | solution.py:76
  52.1 2.2 %collective-permute-start.4 = (bf16[4,8,2,48,128]{4,3,2,1,0:T(8,128)(2,1)}, bf16[4,8,2,48,128]{4,3,2,1,0:T(8,128)(2,1)S(1)}, u32[]{:S(2)}, u32[]{:S(2)}) collective-permute-start(bf16[4,8,2,48,128]{4,3,2,1,0:T(8,128)(2,1)} %get-tuple-element.8), channel_id=1, source_target_pairs={{0,32},{32,0},{1,33},{33,1},{2,34},{34,2},{3,35},{35,3},{4,36},{36... | collective-permute-start | bytes 2359304 | tf_op jit(solution)/shard_map/ppermute | solution.py:182
  54.4 0.7 pad_maximum_fusion.2
  55.1 0.0 all-gather.3.cloned.1.call-update
  55.1 1.3 collective-permute-done.4
  56.5 2.2 %add_convert_fusion = bf16[4,8,2,48,128]{4,3,2,1,0:T(8,128)(2,1)} fusion(bf16[4,8,2,48,128]{4,3,2,1,0:T(8,128)(2,1)S(1)} %collective-permute-done.4, bf16[4,8,2,48,128]{4,3,2,1,0:T(8,128)(2,1)} %get-tuple-element.7), kind=kLoop, calls=%fused_computation.1 | loop fusion | flops 1572864 | bytes 2359296 | tf_op jit(solution)/shard_map/convert_element_type | solution.py:183
  58.7 41.3 %all-to-all-start.1 = ((bf16[32,2,48,128]{3,2,1,0:T(8,128)(2,1)}), bf16[32,2,48,128]{3,2,1,0:T(8,128)(2,1)S(1)}, u32[]{:S(2)}, u32[]{:S(2)}) async-start(bf16[32,2,48,128]{3,2,1,0:T(8,128)(2,1)} %bitcast.13), calls=%async_computation.1 | async-start | bytes 1572864 | tf_op jit(solution)/shard_map/all_to_all | solution.py:184
  100.0 0.7 collective-permute-start
  100.7 26.2 %all-to-all-done.1 = bf16[32,2,48,128]{3,2,1,0:T(8,128)(2,1)S(1)} async-done(((bf16[32,2,48,128]{3,2,1,0:T(8,128)(2,1)}), bf16[32,2,48,128]{3,2,1,0:T(8,128)(2,1)S(1)}, u32[]{:S(2)}, u32[]{:S(2)}) %all-to-all-start.1) | async-done | bytes 786464 | tf_op jit(solution)/shard_map/all_to_all | solution.py:184
  126.9 0.1 reduce_sum.21
  127.0 0.1 slice_bitcast_fusion
  127.1 2.6 %collective-permute-start.13 = (bf16[8,48,128]{2,1,0:T(8,128)(2,1)S(1)}, bf16[8,48,128]{2,1,0:T(8,128)(2,1)S(1)}, u32[]{:S(2)}, u32[]{:S(2)}) collective-permute-start(bf16[8,48,128]{2,1,0:T(8,128)(2,1)S(1)} %get-tuple-element.14), channel_id=1, source_target_pairs={{0,192},{64,0},{128,64},{192,128},{1,193},{65,1},{129,65},{193,129... | collective-permute-start | bytes 294920 | tf_op jit(solution)/shard_map/ppermute | solution.py:154
  129.7 0.5 collective-permute-start.12
  130.2 0.6 collective-permute-start.11
  130.8 0.6 collective-permute-done.13
  131.4 3.4 %collective-permute-done.12 = bf16[8,48,128]{2,1,0:T(8,128)(2,1)S(1)} collective-permute-done((bf16[8,48,128]{2,1,0:T(8,128)(2,1)S(1)}, bf16[8,48,128]{2,1,0:T(8,128)(2,1)S(1)}, u32[]{:S(2)}, u32[]{:S(2)}) %collective-permute-start.12) | collective-permute-done | bytes 98336 | tf_op jit(solution)/shard_map/ppermute | solution.py:154
  134.8 1.4 collective-permute-done.11
  136.2 0.1 pad_maximum_fusion.1.rest_4_
  136.2 1.0 collective-permute-start.16
  137.2 2.9 %collective-permute-start.7 = (bf16[8,48,128]{2,1,0:T(8,128)(2,1)S(1)}, bf16[8,48,128]{2,1,0:T(8,128)(2,1)S(1)}, u32[]{:S(2)}, u32[]{:S(2)}) collective-permute-start(bf16[8,48,128]{2,1,0:T(8,128)(2,1)S(1)} %get-tuple-element.13), channel_id=1, source_target_pairs={{0,3},{1,0},{2,1},{3,2},{4,7},{5,4},{6,5},{7,6},{8,11},{9,8},{10,9... | collective-permute-start | bytes 294920 | tf_op jit(solution)/shard_map/ppermute | solution.py:154
  140.2 0.0 collective-permute-start.6
  140.2 13.9 %collective-permute-done.7 = bf16[8,48,128]{2,1,0:T(8,128)(2,1)S(1)} collective-permute-done((bf16[8,48,128]{2,1,0:T(8,128)(2,1)S(1)}, bf16[8,48,128]{2,1,0:T(8,128)(2,1)S(1)}, u32[]{:S(2)}, u32[]{:S(2)}) %collective-permute-start.7) | collective-permute-done | bytes 98336 | tf_op jit(solution)/shard_map/ppermute | solution.py:154
  154.1 2.8 %collective-permute-start.14 = (bf16[4,8,48,128]{3,2,1,0:T(8,128)(2,1)S(1)}, bf16[4,8,48,128]{3,2,1,0:T(8,128)(2,1)S(1)}, u32[]{:S(2)}, u32[]{:S(2)}) collective-permute-start(bf16[4,8,48,128]{3,2,1,0:T(8,128)(2,1)S(1)} %pad_maximum_fusion.1.rest_4_), channel_id=1, source_target_pairs={{0,1},{1,2},{2,3},{3,0},{4,5},{5,6},{6,7},{7,4},{8,9},{9,10},{10,1... | collective-permute-start | bytes 1179656 | tf_op jit(solution)/shard_map/ppermute | solution.py:154
  156.9 1.8 collective-permute-done.5
  158.8 0.1 pad_maximum_fusion.rest_0_
  158.9 0.4 collective-permute-start.10
  159.3 1.3 collective-permute-start.8
  160.5 4.3 %collective-permute-done.14.rest_5_ = bf16[4,8,48,128]{3,2,1,0:T(8,128)(2,1)S(1)} collective-permute-done((bf16[4,8,48,128]{3,2,1,0:T(8,128)(2,1)S(1)}, bf16[4,8,48,128]{3,2,1,0:T(8,128)(2,1)S(1)}, u32[]{:S(2)}, u32[]{:S(2)}) %collective-permute-start.14) | collective-permute-done | bytes 393248 | tf_op jit(solution)/shard_map/ppermute | solution.py:154
  164.8 1.0 collective-permute-done.10.rest_3_
  165.9 1.7 collective-permute-done.9.rest_2_
  167.6 8.9 %collective-permute-done.8.rest_1_ = bf16[4,8,48,128]{3,2,1,0:T(8,128)(2,1)} collective-permute-done((bf16[4,8,48,128]{3,2,1,0:T(8,128)(2,1)S(1)}, bf16[4,8,48,128]{3,2,1,0:T(8,128)(2,1)}, u32[]{:S(2)}, u32[]{:S(2)}) %collective-permute-start.8) | collective-permute-done | bytes 393248 | tf_op jit(solution)/shard_map/ppermute | solution.py:154
  176.5 11.0 %applied_sums.1 = f32[8,2,4,128]{3,2,1,0:T(4,128)} custom-call(s32[4]{0:T(128)} %pad_add_fusion.place, s32[4096]{0:T(1024)} %bitcast.62, s32[4096]{0:T(1024)} %local.1, bf16[8,16,48,128]{3,2,1,0:T(8,128)(2,1)} %copy-done, bf16[8,16,48,128]{3,2,1,0:T(8,128)(2,1)} %collective-permute-done.other_q, bf16[8,2,16,32,128]{4,3,2,1,0:T(8,128)(2,1)} %bitcast.53, ...), custom_call_target="tpu_custom_call" | custom-call | flops 400000000 | bytes 8000000 | tf_op jit(solution)/shard_map/applied_sums/pallas_call | solution.py:134
  187.5 0.7 slice_bitcast_fusion.4
  188.2 4.4 %collective-permute-start.17 = (f32[8,4,128]{2,1,0:T(4,128)S(1)}, f32[8,4,128]{2,1,0:T(4,128)S(1)}, u32[]{:S(2)}, u32[]{:S(2)}) collective-permute-start(f32[8,4,128]{2,1,0:T(4,128)S(1)} %slice_bitcast_fusion.4), channel_id=1, source_target_pairs={{0,32},{32,0},{1,33},{33,1},{2,34},{34,2},{3,35},{35,3},{4,36},{36... | collective-permute-start | bytes 49160 | tf_op jit(solution)/shard_map/ppermute | solution.py:191
  192.6 0.8 collective-permute-done.17
  193.4 0.7 fusion
  194.1 14.8 %all_to_all.15 = f32[8,4,128]{2,1,0:T(4,128)S(1)} all-to-all(f32[8,4,128]{2,1,0:T(4,128)S(1)} %fusion), channel_id=1, replica_groups=mesh['y'=4,'core'=2,'z'=8,'x'=4] {'z'}, dimensions={0} | all-to-all | bytes 32768 | tf_op jit(solution)/shard_map/all_to_all | solution.py:193
  209.0 0.6 reduce_sum.22
  (23 shorter events, 0.1 us)
Async XLA Ops:
  9.2 49.5 %all-to-all-start = ((bf16[8,16,48,128]{3,2,1,0:T(8,128)(2,1)}), bf16[8,16,48,128]{3,2,1,0:T(8,128)(2,1)S(1)}, u32[]{:S(2)}, u32[]{:S(2)}) async-start(bf16[8,16,48,128]{3,2,1,0:T(8,128)(2,1)} %bitcast.50), calls=%async_computation | async-start | bytes 3145728 | tf_op jit(solution)/shard_map/all_to_all | solution.py:178
  18.2 142.3 %all-gather.3.cloned.1.call-start = ((), (), s32[]{:S(2)}) async-start(), calls=%async_computation.3 | async-start | bytes 2359296 | tf_op jit(solution)/shard_map/all_gather | solution.py:176
  18.2 25.9 %collective-permute-start.3 = (bf16[8,2,128,256]{3,2,1,0:T(8,128)(2,1)}, bf16[8,2,128,256]{3,2,1,0:T(8,128)(2,1)}, u32[]{:S(2)}, u32[]{:S(2)}) collective-permute-start(bf16[8,2,128,256]{3,2,1,0:T(8,128)(2,1)} %bitcast.12.own), channel_id=1, source_target_pairs={{1,0},{2,1},{3,2},{4,3},{5,4},{6,5},{7,6},{8,7},{9,8},{10,9},{11,1... | collective-permute-start | bytes 3145736 | tf_op jit(solution)/shard_map/ppermute | solution.py:170
  19.5 25.5 %collective-permute-start.2 = (bf16[8,2,128,256]{3,2,1,0:T(8,128)(2,1)}, bf16[8,2,128,256]{3,2,1,0:T(8,128)(2,1)}, u32[]{:S(2)}, u32[]{:S(2)}) collective-permute-start(bf16[8,2,128,256]{3,2,1,0:T(8,128)(2,1)} %bitcast.12.own), channel_id=1, source_target_pairs={{0,1},{1,2},{2,3},{3,4},{4,5},{5,6},{6,7},{7,8},{8,9},{9,10},{10,1... | collective-permute-start | bytes 3145736 | tf_op jit(solution)/shard_map/ppermute | solution.py:169
  25.6 28.8 %collective-permute-start.1 = (bf16[16,32,128]{2,1,0:T(8,128)(2,1)S(1)}, bf16[16,32,128]{2,1,0:T(8,128)(2,1)S(1)}, u32[]{:S(2)}, u32[]{:S(2)}) collective-permute-start(bf16[16,32,128]{2,1,0:T(8,128)(2,1)S(1)} %get-tuple-element.10), channel_id=1, source_target_pairs={{0,32},{32,0},{1,33},{33,1},{2,34},{34,2},{3,35},{35,3},{4,36},{36... | collective-permute-start | bytes 393224 | tf_op jit(solution)/shard_map/ppermute | solution.py:175
  52.1 4.4 %collective-permute-start.4 = (bf16[4,8,2,48,128]{4,3,2,1,0:T(8,128)(2,1)}, bf16[4,8,2,48,128]{4,3,2,1,0:T(8,128)(2,1)S(1)}, u32[]{:S(2)}, u32[]{:S(2)}) collective-permute-start(bf16[4,8,2,48,128]{4,3,2,1,0:T(8,128)(2,1)} %get-tuple-element.8), channel_id=1, source_target_pairs={{0,32},{32,0},{1,33},{33,1},{2,34},{34,2},{3,35},{35,3},{4,36},{36... | collective-permute-start | bytes 2359304 | tf_op jit(solution)/shard_map/ppermute | solution.py:182
  58.7 68.4 %copy-start = (bf16[8,16,48,128]{3,2,1,0:T(8,128)(2,1)}, bf16[8,16,48,128]{3,2,1,0:T(8,128)(2,1)S(1)}, u32[]{:S(2)}) copy-start(bf16[8,16,48,128]{3,2,1,0:T(8,128)(2,1)S(1)} %all-to-all-done.own_q) | copy-start | bytes 4718596
  58.7 68.2 %all-to-all-start.1 = ((bf16[32,2,48,128]{3,2,1,0:T(8,128)(2,1)}), bf16[32,2,48,128]{3,2,1,0:T(8,128)(2,1)S(1)}, u32[]{:S(2)}, u32[]{:S(2)}) async-start(bf16[32,2,48,128]{3,2,1,0:T(8,128)(2,1)} %bitcast.13), calls=%async_computation.1 | async-start | bytes 1572864 | tf_op jit(solution)/shard_map/all_to_all | solution.py:184
  100.0 76.5 %collective-permute-start = (bf16[8,16,48,128]{3,2,1,0:T(8,128)(2,1)S(1)}, bf16[8,16,48,128]{3,2,1,0:T(8,128)(2,1)}, u32[]{:S(2)}, u32[]{:S(2)}) collective-permute-start(bf16[8,16,48,128]{3,2,1,0:T(8,128)(2,1)S(1)} %all-to-all-done.own_q), channel_id=1, source_target_pairs={{0,32},{32,0},{1,33},{33,1},{2,34},{34,2},{3,35},{35,3},{4,36},{36... | collective-permute-start | bytes 4718600 | tf_op jit(solution)/shard_map/ppermute | solution.py:179
  127.1 4.3 %collective-permute-start.13 = (bf16[8,48,128]{2,1,0:T(8,128)(2,1)S(1)}, bf16[8,48,128]{2,1,0:T(8,128)(2,1)S(1)}, u32[]{:S(2)}, u32[]{:S(2)}) collective-permute-start(bf16[8,48,128]{2,1,0:T(8,128)(2,1)S(1)} %get-tuple-element.14), channel_id=1, source_target_pairs={{0,192},{64,0},{128,64},{192,128},{1,193},{65,1},{129,65},{193,129... | collective-permute-start | bytes 294920 | tf_op jit(solution)/shard_map/ppermute | solution.py:154
  129.7 5.1 %collective-permute-start.12 = (bf16[8,48,128]{2,1,0:T(8,128)(2,1)S(1)}, bf16[8,48,128]{2,1,0:T(8,128)(2,1)S(1)}, u32[]{:S(2)}, u32[]{:S(2)}) collective-permute-start(bf16[8,48,128]{2,1,0:T(8,128)(2,1)S(1)} %get-tuple-element.14), channel_id=1, source_target_pairs={{0,128},{64,192},{128,0},{192,64},{1,129},{65,193},{129,1},{193,65... | collective-permute-start | bytes 294920 | tf_op jit(solution)/shard_map/ppermute | solution.py:154
  130.2 6.0 %collective-permute-start.11 = (bf16[8,48,128]{2,1,0:T(8,128)(2,1)S(1)}, bf16[8,48,128]{2,1,0:T(8,128)(2,1)S(1)}, u32[]{:S(2)}, u32[]{:S(2)}) collective-permute-start(bf16[8,48,128]{2,1,0:T(8,128)(2,1)S(1)} %get-tuple-element.14), channel_id=1, source_target_pairs={{0,64},{64,128},{128,192},{192,0},{1,65},{65,129},{129,193},{193,1... | collective-permute-start | bytes 294920 | tf_op jit(solution)/shard_map/ppermute | solution.py:154
  136.2 40.2 %copy-start.1 = (bf16[4,8,48,128]{3,2,1,0:T(8,128)(2,1)}, bf16[4,8,48,128]{3,2,1,0:T(8,128)(2,1)S(1)}, u32[]{:S(2)}) copy-start(bf16[4,8,48,128]{3,2,1,0:T(8,128)(2,1)S(1)} %pad_maximum_fusion.1.rest_4_) | copy-start | bytes 1179652
  136.2 23.0 %collective-permute-start.16 = (bf16[4,8,48,128]{3,2,1,0:T(8,128)(2,1)S(1)}, bf16[4,8,48,128]{3,2,1,0:T(8,128)(2,1)S(1)}, u32[]{:S(2)}, u32[]{:S(2)}) collective-permute-start(bf16[4,8,48,128]{3,2,1,0:T(8,128)(2,1)S(1)} %pad_maximum_fusion.1.rest_4_), channel_id=1, source_target_pairs={{0,3},{1,0},{2,1},{3,2},{4,7},{5,4},{6,5},{7,6},{8,11},{9,8},{10,9... | collective-permute-start | bytes 1179656 | tf_op jit(solution)/shard_map/ppermute | solution.py:154
  137.2 22.0 %collective-permute-start.15 = (bf16[4,8,48,128]{3,2,1,0:T(8,128)(2,1)S(1)}, bf16[4,8,48,128]{3,2,1,0:T(8,128)(2,1)S(1)}, u32[]{:S(2)}, u32[]{:S(2)}) collective-permute-start(bf16[4,8,48,128]{3,2,1,0:T(8,128)(2,1)S(1)} %pad_maximum_fusion.1.rest_4_), channel_id=1, source_target_pairs={{0,2},{1,3},{2,0},{3,1},{4,6},{5,7},{6,4},{7,5},{8,10},{9,11},{10,... | collective-permute-start | bytes 1179656 | tf_op jit(solution)/shard_map/ppermute | solution.py:154
  137.2 16.9 %collective-permute-start.7 = (bf16[8,48,128]{2,1,0:T(8,128)(2,1)S(1)}, bf16[8,48,128]{2,1,0:T(8,128)(2,1)S(1)}, u32[]{:S(2)}, u32[]{:S(2)}) collective-permute-start(bf16[8,48,128]{2,1,0:T(8,128)(2,1)S(1)} %get-tuple-element.13), channel_id=1, source_target_pairs={{0,3},{1,0},{2,1},{3,2},{4,7},{5,4},{6,5},{7,6},{8,11},{9,8},{10,9... | collective-permute-start | bytes 294920 | tf_op jit(solution)/shard_map/ppermute | solution.py:154
  140.2 14.0 %collective-permute-start.6 = (bf16[8,48,128]{2,1,0:T(8,128)(2,1)S(1)}, bf16[8,48,128]{2,1,0:T(8,128)(2,1)S(1)}, u32[]{:S(2)}, u32[]{:S(2)}) collective-permute-start(bf16[8,48,128]{2,1,0:T(8,128)(2,1)S(1)} %get-tuple-element.13), channel_id=1, source_target_pairs={{0,2},{1,3},{2,0},{3,1},{4,6},{5,7},{6,4},{7,5},{8,10},{9,11},{10,... | collective-permute-start | bytes 294920 | tf_op jit(solution)/shard_map/ppermute | solution.py:154
  154.1 4.7 %collective-permute-start.5 = (bf16[8,48,128]{2,1,0:T(8,128)(2,1)S(1)}, bf16[8,48,128]{2,1,0:T(8,128)(2,1)S(1)}, u32[]{:S(2)}, u32[]{:S(2)}) collective-permute-start(bf16[8,48,128]{2,1,0:T(8,128)(2,1)S(1)} %get-tuple-element.13), channel_id=1, source_target_pairs={{0,1},{1,2},{2,3},{3,0},{4,5},{5,6},{6,7},{7,4},{8,9},{9,10},{10,1... | collective-permute-start | bytes 294920 | tf_op jit(solution)/shard_map/ppermute | solution.py:154
  154.1 10.7 %collective-permute-start.14 = (bf16[4,8,48,128]{3,2,1,0:T(8,128)(2,1)S(1)}, bf16[4,8,48,128]{3,2,1,0:T(8,128)(2,1)S(1)}, u32[]{:S(2)}, u32[]{:S(2)}) collective-permute-start(bf16[4,8,48,128]{3,2,1,0:T(8,128)(2,1)S(1)} %pad_maximum_fusion.1.rest_4_), channel_id=1, source_target_pairs={{0,1},{1,2},{2,3},{3,0},{4,5},{5,6},{6,7},{7,4},{8,9},{9,10},{10,1... | collective-permute-start | bytes 1179656 | tf_op jit(solution)/shard_map/ppermute | solution.py:154
  158.9 17.6 %copy-start.2 = (bf16[4,8,48,128]{3,2,1,0:T(8,128)(2,1)}, bf16[4,8,48,128]{3,2,1,0:T(8,128)(2,1)S(1)}, u32[]{:S(2)}) copy-start(bf16[4,8,48,128]{3,2,1,0:T(8,128)(2,1)S(1)} %pad_maximum_fusion.rest_0_) | copy-start | bytes 1179652
  158.9 7.0 %collective-permute-start.10 = (bf16[4,8,48,128]{3,2,1,0:T(8,128)(2,1)S(1)}, bf16[4,8,48,128]{3,2,1,0:T(8,128)(2,1)}, u32[]{:S(2)}, u32[]{:S(2)}) collective-permute-start(bf16[4,8,48,128]{3,2,1,0:T(8,128)(2,1)S(1)} %pad_maximum_fusion.rest_0_), channel_id=1, source_target_pairs={{0,192},{64,0},{128,64},{192,128},{1,193},{65,1},{129,65},{193,129... | collective-permute-start | bytes 1179656 | tf_op jit(solution)/shard_map/ppermute | solution.py:154
  159.2 17.2 %copy-start.3 = (bf16[4,8,48,128]{3,2,1,0:T(8,128)(2,1)}, bf16[4,8,48,128]{3,2,1,0:T(8,128)(2,1)S(1)}, u32[]{:S(2)}) copy-start(bf16[4,8,48,128]{3,2,1,0:T(8,128)(2,1)S(1)} %collective-permute-done.16.rest_7_) | copy-start | bytes 1179652
  159.2 8.3 %collective-permute-start.9 = (bf16[4,8,48,128]{3,2,1,0:T(8,128)(2,1)S(1)}, bf16[4,8,48,128]{3,2,1,0:T(8,128)(2,1)}, u32[]{:S(2)}, u32[]{:S(2)}) collective-permute-start(bf16[4,8,48,128]{3,2,1,0:T(8,128)(2,1)S(1)} %pad_maximum_fusion.rest_0_), channel_id=1, source_target_pairs={{0,128},{64,192},{128,0},{192,64},{1,129},{65,193},{129,1},{193,65... | collective-permute-start | bytes 1179656 | tf_op jit(solution)/shard_map/ppermute | solution.py:154
  159.2 17.2 %copy-start.4 = (bf16[4,8,48,128]{3,2,1,0:T(8,128)(2,1)}, bf16[4,8,48,128]{3,2,1,0:T(8,128)(2,1)S(1)}, u32[]{:S(2)}) copy-start(bf16[4,8,48,128]{3,2,1,0:T(8,128)(2,1)S(1)} %collective-permute-done.15.rest_6_) | copy-start | bytes 1179652
  159.3 17.2 %collective-permute-start.8 = (bf16[4,8,48,128]{3,2,1,0:T(8,128)(2,1)S(1)}, bf16[4,8,48,128]{3,2,1,0:T(8,128)(2,1)}, u32[]{:S(2)}, u32[]{:S(2)}) collective-permute-start(bf16[4,8,48,128]{3,2,1,0:T(8,128)(2,1)S(1)} %pad_maximum_fusion.rest_0_), channel_id=1, source_target_pairs={{0,64},{64,128},{128,192},{192,0},{1,65},{65,129},{129,193},{193,1... | collective-permute-start | bytes 1179656 | tf_op jit(solution)/shard_map/ppermute | solution.py:154
  164.8 11.6 %copy-start.5 = (bf16[4,8,48,128]{3,2,1,0:T(8,128)(2,1)}, bf16[4,8,48,128]{3,2,1,0:T(8,128)(2,1)S(1)}, u32[]{:S(2)}) copy-start(bf16[4,8,48,128]{3,2,1,0:T(8,128)(2,1)S(1)} %collective-permute-done.14.rest_5_) | copy-start | bytes 1179652
  188.2 5.2 %collective-permute-start.17 = (f32[8,4,128]{2,1,0:T(4,128)S(1)}, f32[8,4,128]{2,1,0:T(4,128)S(1)}, u32[]{:S(2)}, u32[]{:S(2)}) collective-permute-start(f32[8,4,128]{2,1,0:T(4,128)S(1)} %slice_bitcast_fusion.4), channel_id=1, source_target_pairs={{0,32},{32,0},{1,33},{33,1},{2,34},{34,2},{3,35},{35,3},{4,36},{36... | collective-permute-start | bytes 49160 | tf_op jit(solution)/shard_map/ppermute | solution.py:191
Sparse Core Ops, SparseCore 0:
  55.3 82.8 all-gather.2

commit v2 on v1

v2 whole, which is shorter than its diff:
```python
import jax
import jax.numpy as jnp
from jax import lax
from jax.experimental import pallas as pl
from jax.experimental.pallas import tpu as pltpu
from jax.sharding import Mesh, PartitionSpec as P

NT = (((1,), (1,)), ((), ()))
TN = (((0,), (0,)), ((), ()))
MIB = 1024 * 1024
SMEM = pl.BlockSpec(memory_space=pltpu.SMEM)
VMEM = pl.BlockSpec(memory_space=pltpu.VMEM)
ANY = pl.BlockSpec(memory_space=pl.ANY)


def bf16(*shape):
    return jax.ShapeDtypeStruct(shape, jnp.bfloat16)


def params(mib):
    return pltpu.CompilerParams(vmem_limit_bytes=mib * MIB)


def prepare_kernel(own, sides):
    table = (
        ((0, 0, 1), (0, 1, 1), (0, 0, 1), (1, 1, 1)),
        ((1, 0, 1), (1, 1, 1), (1, 0, 1), (0, 1, -1)),
        ((0, 1, 1), (0, 0, 1), (0, 1, -1), (1, 0, -1)),
        ((1, 1, 1), (1, 0, 1), (1, 1, -1), (0, 0, 1)),
    )

    def one(i, carry):
        pieces = {(part, spin): own[i, part, pl.ds(64 * spin, 64), :] for part in range(2) for spin in range(2)}
        for n, parts in enumerate(table):
            for c, (part, spin, sign) in enumerate(parts):
                piece = pieces[part, spin]
                sides[i, n, pl.ds(64 * c, 64), :] = piece if sign == 1 else -piece
        return carry

    lax.fori_loop(0, 8, one, 0)


def prepare(own):
    return pl.pallas_call(
        prepare_kernel,
        out_shape=bf16(8, 4, 256, 256),
        in_specs=[VMEM],
        out_specs=VMEM,
        compiler_params=params(10),
        cost_estimate=pl.CostEstimate(flops=0, bytes_accessed=5_000_000, transcendentals=0),
        name="prepare",
    )(own)


def cut_kernel(values, chunks, orbitals):
    for e in range(8):
        chunks[e] = values[:, pl.ds(48 * e, 48)]
    orbitals[...] = values[:, :64]


def cut_values(values):
    return pl.pallas_call(
        cut_kernel,
        out_shape=(bf16(8, 16, 48, 128), bf16(16, 64, 128)),
        in_specs=[VMEM],
        out_specs=(VMEM, VMEM),
        compiler_params=params(8),
        cost_estimate=pl.CostEstimate(flops=0, bytes_accessed=3_000_000, transcendentals=0),
        name="cut_values",
    )(values)


def gate_kernel(*refs):
    pass


def gate(value, *after):
    return pl.pallas_call(
        gate_kernel,
        out_shape=jax.ShapeDtypeStruct(value.shape, value.dtype),
        in_specs=[ANY] * (1 + len(after)),
        out_specs=ANY,
        input_output_aliases={0: 0},
        compiler_params=params(1),
        cost_estimate=pl.CostEstimate(flops=0, bytes_accessed=0, transcendentals=0),
        name="gate",
    )(value, *after)


def product_kernel(place, pattern, live, weight, sides, low, own, high, mine, theirs, ext, sems):
    i = pl.program_id(0)

    @pl.when(i == 0)
    def _():
        copies = [
            pltpu.make_async_copy(src, ext.at[pl.ds(8 * n, 8)], sems.at[n]) for n, src in enumerate((low, own, high))
        ]
        for copy in copies:
            copy.start()
        for copy in copies:
            copy.wait()

    first = place[0]
    scale = weight[0]
    even = place[1] == 0
    orbital = lax.broadcasted_iota(jnp.int32, (64, 256), 1) % 64
    row = lax.broadcasted_iota(jnp.int32, (64, 256), 0)
    columns = [pattern[i, k] for k in range(6)]
    total = None
    for n, (spin, part) in enumerate(((0, 0), (0, 1), (1, 0), (1, 1))):
        left = jnp.concatenate([ext[c - first + 8, part, pl.ds(spin * 64, 64), :] for c in columns], axis=0)
        term = lax.dot_general(left, sides[0, n], NT, preferred_element_type=jnp.float32)
        total = term if total is None else total + term
    kept_row = orbital < live[first + i]
    pieces = []
    for k, c in enumerate(columns):
        kept = kept_row & (row < live[c])
        pieces.append(jnp.where(kept, total[64 * k : 64 * k + 64] * scale, 0.0))
    chunks = jnp.concatenate(pieces, axis=0).reshape(4, 2, 48, 256)
    mine[:, 0] = jnp.where(even, chunks[:, 0], chunks[:, 1]).astype(jnp.bfloat16)
    theirs[:, 0] = jnp.where(even, chunks[:, 1], chunks[:, 0]).astype(jnp.bfloat16)


def products(place, pattern, live, weight, sides, low, own, high):
    by_block = pl.BlockSpec((4, 1, 48, 256), lambda i: (0, i, 0, 0))
    return pl.pallas_call(
        product_kernel,
        grid=(8,),
        out_shape=(bf16(4, 8, 48, 256),) * 2,
        in_specs=[SMEM] * 4 + [pl.BlockSpec((1, 4, 256, 256), lambda i: (i, 0, 0, 0))] + [ANY] * 3,
        out_specs=(by_block, by_block),
        scratch_shapes=[pltpu.VMEM((24, 2, 128, 256), jnp.bfloat16), pltpu.SemaphoreType.DMA((3,))],
        compiler_params=params(12),
        cost_estimate=pl.CostEstimate(flops=1_600_000_000, bytes_accessed=9_000_000, transcendentals=0),
        name="products",
    )(place, pattern, live, weight, sides, low, own, high)


def pair_kernel(place, mine, got, *parts):
    for d in range(4):
        at = (place[2] + d) & 3
        parts[d][...] = (mine[at].astype(jnp.float32) + got[at].astype(jnp.float32)).astype(jnp.bfloat16)


def pair_sums(place, mine, got):
    return pl.pallas_call(
        pair_kernel,
        out_shape=(bf16(8, 48, 256),) * 4,
        in_specs=[SMEM, VMEM, VMEM],
        out_specs=(VMEM,) * 4,
        compiler_params=params(6),
        cost_estimate=pl.CostEstimate(flops=400_000, bytes_accessed=2_400_000, transcendentals=0),
        name="pair_sums",
    )(place, mine, got)


def apply_kernel(place, source, local, vals_q, own_o, other_o, *rest):
    count = len(rest) - 3
    shards, out, rows, sems = rest[:count], rest[count], rest[count + 1], rest[count + 2]
    e = pl.program_id(0)
    core, y_at, x_at, z_at = place[1], place[2], place[3], place[4]

    @pl.when(e == 0)
    def _():
        at, copies = 0, []
        for n, shard in enumerate(shards):
            size = shard.shape[0]
            copies.append(pltpu.make_async_copy(shard, rows.at[pl.ds(at, size)], sems.at[n]))
            at += size
        for copy in copies:
            copy.start()
        for copy in copies:
            copy.wait()

    device = e * 32 + 4 * z_at + x_at
    dy = (y_at - e // 2) & 3
    same = (e & 1) == core

    def run(values_o):
        total = jnp.zeros((4, 64, 128), jnp.float32)
        for r in range(16):
            request = device * 16 + r
            src = source[request]
            loc = local[request]
            dx = (x_at - src) & 3
            dz = (z_at - src // 4) & 7
            at = jnp.where(loc < 4, 16 * dz + 4 * dx + loc, 128 + 32 * dx + 4 * dz + loc - 4)
            applied = lax.dot_general(rows[at], vals_q[0, r], TN, preferred_element_type=jnp.float32)
            total = total + applied.reshape(4, 64, 128) * values_o[dy, r].astype(jnp.float32)[None]
        sums = jnp.sum(total, axis=1)
        for at, c in enumerate((0, 1, 3, 2)):
            out[0, pl.ds(c, 1)] = sums[at : at + 1]

    @pl.when(same)
    def _():
        run(own_o)

    @pl.when(jnp.logical_not(same))
    def _():
        run(other_o)


def applied_sums(place, source, local, vals_q, own_o, other_o, shards):
    return pl.pallas_call(
        apply_kernel,
        grid=(8,),
        out_shape=jax.ShapeDtypeStruct((8, 4, 128), jnp.float32),
        in_specs=[SMEM] * 3
        + [pl.BlockSpec((1, 16, 48, 128), lambda e: (e, 0, 0, 0)), VMEM, VMEM]
        + [ANY] * len(shards),
        out_specs=pl.BlockSpec((1, 4, 128), lambda e: (e, 0, 0)),
        scratch_shapes=[pltpu.VMEM((256, 48, 256), jnp.bfloat16), pltpu.SemaphoreType.DMA((len(shards),))],
        compiler_params=params(56),
        cost_estimate=pl.CostEstimate(flops=400_000_000, bytes_accessed=8_000_000, transcendentals=0),
        name="applied_sums",
    )(place, source, local, vals_q, own_o, other_o, *shards)


def shifted(value, axis, by):
    count = lax.axis_size(axis)
    return lax.ppermute(value, axis, [(n, (n + by) % count) for n in range(count)])


def gathered(value, axis):
    return [value] + [shifted(value, axis, d) for d in (1, 2, 3)]


def three_ways(value):
    ahead, behind, around = value, value, {0: value}
    for step in (1, 2, 3):
        ahead, behind = shifted(ahead, "z", 1), shifted(behind, "z", 7)
        around[step], around[8 - step] = ahead, behind
    return around, ahead, behind


def flat(value):
    return value.reshape((-1,) + value.shape[-2:])


def local_program(panels, energy_weight, block_orbitals, pattern_columns, request_source, request_local, orbital_values):
    core = lax.axis_index("core")
    y_at, z_at, x_at = lax.axis_index("y"), lax.axis_index("z"), lax.axis_index("x")
    place = jnp.stack([(z_at * 4 + x_at) * 8, core, y_at, x_at, z_at]).astype(jnp.int32)
    own = panels[0]
    swap = [(0, 1), (1, 0)]
    low = lax.ppermute(own, ("z", "x"), [(n, n + 1) for n in range(31)])
    high = lax.ppermute(own, ("z", "x"), [(n + 1, n) for n in range(31)])

    chunks, orbitals = cut_values(orbital_values)
    own_o = jnp.stack(gathered(orbitals, "y"))
    other_o = lax.ppermute(own_o, "core", swap)
    vals_q = lax.all_to_all(chunks, ("y", "core"), 0, 0, tiled=True)
    sides = gate(prepare(own), vals_q, own_o)

    mine, theirs = products(place, pattern_columns, block_orbitals, energy_weight, sides, low, own, high)
    got = lax.ppermute(theirs, "core", swap)
    parts = pair_sums(place, mine, got)
    total = parts[0].astype(jnp.float32)
    for d in (1, 2, 3):
        total = total + shifted(parts[d], "y", d).astype(jnp.float32)
    total = total.astype(jnp.bfloat16)

    first = jnp.stack(gathered(total[:4], "x"))
    firsts, ahead, behind = three_ways(first)
    last = [shifted(ahead[:2], "z", 1), shifted(behind[2:], "z", 7)]
    shards = [firsts[d] for d in range(4)] + last + [firsts[d] for d in (5, 6, 7)]
    seconds, ahead, behind = three_ways(total[4:])
    seconds[4] = shifted(ahead, "z", 1)
    second = jnp.stack([seconds[d] for d in range(8)])
    right, left = shifted(second, "x", 1), shifted(second, "x", 3)
    shards += [second, right, shifted(right[:4], "x", 1), shifted(left[4:], "x", 3), left]

    sums = applied_sums(
        place, request_source.reshape(-1), request_local, vals_q, own_o, other_o, [flat(s) for s in shards]
    )
    landed = lax.all_to_all(sums, ("y", "core"), 0, 0, tiled=True)
    return jnp.sum(landed, axis=0)


def solution(mesh):
    fine = Mesh(mesh.devices.reshape(4, 2, 8, 4), ("y", "core", "z", "x"))
    energy, rows = ("y", "core"), ("z", "x")
    in_specs = (
        P(energy, rows, None, None, None),
        P(energy),
        P(),
        P(rows, None),
        P(),
        P(),
        P(energy + rows, None, None),
    )
    return jax.shard_map(
        local_program, mesh=fine, in_specs=in_specs, out_specs=P(None, energy + rows), check_vma=False
    )
```

time: 217 us -> 167 us (0.77)
  waiting for transfers between devices: 82.1 us -> 58.9 us
  starting transfers between devices: 77.7 us -> 59.3 us
  between operations: 14.2 us -> 1.12 us
  local copies, waits for them, and re-layouts: 4.44 us -> 12.5 us
  other arithmetic: 5.07 us -> 1.83 us
  Pallas kernels: 18.1 us -> 20.6 us
  blocking collectives: 14.8 us -> 12.4 us
    all_to_all x2 -> x1, starting transfers between devices: 50.3 us -> 6.72 us  [local_program(): vals_q = lax.all_to_all(chunks, ('y', 'core'), 0, 0, tiled=True)]
    ppermute x12 -> x28, starting transfers between devices: 12.1 us -> 41.1 us  [shifted(): lax.ppermute(value, axis, [(n, (n + by) % count) for n in range(count)])]
    all_to_all x2 -> x1, waiting for transfers between devices: 26.2 us -> 0.01 us  [local_program(): vals_q = lax.all_to_all(chunks, ('y', 'core'), 0, 0, tiled=True)]
    ppermute x12 -> x28, waiting for transfers between devices: 37.1 us -> 57 us  [shifted(): lax.ppermute(value, axis, [(n, (n + by) % count) for n in range(count)])]
    ppermute x5 -> x3, waiting for transfers between devices: 17.5 us -> 0.01 us  [the longest x1 0.01 us: local_program(): low = lax.ppermute(own, ('z', 'x'), [(n, n + 1) for n in range(31)])]
    unnamed x12 -> x57, local copies, waits for them, and re-layouts: 0.02 us -> 12.3 us
    reshape x1 -> x0, local copies, waits for them, and re-layouts: 2.65 us -> none  [local_program(): chunks = orbital_values.reshape(16, 8, 48, 128).swapaxes(0, 1)]
    pallas_call x1 -> x5, Pallas kernels: 7.06 us -> 9.64 us  [the longest x1 6.1 us: products(): pl.pallas_call(product_kernel, grid=(8,), out_shape=(bf16(4, 8, 48, 256),...]
  transfers between devices with their start and end apart: 21 -> 33, of which waited for: 14 -> 11; matrix products, arithmetic and copies ran while one was open for 2% -> 1% of each run, Pallas kernels for 3% -> 1%
where the time goes in v2:
time: 167 us
  starting transfers between devices  59.3 us (36%)
  waiting for transfers between devices  58.9 us (35%)
  Pallas kernels  20.6 us (12%)
  local copies, waits for them, and re-layouts  12.5 us (7%)
  blocking collectives  12.4 us (7%)
  other arithmetic  1.83 us (1%)
    ppermute x28, waiting for transfers between devices, shifted(): lax.ppermute(value, axis, [(n, (n + by) % count) for n in range(count)])  57 us
    ppermute x28, starting transfers between devices, shifted(): lax.ppermute(value, axis, [(n, (n + by) % count) for n in range(count)])  41.1 us
    all_to_all x1, blocking collectives, local_program(): landed = lax.all_to_all(sums, ('y', 'core'), 0, 0, tiled=True)  12.4 us
    unnamed x57, local copies, waits for them, and re-layouts  12.3 us
    pallas_call x1, Pallas kernels, applied_sums(): pl.pallas_call(apply_kernel, grid=(8,), out_shape=jax.ShapeDtypeStruct((8...  10.9 us
    all_to_all x1, starting transfers between devices, local_program(): vals_q = lax.all_to_all(chunks, ('y', 'core'), 0, 0, tiled=True)  6.72 us
    pallas_call x1, Pallas kernels, products(): pl.pallas_call(product_kernel, grid=(8,), out_shape=(bf16(4, 8, 48, 256),...  6.1 us
    ppermute x1, starting transfers between devices, local_program(): other_o = lax.ppermute(own_o, 'core', swap)  5.75 us
  transfers between devices with their start and end apart: 33, of which 11 were waited for; matrix products, arithmetic and copies ran while one was open for 1% of the time, Pallas kernels for 1%

profile of v2, /device:TPU:1, one launch (start us, length us, event | category | flops | bytes accessed | tf_op | source)
XLA Modules:
  0.0 166.5 jit_solution(5368308405426188592)
XLA Ops:
  0.0 1.4 copy-done.6
  1.4 1.3 cut_values.1
  2.7 6.7 %all-to-all-start = ((bf16[8,16,48,128]{3,2,1,0:T(8,128)(2,1)}), bf16[8,16,48,128]{3,2,1,0:T(8,128)(2,1)S(1)}, u32[]{:S(2)}, u32[]{:S(2)}) async-start(bf16[8,16,48,128]{3,2,1,0:T(8,128)(2,1)} %get-tuple-element.13), calls=%async_computation | async-start | bytes 3145728 | tf_op jit(solution)/shard_map/all_to_all | solution.py:252
  9.4 3.5 %collective-permute-start.4 = (bf16[8,2,128,256]{3,2,1,0:T(8,128)(2,1)}, bf16[8,2,128,256]{3,2,1,0:T(8,128)(2,1)}, u32[]{:S(2)}, u32[]{:S(2)}) collective-permute-start(bf16[8,2,128,256]{3,2,1,0:T(8,128)(2,1)} %bitcast.10.own), channel_id=1, source_target_pairs={{0,1},{1,2},{2,3},{3,4},{4,5},{5,6},{6,7},{7,8},{8,9},{9,10},{10,1... | collective-permute-start | bytes 3145736 | tf_op jit(solution)/shard_map/ppermute | solution.py:246
  12.9 1.3 collective-permute-start.5
  14.2 1.5 collective-permute-start
  15.7 2.4 %collective-permute-start.1 = (bf16[16,64,128]{2,1,0:T(8,128)(2,1)S(1)}, bf16[16,64,128]{2,1,0:T(8,128)(2,1)S(1)}, u32[]{:S(2)}, u32[]{:S(2)}) collective-permute-start(bf16[16,64,128]{2,1,0:T(8,128)(2,1)S(1)} %get-tuple-element.14), channel_id=1, source_target_pairs={{0,128},{64,192},{128,0},{192,64},{1,129},{65,193},{129,1},{193,65... | collective-permute-start | bytes 786440 | tf_op jit(solution)/shard_map/ppermute | solution.py:221
  18.0 1.2 collective-permute-start.2
  19.2 1.5 prepare.1.refs_0_
  20.7 2.0 %copy-done = bf16[8,4,256,256]{3,2,1,0:T(8,128)(2,1)} copy-done((bf16[8,4,256,256]{3,2,1,0:T(8,128)(2,1)}, bf16[8,4,256,256]{3,2,1,0:T(8,128)(2,1)S(1)}, u32[]{:S(2)}) %copy-start) | copy-done | bytes 4194328
  23.5 12.2 %collective-permute-done = bf16[16,64,128]{2,1,0:T(8,128)(2,1)S(1)} collective-permute-done((bf16[16,64,128]{2,1,0:T(8,128)(2,1)S(1)}, bf16[16,64,128]{2,1,0:T(8,128)(2,1)S(1)}, u32[]{:S(2)}, u32[]{:S(2)}) %collective-permute-start) | collective-permute-done | bytes 262176 | tf_op jit(solution)/shard_map/ppermute | solution.py:221
  35.7 5.8 %collective-permute-done.1 = bf16[16,64,128]{2,1,0:T(8,128)(2,1)S(1)} collective-permute-done((bf16[16,64,128]{2,1,0:T(8,128)(2,1)S(1)}, bf16[16,64,128]{2,1,0:T(8,128)(2,1)S(1)}, u32[]{:S(2)}, u32[]{:S(2)}) %collective-permute-start.1) | collective-permute-done | bytes 262176 | tf_op jit(solution)/shard_map/ppermute | solution.py:221
  41.5 1.1 pad_maximum_fusion.refs_2_.own_o
  42.6 2.6 %copy-done.1 = bf16[8,4,256,256]{3,2,1,0:T(8,128)(2,1)S(1)} copy-done((bf16[8,4,256,256]{3,2,1,0:T(8,128)(2,1)S(1)}, bf16[8,4,256,256]{3,2,1,0:T(8,128)(2,1)}, u32[]{:S(2)}) %copy-start.1) | copy-done | bytes 4194328
  45.1 1.2 copy-done.4
  46.3 2.0 %copy-done.2 = bf16[8,4,256,256]{3,2,1,0:T(8,128)(2,1)} copy-done((bf16[8,4,256,256]{3,2,1,0:T(8,128)(2,1)}, bf16[8,4,256,256]{3,2,1,0:T(8,128)(2,1)S(1)}, u32[]{:S(2)}) %copy-start.2) | copy-done | bytes 4194328
  48.4 2.2 %copy-done.3 = bf16[8,4,256,256]{3,2,1,0:T(8,128)(2,1)S(1)} copy-done((bf16[8,4,256,256]{3,2,1,0:T(8,128)(2,1)S(1)}, bf16[8,4,256,256]{3,2,1,0:T(8,128)(2,1)}, u32[]{:S(2)}) %copy-start.3) | copy-done | bytes 4194328
  50.5 6.1 %products.1 = (bf16[4,8,48,256]{3,2,1,0:T(8,128)(2,1)S(1)}, bf16[4,8,48,256]{3,2,1,0:T(8,128)(2,1)S(1)}) custom-call(s32[5]{0:T(128)S(1)} %stack.80.place, s32[8,6]{1,0:T(8,128)S(1)} %copy-done.8, s32[256]{0:T(256)S(1)} %copy-done.9, f32[1]{0:T(128)S(6)} %copy.17.weight, bf16[8,4,256,256]{3,2,1,0:T(8,128)(2,1)S(1)} %copy-done.3, ...), custom_call_target="tpu_custom_call" | custom-call | flops 1600000000 | bytes 9000000 | tf_op jit(solution)/shard_map/products/pallas_call | solution.py:126
  56.7 1.0 collective-permute-start.6
  57.6 1.9 %collective-permute-done.6.got = bf16[4,8,48,256]{3,2,1,0:T(8,128)(2,1)S(1)} collective-permute-done((bf16[4,8,48,256]{3,2,1,0:T(8,128)(2,1)S(1)}, bf16[4,8,48,256]{3,2,1,0:T(8,128)(2,1)S(1)}, u32[]{:S(2)}, u32[]{:S(2)}) %collective-permute-start.6) | collective-permute-done | bytes 786464 | tf_op jit(solution)/shard_map/ppermute | solution.py:256
  59.5 0.7 pair_sums.1
  60.4 1.1 collective-permute-start.8
  61.4 2.0 %collective-permute-start.9 = (bf16[8,48,256]{2,1,0:T(8,128)(2,1)S(1)}, bf16[8,48,256]{2,1,0:T(8,128)(2,1)S(1)}, u32[]{:S(2)}, u32[]{:S(2)}) collective-permute-start(bf16[8,48,256]{2,1,0:T(8,128)(2,1)S(1)} %get-tuple-element.20), channel_id=1, source_target_pairs={{0,192},{64,0},{128,64},{192,128},{1,193},{65,1},{129,65},{193,129... | collective-permute-start | bytes 589832 | tf_op jit(solution)/shard_map/ppermute | solution.py:221
  63.4 8.5 %collective-permute-done.7 = bf16[8,48,256]{2,1,0:T(8,128)(2,1)S(1)} collective-permute-done((bf16[8,48,256]{2,1,0:T(8,128)(2,1)S(1)}, bf16[8,48,256]{2,1,0:T(8,128)(2,1)S(1)}, u32[]{:S(2)}, u32[]{:S(2)}) %collective-permute-start.7) | collective-permute-done | bytes 196640 | tf_op jit(solution)/shard_map/ppermute | solution.py:221
  72.3 0.5 collective-permute-start.10
  72.8 2.4 %collective-permute-start.11 = (bf16[4,48,256]{2,1,0:T(8,128)(2,1)S(1)}, bf16[4,48,256]{2,1,0:T(8,128)(2,1)S(1)}, u32[]{:S(2)}, u32[]{:S(2)}) collective-permute-start(bf16[4,48,256]{2,1,0:T(8,128)(2,1)S(1)} %get-tuple-element.23), channel_id=1, source_target_pairs={{0,2},{1,3},{2,0},{3,1},{4,6},{5,7},{6,4},{7,5},{8,10},{9,11},{10,... | collective-permute-start | bytes 294920 | tf_op jit(solution)/shard_map/ppermute | solution.py:221
  75.3 1.2 collective-permute-start.12
  76.4 1.7 %collective-permute-start.21 = (bf16[4,48,256]{2,1,0:T(8,128)(2,1)S(1)}, bf16[4,48,256]{2,1,0:T(8,128)(2,1)S(1)}, u32[]{:S(2)}, u32[]{:S(2)}) collective-permute-start(bf16[4,48,256]{2,1,0:T(8,128)(2,1)S(1)} %get-tuple-element.21), channel_id=1, source_target_pairs={{0,4},{4,8},{8,12},{12,16},{16,20},{20,24},{24,28},{28,0},{1,5},{5... | collective-permute-start | bytes 294920 | tf_op jit(solution)/shard_map/ppermute | solution.py:221
  78.2 4.0 %collective-permute-start.25 = (bf16[4,48,256]{2,1,0:T(8,128)(2,1)S(1)}, bf16[4,48,256]{2,1,0:T(8,128)(2,1)S(1)}, u32[]{:S(2)}, u32[]{:S(2)}) collective-permute-start(bf16[4,48,256]{2,1,0:T(8,128)(2,1)S(1)} %get-tuple-element.21), channel_id=1, source_target_pairs={{0,28},{4,0},{8,4},{12,8},{16,12},{20,16},{24,20},{28,24},{1,29},{... | collective-permute-start | bytes 294920 | tf_op jit(solution)/shard_map/ppermute | solution.py:221
  82.4 3.3 %collective-permute-start.17 = (bf16[4,4,48,256]{3,2,1,0:T(8,128)(2,1)S(1)}, bf16[4,4,48,256]{3,2,1,0:T(8,128)(2,1)S(1)}, u32[]{:S(2)}, u32[]{:S(2)}) collective-permute-start(bf16[4,4,48,256]{3,2,1,0:T(8,128)(2,1)S(1)} %pad_maximum_fusion.1), channel_id=1, source_target_pairs={{0,28},{4,0},{8,4},{12,8},{16,12},{20,16},{24,20},{28,24},{1,29},{... | collective-permute-start | bytes 1179656 | tf_op jit(solution)/shard_map/ppermute | solution.py:221
  85.6 2.9 %collective-permute-start.26 = (bf16[4,48,256]{2,1,0:T(8,128)(2,1)S(1)}, bf16[4,48,256]{2,1,0:T(8,128)(2,1)S(1)}, u32[]{:S(2)}, u32[]{:S(2)}) collective-permute-start(bf16[4,48,256]{2,1,0:T(8,128)(2,1)S(1)} %collective-permute-done.25), channel_id=1, source_target_pairs={{0,28},{4,0},{8,4},{12,8},{16,12},{20,16},{24,20},{28,24},{1,29},{... | collective-permute-start | bytes 294920 | tf_op jit(solution)/shard_map/ppermute | solution.py:221
  88.6 6.4 %collective-permute-done.22 = bf16[4,48,256]{2,1,0:T(8,128)(2,1)S(1)} collective-permute-done((bf16[4,48,256]{2,1,0:T(8,128)(2,1)S(1)}, bf16[4,48,256]{2,1,0:T(8,128)(2,1)S(1)}, u32[]{:S(2)}, u32[]{:S(2)}) %collective-permute-start.22) | collective-permute-done | bytes 98336 | tf_op jit(solution)/shard_map/ppermute | solution.py:221
  95.0 3.1 %collective-permute-start.27 = (bf16[4,48,256]{2,1,0:T(8,128)(2,1)S(1)}, bf16[4,48,256]{2,1,0:T(8,128)(2,1)S(1)}, u32[]{:S(2)}, u32[]{:S(2)}) collective-permute-start(bf16[4,48,256]{2,1,0:T(8,128)(2,1)S(1)} %collective-permute-done.26), channel_id=1, source_target_pairs={{0,28},{4,0},{8,4},{12,8},{16,12},{20,16},{24,20},{28,24},{1,29},{... | collective-permute-start | bytes 294920 | tf_op jit(solution)/shard_map/ppermute | solution.py:221
  98.1 1.6 collective-permute-done.23
  99.7 4.7 %collective-permute-done.24 = bf16[4,48,256]{2,1,0:T(8,128)(2,1)S(1)} collective-permute-done((bf16[4,48,256]{2,1,0:T(8,128)(2,1)S(1)}, bf16[4,48,256]{2,1,0:T(8,128)(2,1)S(1)}, u32[]{:S(2)}, u32[]{:S(2)}) %collective-permute-start.24) | collective-permute-done | bytes 98336 | tf_op jit(solution)/shard_map/ppermute | solution.py:221
  104.7 2.5 %collective-permute-start.30 = (bf16[8,4,48,256]{3,2,1,0:T(8,128)(2,1)S(1)}, bf16[8,4,48,256]{3,2,1,0:T(8,128)(2,1)S(1)}, u32[]{:S(2)}, u32[]{:S(2)}) collective-permute-start(bf16[8,4,48,256]{3,2,1,0:T(8,128)(2,1)S(1)} %bitcast_dynamic-update-slice_fusion), channel_id=1, source_target_pairs={{0,3},{1,0},{2,1},{3,2},{4,7},{5,4},{6,5},{7,6},{8,11},{9,8},{10,9... | collective-permute-start | bytes 2359304 | tf_op jit(solution)/shard_map/ppermute | solution.py:221
  107.2 5.8 %collective-permute-start.3 = (bf16[4,16,64,128]{3,2,1,0:T(8,128)(2,1)S(1)}, bf16[4,16,64,128]{3,2,1,0:T(8,128)(2,1)S(1)}, u32[]{:S(2)}, u32[]{:S(2)}) collective-permute-start(bf16[4,16,64,128]{3,2,1,0:T(8,128)(2,1)S(1)} %pad_maximum_fusion.refs_2_.own_o), channel_id=1, source_target_pairs={{0,32},{32,0},{1,33},{33,1},{2,34},{34,2},{3,35},{35,3},{4,36},{36... | collective-permute-start | bytes 3145736 | tf_op jit(solution)/shard_map/ppermute | solution.py:251
  113.0 2.7 %collective-permute-start.18 = (bf16[4,4,48,256]{3,2,1,0:T(8,128)(2,1)S(1)}, bf16[4,4,48,256]{3,2,1,0:T(8,128)(2,1)S(1)}, u32[]{:S(2)}, u32[]{:S(2)}) collective-permute-start(bf16[4,4,48,256]{3,2,1,0:T(8,128)(2,1)S(1)} %collective-permute-done.17), channel_id=1, source_target_pairs={{0,28},{4,0},{8,4},{12,8},{16,12},{20,16},{24,20},{28,24},{1,29},{... | collective-permute-start | bytes 1179656 | tf_op jit(solution)/shard_map/ppermute | solution.py:221
  115.6 9.2 %collective-permute-done.14 = bf16[4,4,48,256]{3,2,1,0:T(8,128)(2,1)S(1)} collective-permute-done((bf16[4,4,48,256]{3,2,1,0:T(8,128)(2,1)S(1)}, bf16[4,4,48,256]{3,2,1,0:T(8,128)(2,1)S(1)}, u32[]{:S(2)}, u32[]{:S(2)}) %collective-permute-start.14) | collective-permute-done | bytes 393248 | tf_op jit(solution)/shard_map/ppermute | solution.py:221
  124.8 2.7 %collective-permute-start.19 = (bf16[4,4,48,256]{3,2,1,0:T(8,128)(2,1)S(1)}, bf16[4,4,48,256]{3,2,1,0:T(8,128)(2,1)S(1)}, u32[]{:S(2)}, u32[]{:S(2)}) collective-permute-start(bf16[4,4,48,256]{3,2,1,0:T(8,128)(2,1)S(1)} %collective-permute-done.18), channel_id=1, source_target_pairs={{0,28},{4,0},{8,4},{12,8},{16,12},{20,16},{24,20},{28,24},{1,29},{... | collective-permute-start | bytes 1179656 | tf_op jit(solution)/shard_map/ppermute | solution.py:221
  127.7 2.7 %collective-permute-start.31 = (bf16[4,4,48,256]{3,2,1,0:T(8,128)(2,1)S(1)}, bf16[4,4,48,256]{3,2,1,0:T(8,128)(2,1)S(1)}, u32[]{:S(2)}, u32[]{:S(2)}) collective-permute-start(bf16[4,4,48,256]{3,2,1,0:T(8,128)(2,1)S(1)} %slice.29), channel_id=1, source_target_pairs={{0,3},{1,0},{2,1},{3,2},{4,7},{5,4},{6,5},{7,6},{8,11},{9,8},{10,9... | collective-permute-start | bytes 1179656 | tf_op jit(solution)/shard_map/ppermute | solution.py:221
  130.4 5.4 %collective-permute-done.15 = bf16[4,4,48,256]{3,2,1,0:T(8,128)(2,1)S(1)} collective-permute-done((bf16[4,4,48,256]{3,2,1,0:T(8,128)(2,1)S(1)}, bf16[4,4,48,256]{3,2,1,0:T(8,128)(2,1)S(1)}, u32[]{:S(2)}, u32[]{:S(2)}) %collective-permute-start.15) | collective-permute-done | bytes 393248 | tf_op jit(solution)/shard_map/ppermute | solution.py:221
  136.0 2.7 %collective-permute-start.20 = (bf16[2,4,48,256]{3,2,1,0:T(8,128)(2,1)S(1)}, bf16[2,4,48,256]{3,2,1,0:T(8,128)(2,1)S(1)}, u32[]{:S(2)}, u32[]{:S(2)}) collective-permute-start(bf16[2,4,48,256]{3,2,1,0:T(8,128)(2,1)S(1)} %slice.26), channel_id=1, source_target_pairs={{0,28},{4,0},{8,4},{12,8},{16,12},{20,16},{24,20},{28,24},{1,29},{... | collective-permute-start | bytes 589832 | tf_op jit(solution)/shard_map/ppermute | solution.py:221
  138.7 2.9 %collective-permute-done.16 = bf16[2,4,48,256]{3,2,1,0:T(8,128)(2,1)S(1)} collective-permute-done((bf16[2,4,48,256]{3,2,1,0:T(8,128)(2,1)S(1)}, bf16[2,4,48,256]{3,2,1,0:T(8,128)(2,1)S(1)}, u32[]{:S(2)}, u32[]{:S(2)}) %collective-permute-start.16) | collective-permute-done | bytes 196640 | tf_op jit(solution)/shard_map/ppermute | solution.py:221
  141.8 0.5 copy-done.23
  142.7 10.9 %applied_sums.1 = f32[8,4,128]{2,1,0:T(4,128)} custom-call(s32[5]{0:T(128)} %copy-done.7, s32[4096]{0:T(1024)} %bitcast.66, s32[4096]{0:T(1024)} %local.1, bf16[8,16,48,128]{3,2,1,0:T(8,128)(2,1)} %copy-done.4, bf16[4,16,64,128]{3,2,1,0:T(8,128)(2,1)} %copy-done.5, bf16[4,16,64,128]{3,2,1,0:T(8,128)(2,1)} %copy-done.13, bf16[16,48,256]{2,1,0:T(8,128)(2,1)} %bitcast.49, ...), custom_call_target="tpu_custom_call" | custom-call | flops 400000000 | bytes 8000000 | tf_op jit(solution)/shard_map/applied_sums/pallas_call | solution.py:204
  153.6 12.4 %all_to_all.10 = f32[8,4,128]{2,1,0:T(4,128)S(1)} all-to-all(f32[8,4,128]{2,1,0:T(4,128)} %applied_sums.1), channel_id=1, replica_groups=mesh['y'=4,'core'=2,'z'=8,'x'=4] {'y','core'}, dimensions={0} | all-to-all | bytes 32768 | tf_op jit(solution)/shard_map/all_to_all | solution.py:276
  166.0 0.6 reduce_sum.9
  (93 shorter events, 1.8 us)
Async XLA Ops:
  2.7 39.8 %all-to-all-start = ((bf16[8,16,48,128]{3,2,1,0:T(8,128)(2,1)}), bf16[8,16,48,128]{3,2,1,0:T(8,128)(2,1)S(1)}, u32[]{:S(2)}, u32[]{:S(2)}) async-start(bf16[8,16,48,128]{3,2,1,0:T(8,128)(2,1)} %get-tuple-element.13), calls=%async_computation | async-start | bytes 3145728 | tf_op jit(solution)/shard_map/all_to_all | solution.py:252
  9.4 38.9 %collective-permute-start.4 = (bf16[8,2,128,256]{3,2,1,0:T(8,128)(2,1)}, bf16[8,2,128,256]{3,2,1,0:T(8,128)(2,1)}, u32[]{:S(2)}, u32[]{:S(2)}) collective-permute-start(bf16[8,2,128,256]{3,2,1,0:T(8,128)(2,1)} %bitcast.10.own), channel_id=1, source_target_pairs={{0,1},{1,2},{2,3},{3,4},{4,5},{5,6},{6,7},{7,8},{8,9},{9,10},{10,1... | collective-permute-start | bytes 3145736 | tf_op jit(solution)/shard_map/ppermute | solution.py:246
  12.9 35.4 %collective-permute-start.5 = (bf16[8,2,128,256]{3,2,1,0:T(8,128)(2,1)}, bf16[8,2,128,256]{3,2,1,0:T(8,128)(2,1)}, u32[]{:S(2)}, u32[]{:S(2)}) collective-permute-start(bf16[8,2,128,256]{3,2,1,0:T(8,128)(2,1)} %bitcast.10.own), channel_id=1, source_target_pairs={{1,0},{2,1},{3,2},{4,3},{5,4},{6,5},{7,6},{8,7},{9,8},{10,9},{11,1... | collective-permute-start | bytes 3145736 | tf_op jit(solution)/shard_map/ppermute | solution.py:247
  14.2 21.5 %collective-permute-start = (bf16[16,64,128]{2,1,0:T(8,128)(2,1)S(1)}, bf16[16,64,128]{2,1,0:T(8,128)(2,1)S(1)}, u32[]{:S(2)}, u32[]{:S(2)}) collective-permute-start(bf16[16,64,128]{2,1,0:T(8,128)(2,1)S(1)} %get-tuple-element.14), channel_id=1, source_target_pairs={{0,64},{64,128},{128,192},{192,0},{1,65},{65,129},{129,193},{193,1... | collective-permute-start | bytes 786440 | tf_op jit(solution)/shard_map/ppermute | solution.py:221
  15.7 25.8 %collective-permute-start.1 = (bf16[16,64,128]{2,1,0:T(8,128)(2,1)S(1)}, bf16[16,64,128]{2,1,0:T(8,128)(2,1)S(1)}, u32[]{:S(2)}, u32[]{:S(2)}) collective-permute-start(bf16[16,64,128]{2,1,0:T(8,128)(2,1)S(1)} %get-tuple-element.14), channel_id=1, source_target_pairs={{0,128},{64,192},{128,0},{192,64},{1,129},{65,193},{129,1},{193,65... | collective-permute-start | bytes 786440 | tf_op jit(solution)/shard_map/ppermute | solution.py:221
  18.0 23.4 %collective-permute-start.2 = (bf16[16,64,128]{2,1,0:T(8,128)(2,1)S(1)}, bf16[16,64,128]{2,1,0:T(8,128)(2,1)}, u32[]{:S(2)}, u32[]{:S(2)}) collective-permute-start(bf16[16,64,128]{2,1,0:T(8,128)(2,1)S(1)} %get-tuple-element.14), channel_id=1, source_target_pairs={{0,192},{64,0},{128,64},{192,128},{1,193},{65,1},{129,65},{193,129... | collective-permute-start | bytes 786440 | tf_op jit(solution)/shard_map/ppermute | solution.py:221
  23.5 36.1 %copy-start.7 = (s32[5]{0:T(128)}, s32[5]{0:T(128)S(1)}, u32[]{:S(2)}) copy-start(s32[5]{0:T(128)S(1)} %stack.80.place) | copy-start | bytes 64
  42.6 64.6 %copy-start.5 = (bf16[4,16,64,128]{3,2,1,0:T(8,128)(2,1)}, bf16[4,16,64,128]{3,2,1,0:T(8,128)(2,1)S(1)}, u32[]{:S(2)}) copy-start(bf16[4,16,64,128]{3,2,1,0:T(8,128)(2,1)S(1)} %pad_maximum_fusion.refs_2_.own_o) | copy-start | bytes 3145732
  45.1 3.2 %copy-start.8 = (s32[8,6]{1,0:T(8,128)S(1)}, s32[8,6]{1,0:T(8,128)}, u32[]{:S(2)}) copy-start(s32[8,6]{1,0:T(8,128)} %pattern.1) | copy-start | bytes 580
  45.1 3.2 %copy-start.9 = (s32[256]{0:T(256)S(1)}, s32[256]{0:T(256)}, u32[]{:S(2)}) copy-start(s32[256]{0:T(256)} %live.1) | copy-start | bytes 3076
  56.7 2.9 %collective-permute-start.6 = (bf16[4,8,48,256]{3,2,1,0:T(8,128)(2,1)S(1)}, bf16[4,8,48,256]{3,2,1,0:T(8,128)(2,1)S(1)}, u32[]{:S(2)}, u32[]{:S(2)}) collective-permute-start(bf16[4,8,48,256]{3,2,1,0:T(8,128)(2,1)S(1)} %get-tuple-element.16), channel_id=1, source_target_pairs={{0,32},{32,0},{1,33},{33,1},{2,34},{34,2},{3,35},{35,3},{4,36},{36... | collective-permute-start | bytes 2359304 | tf_op jit(solution)/shard_map/ppermute | solution.py:256
  60.3 11.6 %collective-permute-start.7 = (bf16[8,48,256]{2,1,0:T(8,128)(2,1)S(1)}, bf16[8,48,256]{2,1,0:T(8,128)(2,1)S(1)}, u32[]{:S(2)}, u32[]{:S(2)}) collective-permute-start(bf16[8,48,256]{2,1,0:T(8,128)(2,1)S(1)} %get-tuple-element.18), channel_id=1, source_target_pairs={{0,64},{64,128},{128,192},{192,0},{1,65},{65,129},{129,193},{193,1... | collective-permute-start | bytes 589832 | tf_op jit(solution)/shard_map/ppermute | solution.py:221
  60.4 11.5 %collective-permute-start.8 = (bf16[8,48,256]{2,1,0:T(8,128)(2,1)S(1)}, bf16[8,48,256]{2,1,0:T(8,128)(2,1)S(1)}, u32[]{:S(2)}, u32[]{:S(2)}) collective-permute-start(bf16[8,48,256]{2,1,0:T(8,128)(2,1)S(1)} %get-tuple-element.19), channel_id=1, source_target_pairs={{0,128},{64,192},{128,0},{192,64},{1,129},{65,193},{129,1},{193,65... | collective-permute-start | bytes 589832 | tf_op jit(solution)/shard_map/ppermute | solution.py:221
  61.4 10.7 %collective-permute-start.9 = (bf16[8,48,256]{2,1,0:T(8,128)(2,1)S(1)}, bf16[8,48,256]{2,1,0:T(8,128)(2,1)S(1)}, u32[]{:S(2)}, u32[]{:S(2)}) collective-permute-start(bf16[8,48,256]{2,1,0:T(8,128)(2,1)S(1)} %get-tuple-element.20), channel_id=1, source_target_pairs={{0,192},{64,0},{128,64},{192,128},{1,193},{65,1},{129,65},{193,129... | collective-permute-start | bytes 589832 | tf_op jit(solution)/shard_map/ppermute | solution.py:221
  72.3 9.9 %collective-permute-start.10 = (bf16[4,48,256]{2,1,0:T(8,128)(2,1)S(1)}, bf16[4,48,256]{2,1,0:T(8,128)(2,1)S(1)}, u32[]{:S(2)}, u32[]{:S(2)}) collective-permute-start(bf16[4,48,256]{2,1,0:T(8,128)(2,1)S(1)} %get-tuple-element.23), channel_id=1, source_target_pairs={{0,1},{1,2},{2,3},{3,0},{4,5},{5,6},{6,7},{7,4},{8,9},{9,10},{10,1... | collective-permute-start | bytes 294920 | tf_op jit(solution)/shard_map/ppermute | solution.py:221
  72.8 9.4 %collective-permute-start.11 = (bf16[4,48,256]{2,1,0:T(8,128)(2,1)S(1)}, bf16[4,48,256]{2,1,0:T(8,128)(2,1)S(1)}, u32[]{:S(2)}, u32[]{:S(2)}) collective-permute-start(bf16[4,48,256]{2,1,0:T(8,128)(2,1)S(1)} %get-tuple-element.23), channel_id=1, source_target_pairs={{0,2},{1,3},{2,0},{3,1},{4,6},{5,7},{6,4},{7,5},{8,10},{9,11},{10,... | collective-permute-start | bytes 294920 | tf_op jit(solution)/shard_map/ppermute | solution.py:221
  75.3 6.9 %collective-permute-start.12 = (bf16[4,48,256]{2,1,0:T(8,128)(2,1)S(1)}, bf16[4,48,256]{2,1,0:T(8,128)(2,1)S(1)}, u32[]{:S(2)}, u32[]{:S(2)}) collective-permute-start(bf16[4,48,256]{2,1,0:T(8,128)(2,1)S(1)} %get-tuple-element.23), channel_id=1, source_target_pairs={{0,3},{1,0},{2,1},{3,2},{4,7},{5,4},{6,5},{7,6},{8,11},{9,8},{10,9... | collective-permute-start | bytes 294920 | tf_op jit(solution)/shard_map/ppermute | solution.py:221
  76.4 9.2 %collective-permute-start.21 = (bf16[4,48,256]{2,1,0:T(8,128)(2,1)S(1)}, bf16[4,48,256]{2,1,0:T(8,128)(2,1)S(1)}, u32[]{:S(2)}, u32[]{:S(2)}) collective-permute-start(bf16[4,48,256]{2,1,0:T(8,128)(2,1)S(1)} %get-tuple-element.21), channel_id=1, source_target_pairs={{0,4},{4,8},{8,12},{12,16},{16,20},{20,24},{24,28},{28,0},{1,5},{5... | collective-permute-start | bytes 294920 | tf_op jit(solution)/shard_map/ppermute | solution.py:221
  78.2 7.5 %collective-permute-start.25 = (bf16[4,48,256]{2,1,0:T(8,128)(2,1)S(1)}, bf16[4,48,256]{2,1,0:T(8,128)(2,1)S(1)}, u32[]{:S(2)}, u32[]{:S(2)}) collective-permute-start(bf16[4,48,256]{2,1,0:T(8,128)(2,1)S(1)} %get-tuple-element.21), channel_id=1, source_target_pairs={{0,28},{4,0},{8,4},{12,8},{16,12},{20,16},{24,20},{28,24},{1,29},{... | collective-permute-start | bytes 294920 | tf_op jit(solution)/shard_map/ppermute | solution.py:221
  82.3 53.6 %copy-start.12 = (bf16[4,4,48,256]{3,2,1,0:T(8,128)(2,1)}, bf16[4,4,48,256]{3,2,1,0:T(8,128)(2,1)S(1)}, u32[]{:S(2)}) copy-start(bf16[4,4,48,256]{3,2,1,0:T(8,128)(2,1)S(1)} %pad_maximum_fusion.1) | copy-start | bytes 1179652
  82.3 30.7 %collective-permute-start.13 = (bf16[4,4,48,256]{3,2,1,0:T(8,128)(2,1)S(1)}, bf16[4,4,48,256]{3,2,1,0:T(8,128)(2,1)S(1)}, u32[]{:S(2)}, u32[]{:S(2)}) collective-permute-start(bf16[4,4,48,256]{3,2,1,0:T(8,128)(2,1)S(1)} %pad_maximum_fusion.1), channel_id=1, source_target_pairs={{0,4},{4,8},{8,12},{12,16},{16,20},{20,24},{24,28},{28,0},{1,5},{5... | collective-permute-start | bytes 1179656 | tf_op jit(solution)/shard_map/ppermute | solution.py:221
  82.4 30.6 %collective-permute-start.17 = (bf16[4,4,48,256]{3,2,1,0:T(8,128)(2,1)S(1)}, bf16[4,4,48,256]{3,2,1,0:T(8,128)(2,1)S(1)}, u32[]{:S(2)}, u32[]{:S(2)}) collective-permute-start(bf16[4,4,48,256]{3,2,1,0:T(8,128)(2,1)S(1)} %pad_maximum_fusion.1), channel_id=1, source_target_pairs={{0,28},{4,0},{8,4},{12,8},{16,12},{20,16},{24,20},{28,24},{1,29},{... | collective-permute-start | bytes 1179656 | tf_op jit(solution)/shard_map/ppermute | solution.py:221
  85.6 9.4 %collective-permute-start.22 = (bf16[4,48,256]{2,1,0:T(8,128)(2,1)S(1)}, bf16[4,48,256]{2,1,0:T(8,128)(2,1)S(1)}, u32[]{:S(2)}, u32[]{:S(2)}) collective-permute-start(bf16[4,48,256]{2,1,0:T(8,128)(2,1)S(1)} %collective-permute-done.21), channel_id=1, source_target_pairs={{0,4},{4,8},{8,12},{12,16},{16,20},{20,24},{24,28},{28,0},{1,5},{5... | collective-permute-start | bytes 294920 | tf_op jit(solution)/shard_map/ppermute | solution.py:221
  85.6 9.4 %collective-permute-start.26 = (bf16[4,48,256]{2,1,0:T(8,128)(2,1)S(1)}, bf16[4,48,256]{2,1,0:T(8,128)(2,1)S(1)}, u32[]{:S(2)}, u32[]{:S(2)}) collective-permute-start(bf16[4,48,256]{2,1,0:T(8,128)(2,1)S(1)} %collective-permute-done.25), channel_id=1, source_target_pairs={{0,28},{4,0},{8,4},{12,8},{16,12},{20,16},{24,20},{28,24},{1,29},{... | collective-permute-start | bytes 294920 | tf_op jit(solution)/shard_map/ppermute | solution.py:221
  95.0 4.7 %collective-permute-start.23 = (bf16[4,48,256]{2,1,0:T(8,128)(2,1)S(1)}, bf16[4,48,256]{2,1,0:T(8,128)(2,1)S(1)}, u32[]{:S(2)}, u32[]{:S(2)}) collective-permute-start(bf16[4,48,256]{2,1,0:T(8,128)(2,1)S(1)} %collective-permute-done.22), channel_id=1, source_target_pairs={{0,4},{4,8},{8,12},{12,16},{16,20},{20,24},{24,28},{28,0},{1,5},{5... | collective-permute-start | bytes 294920 | tf_op jit(solution)/shard_map/ppermute | solution.py:221
  95.0 9.3 %collective-permute-start.27 = (bf16[4,48,256]{2,1,0:T(8,128)(2,1)S(1)}, bf16[4,48,256]{2,1,0:T(8,128)(2,1)S(1)}, u32[]{:S(2)}, u32[]{:S(2)}) collective-permute-start(bf16[4,48,256]{2,1,0:T(8,128)(2,1)S(1)} %collective-permute-done.26), channel_id=1, source_target_pairs={{0,28},{4,0},{8,4},{12,8},{16,12},{20,16},{24,20},{28,24},{1,29},{... | collective-permute-start | bytes 294920 | tf_op jit(solution)/shard_map/ppermute | solution.py:221
  99.7 4.7 %collective-permute-start.24 = (bf16[4,48,256]{2,1,0:T(8,128)(2,1)S(1)}, bf16[4,48,256]{2,1,0:T(8,128)(2,1)S(1)}, u32[]{:S(2)}, u32[]{:S(2)}) collective-permute-start(bf16[4,48,256]{2,1,0:T(8,128)(2,1)S(1)} %collective-permute-done.23), channel_id=1, source_target_pairs={{0,4},{4,8},{8,12},{12,16},{16,20},{20,24},{24,28},{28,0},{1,5},{5... | collective-permute-start | bytes 294920 | tf_op jit(solution)/shard_map/ppermute | solution.py:221
  104.4 37.3 %copy-start.14 = (bf16[8,4,48,256]{3,2,1,0:T(8,128)(2,1)}, bf16[8,4,48,256]{3,2,1,0:T(8,128)(2,1)S(1)}, u32[]{:S(2)}) copy-start(bf16[8,4,48,256]{3,2,1,0:T(8,128)(2,1)S(1)} %bitcast_dynamic-update-slice_fusion) | copy-start | bytes 2359300
  104.4 23.1 %collective-permute-start.28 = (bf16[8,4,48,256]{3,2,1,0:T(8,128)(2,1)S(1)}, bf16[8,4,48,256]{3,2,1,0:T(8,128)(2,1)S(1)}, u32[]{:S(2)}, u32[]{:S(2)}) collective-permute-start(bf16[8,4,48,256]{3,2,1,0:T(8,128)(2,1)S(1)} %bitcast_dynamic-update-slice_fusion), channel_id=1, source_target_pairs={{0,1},{1,2},{2,3},{3,0},{4,5},{5,6},{6,7},{7,4},{8,9},{9,10},{10,1... | collective-permute-start | bytes 2359304 | tf_op jit(solution)/shard_map/ppermute | solution.py:221
  104.7 22.9 %collective-permute-start.30 = (bf16[8,4,48,256]{3,2,1,0:T(8,128)(2,1)S(1)}, bf16[8,4,48,256]{3,2,1,0:T(8,128)(2,1)S(1)}, u32[]{:S(2)}, u32[]{:S(2)}) collective-permute-start(bf16[8,4,48,256]{3,2,1,0:T(8,128)(2,1)S(1)} %bitcast_dynamic-update-slice_fusion), channel_id=1, source_target_pairs={{0,3},{1,0},{2,1},{3,2},{4,7},{5,4},{6,5},{7,6},{8,11},{9,8},{10,9... | collective-permute-start | bytes 2359304 | tf_op jit(solution)/shard_map/ppermute | solution.py:221
  107.2 31.5 %collective-permute-start.3 = (bf16[4,16,64,128]{3,2,1,0:T(8,128)(2,1)S(1)}, bf16[4,16,64,128]{3,2,1,0:T(8,128)(2,1)S(1)}, u32[]{:S(2)}, u32[]{:S(2)}) collective-permute-start(bf16[4,16,64,128]{3,2,1,0:T(8,128)(2,1)S(1)} %pad_maximum_fusion.refs_2_.own_o), channel_id=1, source_target_pairs={{0,32},{32,0},{1,33},{33,1},{2,34},{34,2},{3,35},{35,3},{4,36},{36... | collective-permute-start | bytes 3145736 | tf_op jit(solution)/shard_map/ppermute | solution.py:251
  112.9 28.8 %copy-start.17 = (bf16[4,4,48,256]{3,2,1,0:T(8,128)(2,1)}, bf16[4,4,48,256]{3,2,1,0:T(8,128)(2,1)S(1)}, u32[]{:S(2)}) copy-start(bf16[4,4,48,256]{3,2,1,0:T(8,128)(2,1)S(1)} %collective-permute-done.13) | copy-start | bytes 1179652
  112.9 11.9 %collective-permute-start.14 = (bf16[4,4,48,256]{3,2,1,0:T(8,128)(2,1)S(1)}, bf16[4,4,48,256]{3,2,1,0:T(8,128)(2,1)S(1)}, u32[]{:S(2)}, u32[]{:S(2)}) collective-permute-start(bf16[4,4,48,256]{3,2,1,0:T(8,128)(2,1)S(1)} %collective-permute-done.13), channel_id=1, source_target_pairs={{0,4},{4,8},{8,12},{12,16},{16,20},{20,24},{24,28},{28,0},{1,5},{5... | collective-permute-start | bytes 1179656 | tf_op jit(solution)/shard_map/ppermute | solution.py:221
  112.9 28.8 %copy-start.18 = (bf16[4,4,48,256]{3,2,1,0:T(8,128)(2,1)}, bf16[4,4,48,256]{3,2,1,0:T(8,128)(2,1)S(1)}, u32[]{:S(2)}) copy-start(bf16[4,4,48,256]{3,2,1,0:T(8,128)(2,1)S(1)} %collective-permute-done.17) | copy-start | bytes 1179652
  113.0 11.9 %collective-permute-start.18 = (bf16[4,4,48,256]{3,2,1,0:T(8,128)(2,1)S(1)}, bf16[4,4,48,256]{3,2,1,0:T(8,128)(2,1)S(1)}, u32[]{:S(2)}, u32[]{:S(2)}) collective-permute-start(bf16[4,4,48,256]{3,2,1,0:T(8,128)(2,1)S(1)} %collective-permute-done.17), channel_id=1, source_target_pairs={{0,28},{4,0},{8,4},{12,8},{16,12},{20,16},{24,20},{28,24},{1,29},{... | collective-permute-start | bytes 1179656 | tf_op jit(solution)/shard_map/ppermute | solution.py:221
  124.8 16.9 %copy-start.19 = (bf16[4,4,48,256]{3,2,1,0:T(8,128)(2,1)}, bf16[4,4,48,256]{3,2,1,0:T(8,128)(2,1)S(1)}, u32[]{:S(2)}) copy-start(bf16[4,4,48,256]{3,2,1,0:T(8,128)(2,1)S(1)} %collective-permute-done.14) | copy-start | bytes 1179652
  124.8 11.0 %collective-permute-start.15 = (bf16[4,4,48,256]{3,2,1,0:T(8,128)(2,1)S(1)}, bf16[4,4,48,256]{3,2,1,0:T(8,128)(2,1)S(1)}, u32[]{:S(2)}, u32[]{:S(2)}) collective-permute-start(bf16[4,4,48,256]{3,2,1,0:T(8,128)(2,1)S(1)} %collective-permute-done.14), channel_id=1, source_target_pairs={{0,4},{4,8},{8,12},{12,16},{16,20},{20,24},{24,28},{28,0},{1,5},{5... | collective-permute-start | bytes 1179656 | tf_op jit(solution)/shard_map/ppermute | solution.py:221
  124.8 16.9 %copy-start.20 = (bf16[4,4,48,256]{3,2,1,0:T(8,128)(2,1)}, bf16[4,4,48,256]{3,2,1,0:T(8,128)(2,1)S(1)}, u32[]{:S(2)}) copy-start(bf16[4,4,48,256]{3,2,1,0:T(8,128)(2,1)S(1)} %collective-permute-done.18) | copy-start | bytes 1179652
  124.8 11.1 %collective-permute-start.19 = (bf16[4,4,48,256]{3,2,1,0:T(8,128)(2,1)S(1)}, bf16[4,4,48,256]{3,2,1,0:T(8,128)(2,1)S(1)}, u32[]{:S(2)}, u32[]{:S(2)}) collective-permute-start(bf16[4,4,48,256]{3,2,1,0:T(8,128)(2,1)S(1)} %collective-permute-done.18), channel_id=1, source_target_pairs={{0,28},{4,0},{8,4},{12,8},{16,12},{20,16},{24,20},{28,24},{1,29},{... | collective-permute-start | bytes 1179656 | tf_op jit(solution)/shard_map/ppermute | solution.py:221
  127.5 14.2 %copy-start.10 = (bf16[8,4,48,256]{3,2,1,0:T(8,128)(2,1)}, bf16[8,4,48,256]{3,2,1,0:T(8,128)(2,1)S(1)}, u32[]{:S(2)}) copy-start(bf16[8,4,48,256]{3,2,1,0:T(8,128)(2,1)S(1)} %collective-permute-done.28) | copy-start | bytes 2359300
  127.5 14.1 %collective-permute-start.29 = (bf16[4,4,48,256]{3,2,1,0:T(8,128)(2,1)S(1)}, bf16[4,4,48,256]{3,2,1,0:T(8,128)(2,1)S(1)}, u32[]{:S(2)}, u32[]{:S(2)}) collective-permute-start(bf16[4,4,48,256]{3,2,1,0:T(8,128)(2,1)S(1)} %slice.28), channel_id=1, source_target_pairs={{0,1},{1,2},{2,3},{3,0},{4,5},{5,6},{6,7},{7,4},{8,9},{9,10},{10,1... | collective-permute-start | bytes 1179656 | tf_op jit(solution)/shard_map/ppermute | solution.py:221
  127.6 14.1 %copy-start.11 = (bf16[8,4,48,256]{3,2,1,0:T(8,128)(2,1)}, bf16[8,4,48,256]{3,2,1,0:T(8,128)(2,1)S(1)}, u32[]{:S(2)}) copy-start(bf16[8,4,48,256]{3,2,1,0:T(8,128)(2,1)S(1)} %collective-permute-done.30) | copy-start | bytes 2359300
  127.7 14.0 %collective-permute-start.31 = (bf16[4,4,48,256]{3,2,1,0:T(8,128)(2,1)S(1)}, bf16[4,4,48,256]{3,2,1,0:T(8,128)(2,1)S(1)}, u32[]{:S(2)}, u32[]{:S(2)}) collective-permute-start(bf16[4,4,48,256]{3,2,1,0:T(8,128)(2,1)S(1)} %slice.29), channel_id=1, source_target_pairs={{0,3},{1,0},{2,1},{3,2},{4,7},{5,4},{6,5},{7,6},{8,11},{9,8},{10,9... | collective-permute-start | bytes 1179656 | tf_op jit(solution)/shard_map/ppermute | solution.py:221
  135.8 6.0 %copy-start.15 = (bf16[4,4,48,256]{3,2,1,0:T(8,128)(2,1)}, bf16[4,4,48,256]{3,2,1,0:T(8,128)(2,1)S(1)}, u32[]{:S(2)}) copy-start(bf16[4,4,48,256]{3,2,1,0:T(8,128)(2,1)S(1)} %collective-permute-done.15) | copy-start | bytes 1179652
  135.8 5.8 %collective-permute-start.16 = (bf16[2,4,48,256]{3,2,1,0:T(8,128)(2,1)S(1)}, bf16[2,4,48,256]{3,2,1,0:T(8,128)(2,1)S(1)}, u32[]{:S(2)}, u32[]{:S(2)}) collective-permute-start(bf16[2,4,48,256]{3,2,1,0:T(8,128)(2,1)S(1)} %slice.25), channel_id=1, source_target_pairs={{0,4},{4,8},{8,12},{12,16},{16,20},{20,24},{24,28},{28,0},{1,5},{5... | collective-permute-start | bytes 589832 | tf_op jit(solution)/shard_map/ppermute | solution.py:221
  135.9 5.8 %copy-start.16 = (bf16[4,4,48,256]{3,2,1,0:T(8,128)(2,1)}, bf16[4,4,48,256]{3,2,1,0:T(8,128)(2,1)S(1)}, u32[]{:S(2)}) copy-start(bf16[4,4,48,256]{3,2,1,0:T(8,128)(2,1)S(1)} %collective-permute-done.19) | copy-start | bytes 1179652
  136.0 5.7 %collective-permute-start.20 = (bf16[2,4,48,256]{3,2,1,0:T(8,128)(2,1)S(1)}, bf16[2,4,48,256]{3,2,1,0:T(8,128)(2,1)S(1)}, u32[]{:S(2)}, u32[]{:S(2)}) collective-permute-start(bf16[2,4,48,256]{3,2,1,0:T(8,128)(2,1)S(1)} %slice.26), channel_id=1, source_target_pairs={{0,28},{4,0},{8,4},{12,8},{16,12},{20,16},{24,20},{28,24},{1,29},{... | collective-permute-start | bytes 589832 | tf_op jit(solution)/shard_map/ppermute | solution.py:221
  138.7 3.1 %copy-start.13 = (bf16[4,16,64,128]{3,2,1,0:T(8,128)(2,1)}, bf16[4,16,64,128]{3,2,1,0:T(8,128)(2,1)S(1)}, u32[]{:S(2)}) copy-start(bf16[4,16,64,128]{3,2,1,0:T(8,128)(2,1)S(1)} %collective-permute-done.3.other_o) | copy-start | bytes 3145732
  (10 other events, 14.7 us)

commit v3 on v2

--- a/solution.py
+++ b/solution.py
@@ -11,6 +11,7 @@
 SMEM = pl.BlockSpec(memory_space=pltpu.SMEM)
 VMEM = pl.BlockSpec(memory_space=pltpu.VMEM)
 ANY = pl.BlockSpec(memory_space=pl.ANY)
+SPLIT = 5
 
 
 def bf16(*shape):
@@ -68,23 +69,6 @@
         cost_estimate=pl.CostEstimate(flops=0, bytes_accessed=3_000_000, transcendentals=0),
         name="cut_values",
     )(values)
-
-
-def gate_kernel(*refs):
-    pass
-
-
-def gate(value, *after):
-    return pl.pallas_call(
-        gate_kernel,
-        out_shape=jax.ShapeDtypeStruct(value.shape, value.dtype),
-        in_specs=[ANY] * (1 + len(after)),
-        out_specs=ANY,
-        input_output_aliases={0: 0},
-        compiler_params=params(1),
-        cost_estimate=pl.CostEstimate(flops=0, bytes_accessed=0, transcendentals=0),
-        name="gate",
-    )(value, *after)
 
 
 def product_kernel(place, pattern, live, weight, sides, low, own, high, mine, theirs, ext, sems):
@@ -136,22 +120,22 @@
     )(place, pattern, live, weight, sides, low, own, high)
 
 
-def pair_kernel(place, mine, got, *parts):
+def pair_kernel(place, landed, mine, got, *parts):
     for d in range(4):
         at = (place[2] + d) & 3
         parts[d][...] = (mine[at].astype(jnp.float32) + got[at].astype(jnp.float32)).astype(jnp.bfloat16)
 
 
-def pair_sums(place, mine, got):
+def pair_sums(place, landed, mine, got):
     return pl.pallas_call(
         pair_kernel,
         out_shape=(bf16(8, 48, 256),) * 4,
-        in_specs=[SMEM, VMEM, VMEM],
+        in_specs=[SMEM, ANY, VMEM, VMEM],
         out_specs=(VMEM,) * 4,
         compiler_params=params(6),
         cost_estimate=pl.CostEstimate(flops=400_000, bytes_accessed=2_400_000, transcendentals=0),
         name="pair_sums",
-    )(place, mine, got)
+    )(place, landed, mine, got)
 
 
 def apply_kernel(place, source, local, vals_q, own_o, other_o, *rest):
@@ -177,16 +161,21 @@
     same = (e & 1) == core
 
     def run(values_o):
-        total = jnp.zeros((4, 64, 128), jnp.float32)
+        total = jnp.zeros((4, 8, 128), jnp.float32)
         for r in range(16):
             request = device * 16 + r
             src = source[request]
             loc = local[request]
             dx = (x_at - src) & 3
             dz = (z_at - src // 4) & 7
-            at = jnp.where(loc < 4, 16 * dz + 4 * dx + loc, 128 + 32 * dx + 4 * dz + loc - 4)
+            at = jnp.where(
+                loc < SPLIT,
+                SPLIT * (4 * dz + dx) + loc,
+                32 * SPLIT + (8 - SPLIT) * (8 * dx + dz) + loc - SPLIT,
+            )
             applied = lax.dot_general(rows[at], vals_q[0, r], TN, preferred_element_type=jnp.float32)
-            total = total + applied.reshape(4, 64, 128) * values_o[dy, r].astype(jnp.float32)[None]
+            weighted = applied.reshape(4, 8, 8, 128) * values_o[dy, r].astype(jnp.float32).reshape(1, 8, 8, 128)
+            total = total + jnp.sum(weighted, axis=1)
         sums = jnp.sum(total, axis=1)
         for at, c in enumerate((0, 1, 3, 2)):
             out[0, pl.ds(c, 1)] = sums[at : at + 1]
@@ -250,31 +239,32 @@
     own_o = jnp.stack(gathered(orbitals, "y"))
     other_o = lax.ppermute(own_o, "core", swap)
     vals_q = lax.all_to_all(chunks, ("y", "core"), 0, 0, tiled=True)
-    sides = gate(prepare(own), vals_q, own_o)
+    sides = prepare(own)
+    landed = jnp.stack([vals_q[0, 0, :8], own_o[1, 0, :8] + own_o[2, 0, :8] + own_o[3, 0, :8]])
 
     mine, theirs = products(place, pattern_columns, block_orbitals, energy_weight, sides, low, own, high)
     got = lax.ppermute(theirs, "core", swap)
-    parts = pair_sums(place, mine, got)
+    parts = pair_sums(place, landed, mine, got)
     total = parts[0].astype(jnp.float32)
     for d in (1, 2, 3):
         total = total + shifted(parts[d], "y", d).astype(jnp.float32)
     total = total.astype(jnp.bfloat16)
 
-    first = jnp.stack(gathered(total[:4], "x"))
+    seconds, ahead, behind = three_ways(total[SPLIT:])
+    seconds[4] = shifted(ahead, "z", 1)
+    over_x = gathered(total[:SPLIT], "x")
+    first = jnp.stack(over_x)
+    second = jnp.stack([seconds[d] for d in range(8)])
     firsts, ahead, behind = three_ways(first)
     last = [shifted(ahead[:2], "z", 1), shifted(behind[2:], "z", 7)]
     shards = [firsts[d] for d in range(4)] + last + [firsts[d] for d in (5, 6, 7)]
-    seconds, ahead, behind = three_ways(total[4:])
-    seconds[4] = shifted(ahead, "z", 1)
-    second = jnp.stack([seconds[d] for d in range(8)])
     right, left = shifted(second, "x", 1), shifted(second, "x", 3)
     shards += [second, right, shifted(right[:4], "x", 1), shifted(left[4:], "x", 3), left]
 
     sums = applied_sums(
         place, request_source.reshape(-1), request_local, vals_q, own_o, other_o, [flat(s) for s in shards]
     )
-    landed = lax.all_to_all(sums, ("y", "core"), 0, 0, tiled=True)
-    return jnp.sum(landed, axis=0)
+    return jnp.sum(lax.all_to_all(sums, ("y", "core"), 0, 0, tiled=True), axis=0)
 
 
 def solution(mesh):

time: 167 us -> 155 us (0.928)
  waiting for transfers between devices: 58.9 us -> 51.1 us
  starting transfers between devices: 59.3 us -> 54.5 us
  blocking collectives: 12.4 us -> 16.7 us
  local copies, waits for them, and re-layouts: 12.5 us -> 9.18 us
  Pallas kernels: 20.6 us -> 18.7 us
    ppermute x28, waiting for transfers between devices: 57 us -> 42.7 us  [shifted(): lax.ppermute(value, axis, [(n, (n + by) % count) for n in range(count)])]
    ppermute x1, waiting for transfers between devices: 0.01 us -> 4.5 us  [local_program(): low = lax.ppermute(own, ('z', 'x'), [(n, n + 1) for n in range(31)])]
    all_to_all x1, blocking collectives: 12.4 us -> 16.7 us  [local_program(): lax.all_to_all(sums, ('y', 'core'), 0, 0, tiled=True)]
    unnamed x57 -> x55, local copies, waits for them, and re-layouts: 12.3 us -> 8.32 us
    ppermute x1, starting transfers between devices: 5.75 us -> 1.8 us  [local_program(): other_o = lax.ppermute(own_o, 'core', swap)]
    ppermute x1, waiting for transfers between devices: 0.01 us -> 3.86 us  [local_program(): high = lax.ppermute(own, ('z', 'x'), [(n + 1, n) for n in range(31)])]
    ppermute x1, waiting for transfers between devices: 1.91 us -> 0.01 us  [local_program(): got = lax.ppermute(theirs, 'core', swap)]
  transfers between devices with their start and end apart: 33 -> 33, of which waited for: 11 -> 13; matrix products, arithmetic and copies ran while one was open for 1% -> 2% of each run, Pallas kernels for 1% -> 5%
where the time goes in v3:
time: 155 us; the launch traced here: 154 us
  starting transfers between devices  54.5 us (35%)
  waiting for transfers between devices  51.1 us (33%)
  Pallas kernels  18.7 us (12%)
  blocking collectives  16.7 us (11%)
  local copies, waits for them, and re-layouts  9.18 us (6%)
  other arithmetic  2.7 us (2%)
    ppermute x28, waiting for transfers between devices, shifted(): lax.ppermute(value, axis, [(n, (n + by) % count) for n in range(count)])  42.7 us
    ppermute x28, starting transfers between devices, shifted(): lax.ppermute(value, axis, [(n, (n + by) % count) for n in range(count)])  40.1 us
    all_to_all x1, blocking collectives, local_program(): lax.all_to_all(sums, ('y', 'core'), 0, 0, tiled=True)  16.7 us
    pallas_call x1, Pallas kernels, applied_sums(): pl.pallas_call(apply_kernel, grid=(8,), out_shape=jax.ShapeDtypeStruct((8...  10.8 us
    unnamed x55, local copies, waits for them, and re-layouts  8.32 us
    pallas_call x1, Pallas kernels, products(): pl.pallas_call(product_kernel, grid=(8,), out_shape=(bf16(4, 8, 48, 256),...  5.63 us
    all_to_all x1, starting transfers between devices, local_program(): vals_q = lax.all_to_all(chunks, ('y', 'core'), 0, 0, tiled=True)  5.55 us
    ppermute x1, waiting for transfers between devices, local_program(): low = lax.ppermute(own, ('z', 'x'), [(n, n + 1) for n in range(31)])  4.5 us
  transfers between devices with their start and end apart: 33, of which 13 were waited for; matrix products, arithmetic and copies ran while one was open for 2% of the time, Pallas kernels for 5%

profile of v3, /device:TPU:1, one launch (start us, length us, event | category | flops | bytes accessed | tf_op | source)
XLA Modules:
  0.0 154.0 jit_solution(8122099525006519793)
XLA Ops:
  0.0 4.0 %collective-permute-start.4 = (bf16[8,2,128,256]{3,2,1,0:T(8,128)(2,1)}, bf16[8,2,128,256]{3,2,1,0:T(8,128)(2,1)S(1)}, u32[]{:S(2)}, u32[]{:S(2)}) collective-permute-start(bf16[8,2,128,256]{3,2,1,0:T(8,128)(2,1)} %bitcast.50), channel_id=1, source_target_pairs={{0,1},{1,2},{2,3},{3,4},{4,5},{5,6},{6,7},{7,8},{8,9},{9,10},{10,1... | collective-permute-start | bytes 3145736 | tf_op jit(solution)/shard_map/ppermute | solution.py:235
  4.0 1.3 collective-permute-start.5
  5.3 1.4 copy-done.3
  6.7 1.3 cut_values.1
  8.0 5.6 %all-to-all-start = ((bf16[8,16,48,128]{3,2,1,0:T(8,128)(2,1)}), bf16[8,16,48,128]{3,2,1,0:T(8,128)(2,1)}, u32[]{:S(2)}, u32[]{:S(2)}) async-start(bf16[8,16,48,128]{3,2,1,0:T(8,128)(2,1)} %get-tuple-element.13), calls=%async_computation | async-start | bytes 3145728 | tf_op jit(solution)/shard_map/all_to_all | solution.py:241
  13.5 1.4 collective-permute-start
  14.9 2.4 %collective-permute-start.1 = (bf16[16,64,128]{2,1,0:T(8,128)(2,1)S(1)}, bf16[16,64,128]{2,1,0:T(8,128)(2,1)}, u32[]{:S(2)}, u32[]{:S(2)}) collective-permute-start(bf16[16,64,128]{2,1,0:T(8,128)(2,1)S(1)} %get-tuple-element.14), channel_id=1, source_target_pairs={{0,128},{64,192},{128,0},{192,64},{1,129},{65,193},{129,1},{193,65... | collective-permute-start | bytes 786440 | tf_op jit(solution)/shard_map/ppermute | solution.py:210
  17.3 1.2 collective-permute-start.2
  18.8 2.0 %copy-done = bf16[8,4,256,256]{3,2,1,0:T(8,128)(2,1)} copy-done((bf16[8,4,256,256]{3,2,1,0:T(8,128)(2,1)}, bf16[8,4,256,256]{3,2,1,0:T(8,128)(2,1)S(1)}, u32[]{:S(2)}) %copy-start) | copy-done | bytes 4194328
  21.6 4.5 %collective-permute-done.4.low = bf16[8,2,128,256]{3,2,1,0:T(8,128)(2,1)S(1)} collective-permute-done((bf16[8,2,128,256]{3,2,1,0:T(8,128)(2,1)}, bf16[8,2,128,256]{3,2,1,0:T(8,128)(2,1)S(1)}, u32[]{:S(2)}, u32[]{:S(2)}) %collective-permute-start.4) | collective-permute-done | bytes 1048608 | tf_op jit(solution)/shard_map/ppermute | solution.py:235
  26.1 3.9 %collective-permute-done.5.high = bf16[8,2,128,256]{3,2,1,0:T(8,128)(2,1)S(1)} collective-permute-done((bf16[8,2,128,256]{3,2,1,0:T(8,128)(2,1)}, bf16[8,2,128,256]{3,2,1,0:T(8,128)(2,1)S(1)}, u32[]{:S(2)}, u32[]{:S(2)}) %collective-permute-start.5) | collective-permute-done | bytes 1048608 | tf_op jit(solution)/shard_map/ppermute | solution.py:236
  29.9 2.2 %copy-done.1 = bf16[8,4,256,256]{3,2,1,0:T(8,128)(2,1)S(1)} copy-done((bf16[8,4,256,256]{3,2,1,0:T(8,128)(2,1)S(1)}, bf16[8,4,256,256]{3,2,1,0:T(8,128)(2,1)}, u32[]{:S(2)}) %copy-start.1) | copy-done | bytes 4194328
  32.1 5.6 %products.1 = (bf16[4,8,48,256]{3,2,1,0:T(8,128)(2,1)S(1)}, bf16[4,8,48,256]{3,2,1,0:T(8,128)(2,1)}) custom-call(s32[5]{0:T(128)S(1)} %stack.84.place, s32[8,6]{1,0:T(8,128)S(1)} %copy-done.7, s32[256]{0:T(256)S(1)} %copy-done.8, f32[1]{0:T(128)S(6)} %copy.15.weight, bf16[8,4,256,256]{3,2,1,0:T(8,128)(2,1)S(1)} %copy-done.1, ...), custom_call_target="tpu_custom_call" | custom-call | flops 1600000000 | bytes 9000000 | tf_op jit(solution)/shard_map/products/pallas_call | solution.py:110
  37.8 0.9 copy-done.4
  38.7 1.8 %collective-permute-start.6 = (bf16[4,8,48,256]{3,2,1,0:T(8,128)(2,1)}, bf16[4,8,48,256]{3,2,1,0:T(8,128)(2,1)S(1)}, u32[]{:S(2)}, u32[]{:S(2)}) collective-permute-start(bf16[4,8,48,256]{3,2,1,0:T(8,128)(2,1)} %get-tuple-element.16), channel_id=1, source_target_pairs={{0,32},{32,0},{1,33},{33,1},{2,34},{34,2},{3,35},{35,3},{4,36},{36... | collective-permute-start | bytes 2359304 | tf_op jit(solution)/shard_map/ppermute | solution.py:246
  40.4 5.2 %collective-permute-done.1 = bf16[16,64,128]{2,1,0:T(8,128)(2,1)} collective-permute-done((bf16[16,64,128]{2,1,0:T(8,128)(2,1)S(1)}, bf16[16,64,128]{2,1,0:T(8,128)(2,1)}, u32[]{:S(2)}, u32[]{:S(2)}) %collective-permute-start.1) | collective-permute-done | bytes 262176 | tf_op jit(solution)/shard_map/ppermute | solution.py:210
  45.7 0.7 fusion
  46.3 0.7 slice_bitcast_fusion
  47.0 1.1 copy-done.5
  48.2 0.7 pair_sums.1
  49.0 1.2 collective-permute-start.8
  50.2 1.7 %collective-permute-start.9 = (bf16[8,48,256]{2,1,0:T(8,128)(2,1)S(1)}, bf16[8,48,256]{2,1,0:T(8,128)(2,1)S(1)}, u32[]{:S(2)}, u32[]{:S(2)}) collective-permute-start(bf16[8,48,256]{2,1,0:T(8,128)(2,1)S(1)} %get-tuple-element.20), channel_id=1, source_target_pairs={{0,192},{64,0},{128,64},{192,128},{1,193},{65,1},{129,65},{193,129... | collective-permute-start | bytes 589832 | tf_op jit(solution)/shard_map/ppermute | solution.py:210
  51.9 1.2 pad_maximum_fusion.own_o
  53.2 1.8 %collective-permute-start.3 = (bf16[4,16,64,128]{3,2,1,0:T(8,128)(2,1)S(1)}, bf16[4,16,64,128]{3,2,1,0:T(8,128)(2,1)S(1)}, u32[]{:S(2)}, u32[]{:S(2)}) collective-permute-start(bf16[4,16,64,128]{3,2,1,0:T(8,128)(2,1)S(1)} %pad_maximum_fusion.own_o), channel_id=1, source_target_pairs={{0,32},{32,0},{1,33},{33,1},{2,34},{34,2},{3,35},{35,3},{4,36},{36... | collective-permute-start | bytes 3145736 | tf_op jit(solution)/shard_map/ppermute | solution.py:240
  55.0 1.8 %collective-permute-done.7 = bf16[8,48,256]{2,1,0:T(8,128)(2,1)S(1)} collective-permute-done((bf16[8,48,256]{2,1,0:T(8,128)(2,1)S(1)}, bf16[8,48,256]{2,1,0:T(8,128)(2,1)S(1)}, u32[]{:S(2)}, u32[]{:S(2)}) %collective-permute-start.7) | collective-permute-done | bytes 196640 | tf_op jit(solution)/shard_map/ppermute | solution.py:210
  56.8 2.1 %collective-permute-done.8 = bf16[8,48,256]{2,1,0:T(8,128)(2,1)S(1)} collective-permute-done((bf16[8,48,256]{2,1,0:T(8,128)(2,1)S(1)}, bf16[8,48,256]{2,1,0:T(8,128)(2,1)S(1)}, u32[]{:S(2)}, u32[]{:S(2)}) %collective-permute-start.8) | collective-permute-done | bytes 196640 | tf_op jit(solution)/shard_map/ppermute | solution.py:210
  58.8 1.9 %collective-permute-done.9 = bf16[8,48,256]{2,1,0:T(8,128)(2,1)S(1)} collective-permute-done((bf16[8,48,256]{2,1,0:T(8,128)(2,1)S(1)}, bf16[8,48,256]{2,1,0:T(8,128)(2,1)S(1)}, u32[]{:S(2)}, u32[]{:S(2)}) %collective-permute-start.9) | collective-permute-done | bytes 196640 | tf_op jit(solution)/shard_map/ppermute | solution.py:210
  60.9 4.9 %collective-permute-start.21 = (bf16[3,48,256]{2,1,0:T(8,128)(2,1)S(1)}, bf16[3,48,256]{2,1,0:T(8,128)(2,1)S(1)}, u32[]{:S(2)}, u32[]{:S(2)}) collective-permute-start(bf16[3,48,256]{2,1,0:T(8,128)(2,1)S(1)} %slice.47), channel_id=1, source_target_pairs={{0,4},{4,8},{8,12},{12,16},{16,20},{20,24},{24,28},{28,0},{1,5},{5... | collective-permute-start | bytes 221192 | tf_op jit(solution)/shard_map/ppermute | solution.py:210
  65.8 4.0 %collective-permute-start.25 = (bf16[3,48,256]{2,1,0:T(8,128)(2,1)S(1)}, bf16[3,48,256]{2,1,0:T(8,128)(2,1)S(1)}, u32[]{:S(2)}, u32[]{:S(2)}) collective-permute-start(bf16[3,48,256]{2,1,0:T(8,128)(2,1)S(1)} %slice.47), channel_id=1, source_target_pairs={{0,28},{4,0},{8,4},{12,8},{16,12},{20,16},{24,20},{28,24},{1,29},{... | collective-permute-start | bytes 221192 | tf_op jit(solution)/shard_map/ppermute | solution.py:210
  69.9 1.6 %collective-permute-start.11 = (bf16[5,48,256]{2,1,0:T(8,128)(2,1)S(1)}, bf16[5,48,256]{2,1,0:T(8,128)(2,1)S(1)}, u32[]{:S(2)}, u32[]{:S(2)}) collective-permute-start(bf16[5,48,256]{2,1,0:T(8,128)(2,1)S(1)} %get-tuple-element.22), channel_id=1, source_target_pairs={{0,2},{1,3},{2,0},{3,1},{4,6},{5,7},{6,4},{7,5},{8,10},{9,11},{10,... | collective-permute-start | bytes 368648 | tf_op jit(solution)/shard_map/ppermute | solution.py:210
  71.5 1.1 collective-permute-start.12
  72.7 4.0 %collective-permute-done.10 = bf16[5,48,256]{2,1,0:T(8,128)(2,1)S(1)} collective-permute-done((bf16[5,48,256]{2,1,0:T(8,128)(2,1)S(1)}, bf16[5,48,256]{2,1,0:T(8,128)(2,1)S(1)}, u32[]{:S(2)}, u32[]{:S(2)}) %collective-permute-start.10) | collective-permute-done | bytes 122912 | tf_op jit(solution)/shard_map/ppermute | solution.py:210
  76.7 0.8 collective-permute-start.26
  77.6 0.9 collective-permute-start.13
  78.5 2.1 %collective-permute-start.17 = (bf16[4,5,48,256]{3,2,1,0:T(8,128)(2,1)S(1)}, bf16[4,5,48,256]{3,2,1,0:T(8,128)(2,1)S(1)}, u32[]{:S(2)}, u32[]{:S(2)}) collective-permute-start(bf16[4,5,48,256]{3,2,1,0:T(8,128)(2,1)S(1)} %pad_maximum_fusion.1), channel_id=1, source_target_pairs={{0,28},{4,0},{8,4},{12,8},{16,12},{20,16},{24,20},{28,24},{1,29},{... | collective-permute-start | bytes 1474568 | tf_op jit(solution)/shard_map/ppermute | solution.py:210
  80.6 2.7 %collective-permute-start.27 = (bf16[3,48,256]{2,1,0:T(8,128)(2,1)S(1)}, bf16[3,48,256]{2,1,0:T(8,128)(2,1)S(1)}, u32[]{:S(2)}, u32[]{:S(2)}) collective-permute-start(bf16[3,48,256]{2,1,0:T(8,128)(2,1)S(1)} %collective-permute-done.26), channel_id=1, source_target_pairs={{0,28},{4,0},{8,4},{12,8},{16,12},{20,16},{24,20},{28,24},{1,29},{... | collective-permute-start | bytes 221192 | tf_op jit(solution)/shard_map/ppermute | solution.py:210
  83.4 6.5 %collective-permute-done.23 = bf16[3,48,256]{2,1,0:T(8,128)(2,1)S(1)} collective-permute-done((bf16[3,48,256]{2,1,0:T(8,128)(2,1)S(1)}, bf16[3,48,256]{2,1,0:T(8,128)(2,1)S(1)}, u32[]{:S(2)}, u32[]{:S(2)}) %collective-permute-start.23) | collective-permute-done | bytes 73760 | tf_op jit(solution)/shard_map/ppermute | solution.py:210
  89.8 4.6 %collective-permute-done.24 = bf16[3,48,256]{2,1,0:T(8,128)(2,1)S(1)} collective-permute-done((bf16[3,48,256]{2,1,0:T(8,128)(2,1)S(1)}, bf16[3,48,256]{2,1,0:T(8,128)(2,1)S(1)}, u32[]{:S(2)}, u32[]{:S(2)}) %collective-permute-start.24) | collective-permute-done | bytes 73760 | tf_op jit(solution)/shard_map/ppermute | solution.py:210
  94.6 2.6 %collective-permute-start.18 = (bf16[4,5,48,256]{3,2,1,0:T(8,128)(2,1)S(1)}, bf16[4,5,48,256]{3,2,1,0:T(8,128)(2,1)S(1)}, u32[]{:S(2)}, u32[]{:S(2)}) collective-permute-start(bf16[4,5,48,256]{3,2,1,0:T(8,128)(2,1)S(1)} %collective-permute-done.17), channel_id=1, source_target_pairs={{0,28},{4,0},{8,4},{12,8},{16,12},{20,16},{24,20},{28,24},{1,29},{... | collective-permute-start | bytes 1474568 | tf_op jit(solution)/shard_map/ppermute | solution.py:210
  97.3 2.3 %collective-permute-start.28 = (bf16[8,3,48,256]{3,2,1,0:T(8,128)(2,1)S(1)}, bf16[8,3,48,256]{3,2,1,0:T(8,128)(2,1)S(1)}, u32[]{:S(2)}, u32[]{:S(2)}) collective-permute-start(bf16[8,3,48,256]{3,2,1,0:T(8,128)(2,1)S(1)} %bitcast_dynamic-update-slice_fusion), channel_id=1, source_target_pairs={{0,1},{1,2},{2,3},{3,0},{4,5},{5,6},{6,7},{7,4},{8,9},{9,10},{10,1... | collective-permute-start | bytes 1769480 | tf_op jit(solution)/shard_map/ppermute | solution.py:210
  100.0 4.2 %collective-permute-done.14 = bf16[4,5,48,256]{3,2,1,0:T(8,128)(2,1)S(1)} collective-permute-done((bf16[4,5,48,256]{3,2,1,0:T(8,128)(2,1)S(1)}, bf16[4,5,48,256]{3,2,1,0:T(8,128)(2,1)S(1)}, u32[]{:S(2)}, u32[]{:S(2)}) %collective-permute-start.14) | collective-permute-done | bytes 491552 | tf_op jit(solution)/shard_map/ppermute | solution.py:210
  104.3 2.7 %collective-permute-start.19 = (bf16[4,5,48,256]{3,2,1,0:T(8,128)(2,1)S(1)}, bf16[4,5,48,256]{3,2,1,0:T(8,128)(2,1)S(1)}, u32[]{:S(2)}, u32[]{:S(2)}) collective-permute-start(bf16[4,5,48,256]{3,2,1,0:T(8,128)(2,1)S(1)} %collective-permute-done.18), channel_id=1, source_target_pairs={{0,28},{4,0},{8,4},{12,8},{16,12},{20,16},{24,20},{28,24},{1,29},{... | collective-permute-start | bytes 1474568 | tf_op jit(solution)/shard_map/ppermute | solution.py:210
  107.6 2.2 %collective-permute-start.29 = (bf16[4,3,48,256]{3,2,1,0:T(8,128)(2,1)S(1)}, bf16[4,3,48,256]{3,2,1,0:T(8,128)(2,1)S(1)}, u32[]{:S(2)}, u32[]{:S(2)}) collective-permute-start(bf16[4,3,48,256]{3,2,1,0:T(8,128)(2,1)S(1)} %slice.48), channel_id=1, source_target_pairs={{0,1},{1,2},{2,3},{3,0},{4,5},{5,6},{6,7},{7,4},{8,9},{9,10},{10,1... | collective-permute-start | bytes 884744 | tf_op jit(solution)/shard_map/ppermute | solution.py:210
  110.5 5.3 %collective-permute-done.15 = bf16[4,5,48,256]{3,2,1,0:T(8,128)(2,1)S(1)} collective-permute-done((bf16[4,5,48,256]{3,2,1,0:T(8,128)(2,1)S(1)}, bf16[4,5,48,256]{3,2,1,0:T(8,128)(2,1)S(1)}, u32[]{:S(2)}, u32[]{:S(2)}) %collective-permute-start.15) | collective-permute-done | bytes 491552 | tf_op jit(solution)/shard_map/ppermute | solution.py:210
  115.9 2.7 %collective-permute-start.20 = (bf16[2,5,48,256]{3,2,1,0:T(8,128)(2,1)S(1)}, bf16[2,5,48,256]{3,2,1,0:T(8,128)(2,1)}, u32[]{:S(2)}, u32[]{:S(2)}) collective-permute-start(bf16[2,5,48,256]{3,2,1,0:T(8,128)(2,1)S(1)} %slice.46), channel_id=1, source_target_pairs={{0,28},{4,0},{8,4},{12,8},{16,12},{20,16},{24,20},{28,24},{1,29},{... | collective-permute-start | bytes 737288 | tf_op jit(solution)/shard_map/ppermute | solution.py:210
  118.7 6.4 %collective-permute-done.16 = bf16[2,5,48,256]{3,2,1,0:T(8,128)(2,1)S(1)} collective-permute-done((bf16[2,5,48,256]{3,2,1,0:T(8,128)(2,1)S(1)}, bf16[2,5,48,256]{3,2,1,0:T(8,128)(2,1)S(1)}, u32[]{:S(2)}, u32[]{:S(2)}) %collective-permute-start.16) | collective-permute-done | bytes 245792 | tf_op jit(solution)/shard_map/ppermute | solution.py:210
  125.9 10.8 %applied_sums.1 = f32[8,4,128]{2,1,0:T(4,128)} custom-call(s32[5]{0:T(128)} %copy-done.6, s32[4096]{0:T(1024)} %bitcast.71, s32[4096]{0:T(1024)} %local.1, bf16[8,16,48,128]{3,2,1,0:T(8,128)(2,1)} %all-to-all-done.vals_q, bf16[4,16,64,128]{3,2,1,0:T(8,128)(2,1)} %copy-done.9, bf16[4,16,64,128]{3,2,1,0:T(8,128)(2,1)} %copy-done.15, ...), custom_call_target="tpu_custom_call" | custom-call | flops 400000000 | bytes 8000000 | tf_op jit(solution)/shard_map/applied_sums/pallas_call | solution.py:193
  136.7 16.7 %all_to_all.10 = f32[8,4,128]{2,1,0:T(4,128)S(1)} all-to-all(f32[8,4,128]{2,1,0:T(4,128)} %applied_sums.1), channel_id=1, replica_groups=mesh['y'=4,'core'=2,'z'=8,'x'=4] {'y','core'}, dimensions={0} | all-to-all | bytes 32768 | tf_op jit(solution)/shard_map/all_to_all | solution.py:267
  (94 shorter events, 4.2 us)
Async XLA Ops:
  0.0 26.1 %collective-permute-start.4 = (bf16[8,2,128,256]{3,2,1,0:T(8,128)(2,1)}, bf16[8,2,128,256]{3,2,1,0:T(8,128)(2,1)S(1)}, u32[]{:S(2)}, u32[]{:S(2)}) collective-permute-start(bf16[8,2,128,256]{3,2,1,0:T(8,128)(2,1)} %bitcast.50), channel_id=1, source_target_pairs={{0,1},{1,2},{2,3},{3,4},{4,5},{5,6},{6,7},{7,8},{8,9},{9,10},{10,1... | collective-permute-start | bytes 3145736 | tf_op jit(solution)/shard_map/ppermute | solution.py:235
  4.0 25.9 %collective-permute-start.5 = (bf16[8,2,128,256]{3,2,1,0:T(8,128)(2,1)}, bf16[8,2,128,256]{3,2,1,0:T(8,128)(2,1)S(1)}, u32[]{:S(2)}, u32[]{:S(2)}) collective-permute-start(bf16[8,2,128,256]{3,2,1,0:T(8,128)(2,1)} %bitcast.51), channel_id=1, source_target_pairs={{1,0},{2,1},{3,2},{4,3},{5,4},{6,5},{7,6},{8,7},{9,8},{10,9},{11,1... | collective-permute-start | bytes 3145736 | tf_op jit(solution)/shard_map/ppermute | solution.py:236
  8.0 10.5 %copy-start.2 = (bf16[1,8,2,128,256]{4,3,2,1,0:T(8,128)(2,1)S(1)}, bf16[1,8,2,128,256]{4,3,2,1,0:T(8,128)(2,1)}, u32[]{:S(2)}) copy-start(bf16[1,8,2,128,256]{4,3,2,1,0:T(8,128)(2,1)} %param.7) | copy-start | bytes 3145732
  8.0 38.4 %all-to-all-start = ((bf16[8,16,48,128]{3,2,1,0:T(8,128)(2,1)}), bf16[8,16,48,128]{3,2,1,0:T(8,128)(2,1)}, u32[]{:S(2)}, u32[]{:S(2)}) async-start(bf16[8,16,48,128]{3,2,1,0:T(8,128)(2,1)} %get-tuple-element.13), calls=%async_computation | async-start | bytes 3145728 | tf_op jit(solution)/shard_map/all_to_all | solution.py:241
  13.5 26.9 %collective-permute-start = (bf16[16,64,128]{2,1,0:T(8,128)(2,1)S(1)}, bf16[16,64,128]{2,1,0:T(8,128)(2,1)}, u32[]{:S(2)}, u32[]{:S(2)}) collective-permute-start(bf16[16,64,128]{2,1,0:T(8,128)(2,1)S(1)} %get-tuple-element.14), channel_id=1, source_target_pairs={{0,64},{64,128},{128,192},{192,0},{1,65},{65,129},{129,193},{193,1... | collective-permute-start | bytes 786440 | tf_op jit(solution)/shard_map/ppermute | solution.py:210
  14.9 30.7 %collective-permute-start.1 = (bf16[16,64,128]{2,1,0:T(8,128)(2,1)S(1)}, bf16[16,64,128]{2,1,0:T(8,128)(2,1)}, u32[]{:S(2)}, u32[]{:S(2)}) collective-permute-start(bf16[16,64,128]{2,1,0:T(8,128)(2,1)S(1)} %get-tuple-element.14), channel_id=1, source_target_pairs={{0,128},{64,192},{128,0},{192,64},{1,129},{65,193},{129,1},{193,65... | collective-permute-start | bytes 786440 | tf_op jit(solution)/shard_map/ppermute | solution.py:210
  17.3 28.3 %collective-permute-start.2 = (bf16[16,64,128]{2,1,0:T(8,128)(2,1)S(1)}, bf16[16,64,128]{2,1,0:T(8,128)(2,1)}, u32[]{:S(2)}, u32[]{:S(2)}) collective-permute-start(bf16[16,64,128]{2,1,0:T(8,128)(2,1)S(1)} %get-tuple-element.14), channel_id=1, source_target_pairs={{0,192},{64,0},{128,64},{192,128},{1,193},{65,1},{129,65},{193,129... | collective-permute-start | bytes 786440 | tf_op jit(solution)/shard_map/ppermute | solution.py:210
  18.5 11.4 %copy-start.7 = (s32[8,6]{1,0:T(8,128)S(1)}, s32[8,6]{1,0:T(8,128)}, u32[]{:S(2)}) copy-start(s32[8,6]{1,0:T(8,128)} %pattern.1) | copy-start | bytes 580
  18.5 11.4 %copy-start.8 = (s32[256]{0:T(256)S(1)}, s32[256]{0:T(256)}, u32[]{:S(2)}) copy-start(s32[256]{0:T(256)} %live.1) | copy-start | bytes 3076
  21.6 25.5 %copy-start.6 = (s32[5]{0:T(128)}, s32[5]{0:T(128)S(1)}, u32[]{:S(2)}) copy-start(s32[5]{0:T(128)S(1)} %stack.84.place) | copy-start | bytes 64
  38.7 8.4 %collective-permute-start.6 = (bf16[4,8,48,256]{3,2,1,0:T(8,128)(2,1)}, bf16[4,8,48,256]{3,2,1,0:T(8,128)(2,1)S(1)}, u32[]{:S(2)}, u32[]{:S(2)}) collective-permute-start(bf16[4,8,48,256]{3,2,1,0:T(8,128)(2,1)} %get-tuple-element.16), channel_id=1, source_target_pairs={{0,32},{32,0},{1,33},{33,1},{2,34},{34,2},{3,35},{35,3},{4,36},{36... | collective-permute-start | bytes 2359304 | tf_op jit(solution)/shard_map/ppermute | solution.py:246
  48.9 7.9 %collective-permute-start.7 = (bf16[8,48,256]{2,1,0:T(8,128)(2,1)S(1)}, bf16[8,48,256]{2,1,0:T(8,128)(2,1)S(1)}, u32[]{:S(2)}, u32[]{:S(2)}) collective-permute-start(bf16[8,48,256]{2,1,0:T(8,128)(2,1)S(1)} %get-tuple-element.18), channel_id=1, source_target_pairs={{0,64},{64,128},{128,192},{192,0},{1,65},{65,129},{129,193},{193,1... | collective-permute-start | bytes 589832 | tf_op jit(solution)/shard_map/ppermute | solution.py:210
  49.0 9.9 %collective-permute-start.8 = (bf16[8,48,256]{2,1,0:T(8,128)(2,1)S(1)}, bf16[8,48,256]{2,1,0:T(8,128)(2,1)S(1)}, u32[]{:S(2)}, u32[]{:S(2)}) collective-permute-start(bf16[8,48,256]{2,1,0:T(8,128)(2,1)S(1)} %get-tuple-element.19), channel_id=1, source_target_pairs={{0,128},{64,192},{128,0},{192,64},{1,129},{65,193},{129,1},{193,65... | collective-permute-start | bytes 589832 | tf_op jit(solution)/shard_map/ppermute | solution.py:210
  50.2 10.6 %collective-permute-start.9 = (bf16[8,48,256]{2,1,0:T(8,128)(2,1)S(1)}, bf16[8,48,256]{2,1,0:T(8,128)(2,1)S(1)}, u32[]{:S(2)}, u32[]{:S(2)}) collective-permute-start(bf16[8,48,256]{2,1,0:T(8,128)(2,1)S(1)} %get-tuple-element.20), channel_id=1, source_target_pairs={{0,192},{64,0},{128,64},{192,128},{1,193},{65,1},{129,65},{193,129... | collective-permute-start | bytes 589832 | tf_op jit(solution)/shard_map/ppermute | solution.py:210
  53.2 41.3 %copy-start.9 = (bf16[4,16,64,128]{3,2,1,0:T(8,128)(2,1)}, bf16[4,16,64,128]{3,2,1,0:T(8,128)(2,1)S(1)}, u32[]{:S(2)}) copy-start(bf16[4,16,64,128]{3,2,1,0:T(8,128)(2,1)S(1)} %pad_maximum_fusion.own_o) | copy-start | bytes 3145732
  53.2 65.5 %collective-permute-start.3 = (bf16[4,16,64,128]{3,2,1,0:T(8,128)(2,1)S(1)}, bf16[4,16,64,128]{3,2,1,0:T(8,128)(2,1)S(1)}, u32[]{:S(2)}, u32[]{:S(2)}) collective-permute-start(bf16[4,16,64,128]{3,2,1,0:T(8,128)(2,1)S(1)} %pad_maximum_fusion.own_o), channel_id=1, source_target_pairs={{0,32},{32,0},{1,33},{33,1},{2,34},{34,2},{3,35},{35,3},{4,36},{36... | collective-permute-start | bytes 3145736 | tf_op jit(solution)/shard_map/ppermute | solution.py:240
  60.9 10.7 %collective-permute-start.21 = (bf16[3,48,256]{2,1,0:T(8,128)(2,1)S(1)}, bf16[3,48,256]{2,1,0:T(8,128)(2,1)S(1)}, u32[]{:S(2)}, u32[]{:S(2)}) collective-permute-start(bf16[3,48,256]{2,1,0:T(8,128)(2,1)S(1)} %slice.47), channel_id=1, source_target_pairs={{0,4},{4,8},{8,12},{12,16},{16,20},{20,24},{24,28},{28,0},{1,5},{5... | collective-permute-start | bytes 221192 | tf_op jit(solution)/shard_map/ppermute | solution.py:210
  65.8 6.8 %collective-permute-start.25 = (bf16[3,48,256]{2,1,0:T(8,128)(2,1)S(1)}, bf16[3,48,256]{2,1,0:T(8,128)(2,1)S(1)}, u32[]{:S(2)}, u32[]{:S(2)}) collective-permute-start(bf16[3,48,256]{2,1,0:T(8,128)(2,1)S(1)} %slice.47), channel_id=1, source_target_pairs={{0,28},{4,0},{8,4},{12,8},{16,12},{20,16},{24,20},{28,24},{1,29},{... | collective-permute-start | bytes 221192 | tf_op jit(solution)/shard_map/ppermute | solution.py:210
  69.9 6.9 %collective-permute-start.10 = (bf16[5,48,256]{2,1,0:T(8,128)(2,1)S(1)}, bf16[5,48,256]{2,1,0:T(8,128)(2,1)S(1)}, u32[]{:S(2)}, u32[]{:S(2)}) collective-permute-start(bf16[5,48,256]{2,1,0:T(8,128)(2,1)S(1)} %get-tuple-element.22), channel_id=1, source_target_pairs={{0,1},{1,2},{2,3},{3,0},{4,5},{5,6},{6,7},{7,4},{8,9},{9,10},{10,1... | collective-permute-start | bytes 368648 | tf_op jit(solution)/shard_map/ppermute | solution.py:210
  69.9 7.6 %collective-permute-start.11 = (bf16[5,48,256]{2,1,0:T(8,128)(2,1)S(1)}, bf16[5,48,256]{2,1,0:T(8,128)(2,1)S(1)}, u32[]{:S(2)}, u32[]{:S(2)}) collective-permute-start(bf16[5,48,256]{2,1,0:T(8,128)(2,1)S(1)} %get-tuple-element.22), channel_id=1, source_target_pairs={{0,2},{1,3},{2,0},{3,1},{4,6},{5,7},{6,4},{7,5},{8,10},{9,11},{10,... | collective-permute-start | bytes 368648 | tf_op jit(solution)/shard_map/ppermute | solution.py:210
  71.5 6.0 %collective-permute-start.12 = (bf16[5,48,256]{2,1,0:T(8,128)(2,1)S(1)}, bf16[5,48,256]{2,1,0:T(8,128)(2,1)S(1)}, u32[]{:S(2)}, u32[]{:S(2)}) collective-permute-start(bf16[5,48,256]{2,1,0:T(8,128)(2,1)S(1)} %get-tuple-element.22), channel_id=1, source_target_pairs={{0,3},{1,0},{2,1},{3,2},{4,7},{5,4},{6,5},{7,6},{8,11},{9,8},{10,9... | collective-permute-start | bytes 368648 | tf_op jit(solution)/shard_map/ppermute | solution.py:210
  72.7 7.9 %collective-permute-start.22 = (bf16[3,48,256]{2,1,0:T(8,128)(2,1)S(1)}, bf16[3,48,256]{2,1,0:T(8,128)(2,1)S(1)}, u32[]{:S(2)}, u32[]{:S(2)}) collective-permute-start(bf16[3,48,256]{2,1,0:T(8,128)(2,1)S(1)} %collective-permute-done.21), channel_id=1, source_target_pairs={{0,4},{4,8},{8,12},{12,16},{16,20},{20,24},{24,28},{28,0},{1,5},{5... | collective-permute-start | bytes 221192 | tf_op jit(solution)/shard_map/ppermute | solution.py:210
  76.7 3.9 %collective-permute-start.26 = (bf16[3,48,256]{2,1,0:T(8,128)(2,1)S(1)}, bf16[3,48,256]{2,1,0:T(8,128)(2,1)S(1)}, u32[]{:S(2)}, u32[]{:S(2)}) collective-permute-start(bf16[3,48,256]{2,1,0:T(8,128)(2,1)S(1)} %collective-permute-done.25), channel_id=1, source_target_pairs={{0,28},{4,0},{8,4},{12,8},{16,12},{20,16},{24,20},{28,24},{1,29},{... | collective-permute-start | bytes 221192 | tf_op jit(solution)/shard_map/ppermute | solution.py:210
  77.6 47.5 %copy-start.10 = (bf16[4,5,48,256]{3,2,1,0:T(8,128)(2,1)}, bf16[4,5,48,256]{3,2,1,0:T(8,128)(2,1)S(1)}, u32[]{:S(2)}) copy-start(bf16[4,5,48,256]{3,2,1,0:T(8,128)(2,1)S(1)} %pad_maximum_fusion.1) | copy-start | bytes 1474564
  77.6 16.8 %collective-permute-start.13 = (bf16[4,5,48,256]{3,2,1,0:T(8,128)(2,1)S(1)}, bf16[4,5,48,256]{3,2,1,0:T(8,128)(2,1)S(1)}, u32[]{:S(2)}, u32[]{:S(2)}) collective-permute-start(bf16[4,5,48,256]{3,2,1,0:T(8,128)(2,1)S(1)} %pad_maximum_fusion.1), channel_id=1, source_target_pairs={{0,4},{4,8},{8,12},{12,16},{16,20},{20,24},{24,28},{28,0},{1,5},{5... | collective-permute-start | bytes 1474568 | tf_op jit(solution)/shard_map/ppermute | solution.py:210
  78.5 16.1 %collective-permute-start.17 = (bf16[4,5,48,256]{3,2,1,0:T(8,128)(2,1)S(1)}, bf16[4,5,48,256]{3,2,1,0:T(8,128)(2,1)S(1)}, u32[]{:S(2)}, u32[]{:S(2)}) collective-permute-start(bf16[4,5,48,256]{3,2,1,0:T(8,128)(2,1)S(1)} %pad_maximum_fusion.1), channel_id=1, source_target_pairs={{0,28},{4,0},{8,4},{12,8},{16,12},{20,16},{24,20},{28,24},{1,29},{... | collective-permute-start | bytes 1474568 | tf_op jit(solution)/shard_map/ppermute | solution.py:210
  80.6 9.2 %collective-permute-start.23 = (bf16[3,48,256]{2,1,0:T(8,128)(2,1)S(1)}, bf16[3,48,256]{2,1,0:T(8,128)(2,1)S(1)}, u32[]{:S(2)}, u32[]{:S(2)}) collective-permute-start(bf16[3,48,256]{2,1,0:T(8,128)(2,1)S(1)} %collective-permute-done.22), channel_id=1, source_target_pairs={{0,4},{4,8},{8,12},{12,16},{16,20},{20,24},{24,28},{28,0},{1,5},{5... | collective-permute-start | bytes 221192 | tf_op jit(solution)/shard_map/ppermute | solution.py:210
  80.6 13.8 %collective-permute-start.27 = (bf16[3,48,256]{2,1,0:T(8,128)(2,1)S(1)}, bf16[3,48,256]{2,1,0:T(8,128)(2,1)S(1)}, u32[]{:S(2)}, u32[]{:S(2)}) collective-permute-start(bf16[3,48,256]{2,1,0:T(8,128)(2,1)S(1)} %collective-permute-done.26), channel_id=1, source_target_pairs={{0,28},{4,0},{8,4},{12,8},{16,12},{20,16},{24,20},{28,24},{1,29},{... | collective-permute-start | bytes 221192 | tf_op jit(solution)/shard_map/ppermute | solution.py:210
  89.8 4.6 %collective-permute-start.24 = (bf16[3,48,256]{2,1,0:T(8,128)(2,1)S(1)}, bf16[3,48,256]{2,1,0:T(8,128)(2,1)S(1)}, u32[]{:S(2)}, u32[]{:S(2)}) collective-permute-start(bf16[3,48,256]{2,1,0:T(8,128)(2,1)S(1)} %collective-permute-done.23), channel_id=1, source_target_pairs={{0,4},{4,8},{8,12},{12,16},{16,20},{20,24},{24,28},{28,0},{1,5},{5... | collective-permute-start | bytes 221192 | tf_op jit(solution)/shard_map/ppermute | solution.py:210
  94.5 30.7 %copy-start.17 = (bf16[4,5,48,256]{3,2,1,0:T(8,128)(2,1)}, bf16[4,5,48,256]{3,2,1,0:T(8,128)(2,1)S(1)}, u32[]{:S(2)}) copy-start(bf16[4,5,48,256]{3,2,1,0:T(8,128)(2,1)S(1)} %collective-permute-done.13) | copy-start | bytes 1474564
  94.5 9.8 %collective-permute-start.14 = (bf16[4,5,48,256]{3,2,1,0:T(8,128)(2,1)S(1)}, bf16[4,5,48,256]{3,2,1,0:T(8,128)(2,1)S(1)}, u32[]{:S(2)}, u32[]{:S(2)}) collective-permute-start(bf16[4,5,48,256]{3,2,1,0:T(8,128)(2,1)S(1)} %collective-permute-done.13), channel_id=1, source_target_pairs={{0,4},{4,8},{8,12},{12,16},{16,20},{20,24},{24,28},{28,0},{1,5},{5... | collective-permute-start | bytes 1474568 | tf_op jit(solution)/shard_map/ppermute | solution.py:210
  94.6 30.6 %copy-start.18 = (bf16[4,5,48,256]{3,2,1,0:T(8,128)(2,1)}, bf16[4,5,48,256]{3,2,1,0:T(8,128)(2,1)S(1)}, u32[]{:S(2)}) copy-start(bf16[4,5,48,256]{3,2,1,0:T(8,128)(2,1)S(1)} %collective-permute-done.17) | copy-start | bytes 1474564
  94.6 9.7 %collective-permute-start.18 = (bf16[4,5,48,256]{3,2,1,0:T(8,128)(2,1)S(1)}, bf16[4,5,48,256]{3,2,1,0:T(8,128)(2,1)S(1)}, u32[]{:S(2)}, u32[]{:S(2)}) collective-permute-start(bf16[4,5,48,256]{3,2,1,0:T(8,128)(2,1)S(1)} %collective-permute-done.17), channel_id=1, source_target_pairs={{0,28},{4,0},{8,4},{12,8},{16,12},{20,16},{24,20},{28,24},{1,29},{... | collective-permute-start | bytes 1474568 | tf_op jit(solution)/shard_map/ppermute | solution.py:210
  97.3 27.9 %copy-start.16 = (bf16[8,3,48,256]{3,2,1,0:T(8,128)(2,1)}, bf16[8,3,48,256]{3,2,1,0:T(8,128)(2,1)S(1)}, u32[]{:S(2)}) copy-start(bf16[8,3,48,256]{3,2,1,0:T(8,128)(2,1)S(1)} %bitcast_dynamic-update-slice_fusion) | copy-start | bytes 1769476
  97.3 10.3 %collective-permute-start.28 = (bf16[8,3,48,256]{3,2,1,0:T(8,128)(2,1)S(1)}, bf16[8,3,48,256]{3,2,1,0:T(8,128)(2,1)S(1)}, u32[]{:S(2)}, u32[]{:S(2)}) collective-permute-start(bf16[8,3,48,256]{3,2,1,0:T(8,128)(2,1)S(1)} %bitcast_dynamic-update-slice_fusion), channel_id=1, source_target_pairs={{0,1},{1,2},{2,3},{3,0},{4,5},{5,6},{6,7},{7,4},{8,9},{9,10},{10,1... | collective-permute-start | bytes 1769480 | tf_op jit(solution)/shard_map/ppermute | solution.py:210
  99.6 10.2 %collective-permute-start.30 = (bf16[8,3,48,256]{3,2,1,0:T(8,128)(2,1)S(1)}, bf16[8,3,48,256]{3,2,1,0:T(8,128)(2,1)S(1)}, u32[]{:S(2)}, u32[]{:S(2)}) collective-permute-start(bf16[8,3,48,256]{3,2,1,0:T(8,128)(2,1)S(1)} %bitcast_dynamic-update-slice_fusion), channel_id=1, source_target_pairs={{0,3},{1,0},{2,1},{3,2},{4,7},{5,4},{6,5},{7,6},{8,11},{9,8},{10,9... | collective-permute-start | bytes 1769480 | tf_op jit(solution)/shard_map/ppermute | solution.py:210
  104.3 20.9 %copy-start.19 = (bf16[4,5,48,256]{3,2,1,0:T(8,128)(2,1)}, bf16[4,5,48,256]{3,2,1,0:T(8,128)(2,1)S(1)}, u32[]{:S(2)}) copy-start(bf16[4,5,48,256]{3,2,1,0:T(8,128)(2,1)S(1)} %collective-permute-done.14) | copy-start | bytes 1474564
  104.3 11.5 %collective-permute-start.15 = (bf16[4,5,48,256]{3,2,1,0:T(8,128)(2,1)S(1)}, bf16[4,5,48,256]{3,2,1,0:T(8,128)(2,1)S(1)}, u32[]{:S(2)}, u32[]{:S(2)}) collective-permute-start(bf16[4,5,48,256]{3,2,1,0:T(8,128)(2,1)S(1)} %collective-permute-done.14), channel_id=1, source_target_pairs={{0,4},{4,8},{8,12},{12,16},{16,20},{20,24},{24,28},{28,0},{1,5},{5... | collective-permute-start | bytes 1474568 | tf_op jit(solution)/shard_map/ppermute | solution.py:210
  104.3 20.9 %copy-start.20 = (bf16[4,5,48,256]{3,2,1,0:T(8,128)(2,1)}, bf16[4,5,48,256]{3,2,1,0:T(8,128)(2,1)S(1)}, u32[]{:S(2)}) copy-start(bf16[4,5,48,256]{3,2,1,0:T(8,128)(2,1)S(1)} %collective-permute-done.18) | copy-start | bytes 1474564
  104.3 11.6 %collective-permute-start.19 = (bf16[4,5,48,256]{3,2,1,0:T(8,128)(2,1)S(1)}, bf16[4,5,48,256]{3,2,1,0:T(8,128)(2,1)S(1)}, u32[]{:S(2)}, u32[]{:S(2)}) collective-permute-start(bf16[4,5,48,256]{3,2,1,0:T(8,128)(2,1)S(1)} %collective-permute-done.18), channel_id=1, source_target_pairs={{0,28},{4,0},{8,4},{12,8},{16,12},{20,16},{24,20},{28,24},{1,29},{... | collective-permute-start | bytes 1474568 | tf_op jit(solution)/shard_map/ppermute | solution.py:210
  107.6 17.6 %copy-start.11 = (bf16[8,3,48,256]{3,2,1,0:T(8,128)(2,1)}, bf16[8,3,48,256]{3,2,1,0:T(8,128)(2,1)S(1)}, u32[]{:S(2)}) copy-start(bf16[8,3,48,256]{3,2,1,0:T(8,128)(2,1)S(1)} %collective-permute-done.28) | copy-start | bytes 1769476
  107.6 11.1 %collective-permute-start.29 = (bf16[4,3,48,256]{3,2,1,0:T(8,128)(2,1)S(1)}, bf16[4,3,48,256]{3,2,1,0:T(8,128)(2,1)S(1)}, u32[]{:S(2)}, u32[]{:S(2)}) collective-permute-start(bf16[4,3,48,256]{3,2,1,0:T(8,128)(2,1)S(1)} %slice.48), channel_id=1, source_target_pairs={{0,1},{1,2},{2,3},{3,0},{4,5},{5,6},{6,7},{7,4},{8,9},{9,10},{10,1... | collective-permute-start | bytes 884744 | tf_op jit(solution)/shard_map/ppermute | solution.py:210
  109.8 15.4 %copy-start.12 = (bf16[8,3,48,256]{3,2,1,0:T(8,128)(2,1)}, bf16[8,3,48,256]{3,2,1,0:T(8,128)(2,1)S(1)}, u32[]{:S(2)}) copy-start(bf16[8,3,48,256]{3,2,1,0:T(8,128)(2,1)S(1)} %collective-permute-done.30) | copy-start | bytes 1769476
  109.9 8.8 %collective-permute-start.31 = (bf16[4,3,48,256]{3,2,1,0:T(8,128)(2,1)S(1)}, bf16[4,3,48,256]{3,2,1,0:T(8,128)(2,1)S(1)}, u32[]{:S(2)}, u32[]{:S(2)}) collective-permute-start(bf16[4,3,48,256]{3,2,1,0:T(8,128)(2,1)S(1)} %slice.49), channel_id=1, source_target_pairs={{0,3},{1,0},{2,1},{3,2},{4,7},{5,4},{6,5},{7,6},{8,11},{9,8},{10,9... | collective-permute-start | bytes 884744 | tf_op jit(solution)/shard_map/ppermute | solution.py:210
  115.8 9.4 %copy-start.13 = (bf16[4,5,48,256]{3,2,1,0:T(8,128)(2,1)}, bf16[4,5,48,256]{3,2,1,0:T(8,128)(2,1)S(1)}, u32[]{:S(2)}) copy-start(bf16[4,5,48,256]{3,2,1,0:T(8,128)(2,1)S(1)} %collective-permute-done.15) | copy-start | bytes 1474564
  115.8 9.3 %collective-permute-start.16 = (bf16[2,5,48,256]{3,2,1,0:T(8,128)(2,1)S(1)}, bf16[2,5,48,256]{3,2,1,0:T(8,128)(2,1)S(1)}, u32[]{:S(2)}, u32[]{:S(2)}) collective-permute-start(bf16[2,5,48,256]{3,2,1,0:T(8,128)(2,1)S(1)} %slice.45), channel_id=1, source_target_pairs={{0,4},{4,8},{8,12},{12,16},{16,20},{20,24},{24,28},{28,0},{1,5},{5... | collective-permute-start | bytes 737288 | tf_op jit(solution)/shard_map/ppermute | solution.py:210
  115.9 9.3 %copy-start.14 = (bf16[4,5,48,256]{3,2,1,0:T(8,128)(2,1)}, bf16[4,5,48,256]{3,2,1,0:T(8,128)(2,1)S(1)}, u32[]{:S(2)}) copy-start(bf16[4,5,48,256]{3,2,1,0:T(8,128)(2,1)S(1)} %collective-permute-done.19) | copy-start | bytes 1474564
  115.9 9.2 %collective-permute-start.20 = (bf16[2,5,48,256]{3,2,1,0:T(8,128)(2,1)S(1)}, bf16[2,5,48,256]{3,2,1,0:T(8,128)(2,1)}, u32[]{:S(2)}, u32[]{:S(2)}) collective-permute-start(bf16[2,5,48,256]{3,2,1,0:T(8,128)(2,1)S(1)} %slice.46), channel_id=1, source_target_pairs={{0,28},{4,0},{8,4},{12,8},{16,12},{20,16},{24,20},{28,24},{1,29},{... | collective-permute-start | bytes 737288 | tf_op jit(solution)/shard_map/ppermute | solution.py:210
  (9 other events, 28.1 us)

commit v4 on v3

--- a/solution.py
+++ b/solution.py
@@ -22,35 +22,12 @@
     return pltpu.CompilerParams(vmem_limit_bytes=mib * MIB)
 
 
-def prepare_kernel(own, sides):
-    table = (
-        ((0, 0, 1), (0, 1, 1), (0, 0, 1), (1, 1, 1)),
-        ((1, 0, 1), (1, 1, 1), (1, 0, 1), (0, 1, -1)),
-        ((0, 1, 1), (0, 0, 1), (0, 1, -1), (1, 0, -1)),
-        ((1, 1, 1), (1, 0, 1), (1, 1, -1), (0, 0, 1)),
-    )
-
-    def one(i, carry):
-        pieces = {(part, spin): own[i, part, pl.ds(64 * spin, 64), :] for part in range(2) for spin in range(2)}
-        for n, parts in enumerate(table):
-            for c, (part, spin, sign) in enumerate(parts):
-                piece = pieces[part, spin]
-                sides[i, n, pl.ds(64 * c, 64), :] = piece if sign == 1 else -piece
-        return carry
-
-    lax.fori_loop(0, 8, one, 0)
-
-
-def prepare(own):
-    return pl.pallas_call(
-        prepare_kernel,
-        out_shape=bf16(8, 4, 256, 256),
-        in_specs=[VMEM],
-        out_specs=VMEM,
-        compiler_params=params(10),
-        cost_estimate=pl.CostEstimate(flops=0, bytes_accessed=5_000_000, transcendentals=0),
-        name="prepare",
-    )(own)
+SIDES = {
+    (0, 0): ((0, 0, 1), (0, 1, 1), (0, 0, 1), (1, 1, 1)),
+    (0, 1): ((1, 0, 1), (1, 1, 1), (1, 0, 1), (0, 1, -1)),
+    (1, 0): ((0, 1, 1), (0, 0, 1), (0, 1, -1), (1, 0, -1)),
+    (1, 1): ((1, 1, 1), (1, 0, 1), (1, 1, -1), (0, 0, 1)),
+}
 
 
 def cut_kernel(values, chunks, orbitals):
@@ -71,7 +48,7 @@
     )(values)
 
 
-def product_kernel(place, pattern, live, weight, sides, low, own, high, mine, theirs, ext, sems):
+def product_kernel(place, pattern, live, weight, low, own, high, mine, theirs, ext, sems):
     i = pl.program_id(0)
 
     @pl.when(i == 0)
@@ -91,9 +68,11 @@
     row = lax.broadcasted_iota(jnp.int32, (64, 256), 0)
     columns = [pattern[i, k] for k in range(6)]
     total = None
-    for n, (spin, part) in enumerate(((0, 0), (0, 1), (1, 0), (1, 1))):
+    own_pieces = {(part, spin): ext[8 + i, part, pl.ds(64 * spin, 64), :] for part in range(2) for spin in range(2)}
+    for (spin, part), rows in SIDES.items():
+        side = jnp.concatenate([own_pieces[p, s] if sign == 1 else -own_pieces[p, s] for p, s, sign in rows], axis=0)
         left = jnp.concatenate([ext[c - first + 8, part, pl.ds(spin * 64, 64), :] for c in columns], axis=0)
-        term = lax.dot_general(left, sides[0, n], NT, preferred_element_type=jnp.float32)
+        term = lax.dot_general(left, side, NT, preferred_element_type=jnp.float32)
         total = term if total is None else total + term
     kept_row = orbital < live[first + i]
     pieces = []
@@ -105,19 +84,19 @@
     theirs[:, 0] = jnp.where(even, chunks[:, 1], chunks[:, 0]).astype(jnp.bfloat16)
 
 
-def products(place, pattern, live, weight, sides, low, own, high):
+def products(place, pattern, live, weight, low, own, high):
     by_block = pl.BlockSpec((4, 1, 48, 256), lambda i: (0, i, 0, 0))
     return pl.pallas_call(
         product_kernel,
         grid=(8,),
         out_shape=(bf16(4, 8, 48, 256),) * 2,
-        in_specs=[SMEM] * 4 + [pl.BlockSpec((1, 4, 256, 256), lambda i: (i, 0, 0, 0))] + [ANY] * 3,
+        in_specs=[SMEM] * 4 + [ANY] * 3,
         out_specs=(by_block, by_block),
         scratch_shapes=[pltpu.VMEM((24, 2, 128, 256), jnp.bfloat16), pltpu.SemaphoreType.DMA((3,))],
         compiler_params=params(12),
         cost_estimate=pl.CostEstimate(flops=1_600_000_000, bytes_accessed=9_000_000, transcendentals=0),
         name="products",
-    )(place, pattern, live, weight, sides, low, own, high)
+    )(place, pattern, live, weight, low, own, high)
 
 
 def pair_kernel(place, landed, mine, got, *parts):
@@ -199,7 +178,7 @@
         + [ANY] * len(shards),
         out_specs=pl.BlockSpec((1, 4, 128), lambda e: (e, 0, 0)),
         scratch_shapes=[pltpu.VMEM((256, 48, 256), jnp.bfloat16), pltpu.SemaphoreType.DMA((len(shards),))],
-        compiler_params=params(56),
+        compiler_params=params(24),
         cost_estimate=pl.CostEstimate(flops=400_000_000, bytes_accessed=8_000_000, transcendentals=0),
         name="applied_sums",
     )(place, source, local, vals_q, own_o, other_o, *shards)
@@ -239,10 +218,9 @@
     own_o = jnp.stack(gathered(orbitals, "y"))
     other_o = lax.ppermute(own_o, "core", swap)
     vals_q = lax.all_to_all(chunks, ("y", "core"), 0, 0, tiled=True)
-    sides = prepare(own)
     landed = jnp.stack([vals_q[0, 0, :8], own_o[1, 0, :8] + own_o[2, 0, :8] + own_o[3, 0, :8]])
 
-    mine, theirs = products(place, pattern_columns, block_orbitals, energy_weight, sides, low, own, high)
+    mine, theirs = products(place, pattern_columns, block_orbitals, energy_weight, low, own, high)
     got = lax.ppermute(theirs, "core", swap)
     parts = pair_sums(place, landed, mine, got)
     total = parts[0].astype(jnp.float32)

time: 155 us -> 150 us (0.968)
  waiting for transfers between devices: 51.1 us -> 55.6 us
  local copies, waits for them, and re-layouts: 9.18 us -> 5.1 us
  starting transfers between devices: 54.5 us -> 51.5 us
    ppermute x28, waiting for transfers between devices: 42.7 us -> 51.8 us  [shifted(): lax.ppermute(value, axis, [(n, (n + by) % count) for n in range(count)])]
    ppermute x28, starting transfers between devices: 40.1 us -> 32.4 us  [shifted(): lax.ppermute(value, axis, [(n, (n + by) % count) for n in range(count)])]
    ppermute x1, waiting for transfers between devices: 4.5 us -> 0.01 us  [local_program(): low = lax.ppermute(own, ('z', 'x'), [(n, n + 1) for n in range(31)])]
    unnamed x55 -> x23, local copies, waits for them, and re-layouts: 8.32 us -> 4.91 us
    ppermute x1, starting transfers between devices: 1.76 us -> 3.93 us  [local_program(): got = lax.ppermute(theirs, 'core', swap)]
    ppermute x1, starting transfers between devices: 4 us -> 5.58 us  [local_program(): low = lax.ppermute(own, ('z', 'x'), [(n, n + 1) for n in range(31)])]
  transfers between devices with their start and end apart: 33 -> 33, of which waited for: 13 -> 18; matrix products, arithmetic and copies ran while one was open for 2% -> 2% of each run, Pallas kernels for 5% -> 5%
where the time goes in v4:
time: 150 us
  waiting for transfers between devices  55.6 us (37%)
  starting transfers between devices  51.5 us (34%)
  Pallas kernels  18.1 us (12%)
  blocking collectives  15.6 us (10%)
  local copies, waits for them, and re-layouts  5.1 us (3%)
  other arithmetic  2.69 us (2%)
    ppermute x28, waiting for transfers between devices, shifted(): lax.ppermute(value, axis, [(n, (n + by) % count) for n in range(count)])  51.8 us
    ppermute x28, starting transfers between devices, shifted(): lax.ppermute(value, axis, [(n, (n + by) % count) for n in range(count)])  32.4 us
    all_to_all x1, blocking collectives, local_program(): lax.all_to_all(sums, ('y', 'core'), 0, 0, tiled=True)  15.6 us
    pallas_call x1, Pallas kernels, applied_sums(): pl.pallas_call(apply_kernel, grid=(8,), out_shape=jax.ShapeDtypeStruct((8...  9.54 us
    all_to_all x1, starting transfers between devices, local_program(): vals_q = lax.all_to_all(chunks, ('y', 'core'), 0, 0, tiled=True)  6.83 us
    pallas_call x1, Pallas kernels, products(): pl.pallas_call(product_kernel, grid=(8,), out_shape=(bf16(4, 8, 48, 256),...  6.58 us
    ppermute x1, starting transfers between devices, local_program(): low = lax.ppermute(own, ('z', 'x'), [(n, n + 1) for n in range(31)])  5.58 us
    unnamed x23, local copies, waits for them, and re-layouts  4.91 us
  transfers between devices with their start and end apart: 33, of which 18 were waited for; matrix products, arithmetic and copies ran while one was open for 2% of the time, Pallas kernels for 5%

profile of v4, /device:TPU:1, one launch (start us, length us, event | category | flops | bytes accessed | tf_op | source)
XLA Modules:
  0.0 149.5 jit_solution(14945305755919369769)
XLA Ops:
  0.0 1.3 collective-permute-start.5
  1.3 5.6 %collective-permute-start.4 = (bf16[8,2,128,256]{3,2,1,0:T(8,128)(2,1)}, bf16[8,2,128,256]{3,2,1,0:T(8,128)(2,1)}, u32[]{:S(2)}, u32[]{:S(2)}) collective-permute-start(bf16[8,2,128,256]{3,2,1,0:T(8,128)(2,1)} %bitcast.67), channel_id=1, source_target_pairs={{0,1},{1,2},{2,3},{3,4},{4,5},{5,6},{6,7},{7,8},{8,9},{9,10},{10,1... | collective-permute-start | bytes 3145736 | tf_op jit(solution)/shard_map/ppermute | solution.py:214
  6.9 1.4 copy-done
  8.3 1.3 cut_values.1
  9.6 6.8 %all-to-all-start = ((bf16[8,16,48,128]{3,2,1,0:T(8,128)(2,1)}), bf16[8,16,48,128]{3,2,1,0:T(8,128)(2,1)S(1)}, u32[]{:S(2)}, u32[]{:S(2)}) async-start(bf16[8,16,48,128]{3,2,1,0:T(8,128)(2,1)} %get-tuple-element.13), calls=%async_computation | async-start | bytes 3145728 | tf_op jit(solution)/shard_map/all_to_all | solution.py:220
  16.4 2.6 %collective-permute-start.2 = (bf16[16,64,128]{2,1,0:T(8,128)(2,1)S(1)}, bf16[16,64,128]{2,1,0:T(8,128)(2,1)}, u32[]{:S(2)}, u32[]{:S(2)}) collective-permute-start(bf16[16,64,128]{2,1,0:T(8,128)(2,1)S(1)} %get-tuple-element.14), channel_id=1, source_target_pairs={{0,192},{64,0},{128,64},{192,128},{1,193},{65,1},{129,65},{193,129... | collective-permute-start | bytes 786440 | tf_op jit(solution)/shard_map/ppermute | solution.py:189
  19.6 0.6 collective-permute-start
  20.9 3.8 %collective-permute-done.5.high = bf16[8,2,128,256]{3,2,1,0:T(8,128)(2,1)S(1)} collective-permute-done((bf16[8,2,128,256]{3,2,1,0:T(8,128)(2,1)}, bf16[8,2,128,256]{3,2,1,0:T(8,128)(2,1)S(1)}, u32[]{:S(2)}, u32[]{:S(2)}) %collective-permute-start.5) | collective-permute-done | bytes 1048608 | tf_op jit(solution)/shard_map/ppermute | solution.py:215
  24.7 1.0 copy-done.4
  25.7 1.2 copy-done.3
  26.9 1.2 copy-done.5
  28.1 6.6 %products.1 = (bf16[4,8,48,256]{3,2,1,0:T(8,128)(2,1)S(1)}, bf16[4,8,48,256]{3,2,1,0:T(8,128)(2,1)}) custom-call(s32[5]{0:T(128)S(1)} %stack.84.place, s32[8,6]{1,0:T(8,128)S(1)} %copy-done.6, s32[256]{0:T(256)S(1)} %copy-done.7, f32[1]{0:T(128)S(6)} %copy.15.weight, bf16[8,2,128,256]{3,2,1,0:T(8,128)(2,1)} %collective-permute-done.4.low, ...), custom_call_target="tpu_custom_call" | custom-call | flops 1600000000 | bytes 9000000 | tf_op jit(solution)/shard_map/products/pallas_call | solution.py:89
  34.7 3.9 %collective-permute-start.6 = (bf16[4,8,48,256]{3,2,1,0:T(8,128)(2,1)}, bf16[4,8,48,256]{3,2,1,0:T(8,128)(2,1)S(1)}, u32[]{:S(2)}, u32[]{:S(2)}) collective-permute-start(bf16[4,8,48,256]{3,2,1,0:T(8,128)(2,1)} %get-tuple-element.16), channel_id=1, source_target_pairs={{0,32},{32,0},{1,33},{33,1},{2,34},{34,2},{3,35},{35,3},{4,36},{36... | collective-permute-start | bytes 2359304 | tf_op jit(solution)/shard_map/ppermute | solution.py:224
  38.7 2.7 %collective-permute-done.2 = bf16[16,64,128]{2,1,0:T(8,128)(2,1)} collective-permute-done((bf16[16,64,128]{2,1,0:T(8,128)(2,1)S(1)}, bf16[16,64,128]{2,1,0:T(8,128)(2,1)}, u32[]{:S(2)}, u32[]{:S(2)}) %collective-permute-start.2) | collective-permute-done | bytes 262176 | tf_op jit(solution)/shard_map/ppermute | solution.py:189
  41.4 1.5 %collective-permute-done.1 = bf16[16,64,128]{2,1,0:T(8,128)(2,1)} collective-permute-done((bf16[16,64,128]{2,1,0:T(8,128)(2,1)S(1)}, bf16[16,64,128]{2,1,0:T(8,128)(2,1)}, u32[]{:S(2)}, u32[]{:S(2)}) %collective-permute-start.1) | collective-permute-done | bytes 262176 | tf_op jit(solution)/shard_map/ppermute | solution.py:189
  42.9 5.5 %collective-permute-done = bf16[16,64,128]{2,1,0:T(8,128)(2,1)} collective-permute-done((bf16[16,64,128]{2,1,0:T(8,128)(2,1)S(1)}, bf16[16,64,128]{2,1,0:T(8,128)(2,1)}, u32[]{:S(2)}, u32[]{:S(2)}) %collective-permute-start) | collective-permute-done | bytes 262176 | tf_op jit(solution)/shard_map/ppermute | solution.py:189
  48.4 0.7 fusion
  49.1 0.7 pair_sums.1
  50.4 1.8 %collective-permute-start.8 = (bf16[8,48,256]{2,1,0:T(8,128)(2,1)S(1)}, bf16[8,48,256]{2,1,0:T(8,128)(2,1)S(1)}, u32[]{:S(2)}, u32[]{:S(2)}) collective-permute-start(bf16[8,48,256]{2,1,0:T(8,128)(2,1)S(1)} %get-tuple-element.19), channel_id=1, source_target_pairs={{0,128},{64,192},{128,0},{192,64},{1,129},{65,193},{129,1},{193,65... | collective-permute-start | bytes 589832 | tf_op jit(solution)/shard_map/ppermute | solution.py:189
  52.1 0.7 collective-permute-start.9
  52.8 1.2 pad_maximum_fusion.own_o
  54.1 1.5 %collective-permute-start.3 = (bf16[4,16,64,128]{3,2,1,0:T(8,128)(2,1)S(1)}, bf16[4,16,64,128]{3,2,1,0:T(8,128)(2,1)S(1)}, u32[]{:S(2)}, u32[]{:S(2)}) collective-permute-start(bf16[4,16,64,128]{3,2,1,0:T(8,128)(2,1)S(1)} %pad_maximum_fusion.own_o), channel_id=1, source_target_pairs={{0,32},{32,0},{1,33},{33,1},{2,34},{34,2},{3,35},{35,3},{4,36},{36... | collective-permute-start | bytes 3145736 | tf_op jit(solution)/shard_map/ppermute | solution.py:219
  55.6 1.9 %collective-permute-done.7 = bf16[8,48,256]{2,1,0:T(8,128)(2,1)S(1)} collective-permute-done((bf16[8,48,256]{2,1,0:T(8,128)(2,1)S(1)}, bf16[8,48,256]{2,1,0:T(8,128)(2,1)S(1)}, u32[]{:S(2)}, u32[]{:S(2)}) %collective-permute-start.7) | collective-permute-done | bytes 196640 | tf_op jit(solution)/shard_map/ppermute | solution.py:189
  57.5 3.0 %collective-permute-done.8 = bf16[8,48,256]{2,1,0:T(8,128)(2,1)S(1)} collective-permute-done((bf16[8,48,256]{2,1,0:T(8,128)(2,1)S(1)}, bf16[8,48,256]{2,1,0:T(8,128)(2,1)S(1)}, u32[]{:S(2)}, u32[]{:S(2)}) %collective-permute-start.8) | collective-permute-done | bytes 196640 | tf_op jit(solution)/shard_map/ppermute | solution.py:189
  60.4 1.2 collective-permute-done.9
  62.0 4.9 %collective-permute-start.25 = (bf16[3,48,256]{2,1,0:T(8,128)(2,1)S(1)}, bf16[3,48,256]{2,1,0:T(8,128)(2,1)S(1)}, u32[]{:S(2)}, u32[]{:S(2)}) collective-permute-start(bf16[3,48,256]{2,1,0:T(8,128)(2,1)S(1)} %slice.47), channel_id=1, source_target_pairs={{0,28},{4,0},{8,4},{12,8},{16,12},{20,16},{24,20},{28,24},{1,29},{... | collective-permute-start | bytes 221192 | tf_op jit(solution)/shard_map/ppermute | solution.py:189
  67.0 1.7 %collective-permute-start.11 = (bf16[5,48,256]{2,1,0:T(8,128)(2,1)S(1)}, bf16[5,48,256]{2,1,0:T(8,128)(2,1)S(1)}, u32[]{:S(2)}, u32[]{:S(2)}) collective-permute-start(bf16[5,48,256]{2,1,0:T(8,128)(2,1)S(1)} %get-tuple-element.22), channel_id=1, source_target_pairs={{0,2},{1,3},{2,0},{3,1},{4,6},{5,7},{6,4},{7,5},{8,10},{9,11},{10,... | collective-permute-start | bytes 368648 | tf_op jit(solution)/shard_map/ppermute | solution.py:189
  68.7 2.7 %collective-permute-start.12 = (bf16[5,48,256]{2,1,0:T(8,128)(2,1)S(1)}, bf16[5,48,256]{2,1,0:T(8,128)(2,1)S(1)}, u32[]{:S(2)}, u32[]{:S(2)}) collective-permute-start(bf16[5,48,256]{2,1,0:T(8,128)(2,1)S(1)} %get-tuple-element.22), channel_id=1, source_target_pairs={{0,3},{1,0},{2,1},{3,2},{4,7},{5,4},{6,5},{7,6},{8,11},{9,8},{10,9... | collective-permute-start | bytes 368648 | tf_op jit(solution)/shard_map/ppermute | solution.py:189
  71.6 0.7 collective-permute-done.11
  72.3 1.9 %collective-permute-start.26 = (bf16[3,48,256]{2,1,0:T(8,128)(2,1)S(1)}, bf16[3,48,256]{2,1,0:T(8,128)(2,1)S(1)}, u32[]{:S(2)}, u32[]{:S(2)}) collective-permute-start(bf16[3,48,256]{2,1,0:T(8,128)(2,1)S(1)} %collective-permute-done.25), channel_id=1, source_target_pairs={{0,28},{4,0},{8,4},{12,8},{16,12},{20,16},{24,20},{28,24},{1,29},{... | collective-permute-start | bytes 221192 | tf_op jit(solution)/shard_map/ppermute | solution.py:189
  74.3 2.5 %collective-permute-start.17 = (bf16[4,5,48,256]{3,2,1,0:T(8,128)(2,1)S(1)}, bf16[4,5,48,256]{3,2,1,0:T(8,128)(2,1)S(1)}, u32[]{:S(2)}, u32[]{:S(2)}) collective-permute-start(bf16[4,5,48,256]{3,2,1,0:T(8,128)(2,1)S(1)} %pad_maximum_fusion.1), channel_id=1, source_target_pairs={{0,28},{4,0},{8,4},{12,8},{16,12},{20,16},{24,20},{28,24},{1,29},{... | collective-permute-start | bytes 1474568 | tf_op jit(solution)/shard_map/ppermute | solution.py:189
  76.9 2.7 %collective-permute-start.27 = (bf16[3,48,256]{2,1,0:T(8,128)(2,1)S(1)}, bf16[3,48,256]{2,1,0:T(8,128)(2,1)S(1)}, u32[]{:S(2)}, u32[]{:S(2)}) collective-permute-start(bf16[3,48,256]{2,1,0:T(8,128)(2,1)S(1)} %collective-permute-done.26), channel_id=1, source_target_pairs={{0,28},{4,0},{8,4},{12,8},{16,12},{20,16},{24,20},{28,24},{1,29},{... | collective-permute-start | bytes 221192 | tf_op jit(solution)/shard_map/ppermute | solution.py:189
  79.6 9.8 %collective-permute-done.23 = bf16[3,48,256]{2,1,0:T(8,128)(2,1)S(1)} collective-permute-done((bf16[3,48,256]{2,1,0:T(8,128)(2,1)S(1)}, bf16[3,48,256]{2,1,0:T(8,128)(2,1)S(1)}, u32[]{:S(2)}, u32[]{:S(2)}) %collective-permute-start.23) | collective-permute-done | bytes 73760 | tf_op jit(solution)/shard_map/ppermute | solution.py:189
  89.5 4.4 %collective-permute-done.24 = bf16[3,48,256]{2,1,0:T(8,128)(2,1)S(1)} collective-permute-done((bf16[3,48,256]{2,1,0:T(8,128)(2,1)S(1)}, bf16[3,48,256]{2,1,0:T(8,128)(2,1)S(1)}, u32[]{:S(2)}, u32[]{:S(2)}) %collective-permute-start.24) | collective-permute-done | bytes 73760 | tf_op jit(solution)/shard_map/ppermute | solution.py:189
  94.0 1.4 collective-permute-start.14
  95.5 1.6 %collective-permute-start.30 = (bf16[8,3,48,256]{3,2,1,0:T(8,128)(2,1)S(1)}, bf16[8,3,48,256]{3,2,1,0:T(8,128)(2,1)S(1)}, u32[]{:S(2)}, u32[]{:S(2)}) collective-permute-start(bf16[8,3,48,256]{3,2,1,0:T(8,128)(2,1)S(1)} %bitcast_dynamic-update-slice_fusion), channel_id=1, source_target_pairs={{0,3},{1,0},{2,1},{3,2},{4,7},{5,4},{6,5},{7,6},{8,11},{9,8},{10,9... | collective-permute-start | bytes 1769480 | tf_op jit(solution)/shard_map/ppermute | solution.py:189
  97.0 4.6 %collective-permute-done.18 = bf16[4,5,48,256]{3,2,1,0:T(8,128)(2,1)S(1)} collective-permute-done((bf16[4,5,48,256]{3,2,1,0:T(8,128)(2,1)S(1)}, bf16[4,5,48,256]{3,2,1,0:T(8,128)(2,1)S(1)}, u32[]{:S(2)}, u32[]{:S(2)}) %collective-permute-start.18) | collective-permute-done | bytes 491552 | tf_op jit(solution)/shard_map/ppermute | solution.py:189
  101.7 1.2 collective-permute-start.19
  103.4 1.1 collective-permute-done.30
  104.6 2.8 %collective-permute-start.31 = (bf16[4,3,48,256]{3,2,1,0:T(8,128)(2,1)S(1)}, bf16[4,3,48,256]{3,2,1,0:T(8,128)(2,1)S(1)}, u32[]{:S(2)}, u32[]{:S(2)}) collective-permute-start(bf16[4,3,48,256]{3,2,1,0:T(8,128)(2,1)S(1)} %slice.49), channel_id=1, source_target_pairs={{0,3},{1,0},{2,1},{3,2},{4,7},{5,4},{6,5},{7,6},{8,11},{9,8},{10,9... | collective-permute-start | bytes 884744 | tf_op jit(solution)/shard_map/ppermute | solution.py:189
  107.5 5.6 %collective-permute-done.19 = bf16[4,5,48,256]{3,2,1,0:T(8,128)(2,1)S(1)} collective-permute-done((bf16[4,5,48,256]{3,2,1,0:T(8,128)(2,1)S(1)}, bf16[4,5,48,256]{3,2,1,0:T(8,128)(2,1)S(1)}, u32[]{:S(2)}, u32[]{:S(2)}) %collective-permute-start.19) | collective-permute-done | bytes 491552 | tf_op jit(solution)/shard_map/ppermute | solution.py:189
  113.1 1.0 collective-permute-start.20
  115.0 2.8 %collective-permute-done.29 = bf16[4,3,48,256]{3,2,1,0:T(8,128)(2,1)S(1)} collective-permute-done((bf16[4,3,48,256]{3,2,1,0:T(8,128)(2,1)S(1)}, bf16[4,3,48,256]{3,2,1,0:T(8,128)(2,1)S(1)}, u32[]{:S(2)}, u32[]{:S(2)}) %collective-permute-start.29) | collective-permute-done | bytes 294944 | tf_op jit(solution)/shard_map/ppermute | solution.py:189
  117.8 3.4 %collective-permute-done.20 = bf16[2,5,48,256]{3,2,1,0:T(8,128)(2,1)S(1)} collective-permute-done((bf16[2,5,48,256]{3,2,1,0:T(8,128)(2,1)S(1)}, bf16[2,5,48,256]{3,2,1,0:T(8,128)(2,1)S(1)}, u32[]{:S(2)}, u32[]{:S(2)}) %collective-permute-start.20) | collective-permute-done | bytes 245792 | tf_op jit(solution)/shard_map/ppermute | solution.py:189
  121.2 2.6 %collective-permute-done.16 = bf16[2,5,48,256]{3,2,1,0:T(8,128)(2,1)S(1)} collective-permute-done((bf16[2,5,48,256]{3,2,1,0:T(8,128)(2,1)S(1)}, bf16[2,5,48,256]{3,2,1,0:T(8,128)(2,1)S(1)}, u32[]{:S(2)}, u32[]{:S(2)}) %collective-permute-start.16) | collective-permute-done | bytes 245792 | tf_op jit(solution)/shard_map/ppermute | solution.py:189
  123.8 9.5 %applied_sums.1 = f32[8,4,128]{2,1,0:T(4,128)S(1)} custom-call(s32[5]{0:T(128)S(1)} %stack.84.place, s32[4096]{0:T(1024)S(1)} %bitcast.65, s32[4096]{0:T(1024)S(1)} %copy-done.2, bf16[8,16,48,128]{3,2,1,0:T(8,128)(2,1)S(1)} %all-to-all-done.vals_q, bf16[4,16,64,128]{3,2,1,0:T(8,128)(2,1)S(1)} %pad_maximum_fusion.own_o, ...), custom_call_target="tpu_custom_call" | custom-call | flops 400000000 | bytes 8000000 | tf_op jit(solution)/shard_map/applied_sums/pallas_call | solution.py:172
  133.3 15.6 %all_to_all.10 = f32[8,4,128]{2,1,0:T(4,128)S(1)} all-to-all(f32[8,4,128]{2,1,0:T(4,128)S(1)} %applied_sums.1), channel_id=1, replica_groups=mesh['y'=4,'core'=2,'z'=8,'x'=4] {'y','core'}, dimensions={0} | all-to-all | bytes 32768 | tf_op jit(solution)/shard_map/all_to_all | solution.py:245
  148.9 0.6 reduce_sum.9
  (61 shorter events, 3.4 us)
Async XLA Ops:
  0.0 24.7 %collective-permute-start.5 = (bf16[8,2,128,256]{3,2,1,0:T(8,128)(2,1)}, bf16[8,2,128,256]{3,2,1,0:T(8,128)(2,1)S(1)}, u32[]{:S(2)}, u32[]{:S(2)}) collective-permute-start(bf16[8,2,128,256]{3,2,1,0:T(8,128)(2,1)} %bitcast.66), channel_id=1, source_target_pairs={{1,0},{2,1},{3,2},{4,3},{5,4},{6,5},{7,6},{8,7},{9,8},{10,9},{11,1... | collective-permute-start | bytes 3145736 | tf_op jit(solution)/shard_map/ppermute | solution.py:215
  1.3 24.4 %collective-permute-start.4 = (bf16[8,2,128,256]{3,2,1,0:T(8,128)(2,1)}, bf16[8,2,128,256]{3,2,1,0:T(8,128)(2,1)}, u32[]{:S(2)}, u32[]{:S(2)}) collective-permute-start(bf16[8,2,128,256]{3,2,1,0:T(8,128)(2,1)} %bitcast.67), channel_id=1, source_target_pairs={{0,1},{1,2},{2,3},{3,4},{4,5},{5,6},{6,7},{7,8},{8,9},{9,10},{10,1... | collective-permute-start | bytes 3145736 | tf_op jit(solution)/shard_map/ppermute | solution.py:214
  6.9 1.4 copy-start
  9.6 16.1 %copy-start.6 = (s32[8,6]{1,0:T(8,128)S(1)}, s32[8,6]{1,0:T(8,128)}, u32[]{:S(2)}) copy-start(s32[8,6]{1,0:T(8,128)} %pattern.1) | copy-start | bytes 580
  9.6 16.1 %copy-start.7 = (s32[256]{0:T(256)S(1)}, s32[256]{0:T(256)}, u32[]{:S(2)}) copy-start(s32[256]{0:T(256)} %live.1) | copy-start | bytes 3076
  9.6 39.5 %all-to-all-start = ((bf16[8,16,48,128]{3,2,1,0:T(8,128)(2,1)}), bf16[8,16,48,128]{3,2,1,0:T(8,128)(2,1)S(1)}, u32[]{:S(2)}, u32[]{:S(2)}) async-start(bf16[8,16,48,128]{3,2,1,0:T(8,128)(2,1)} %get-tuple-element.13), calls=%async_computation | async-start | bytes 3145728 | tf_op jit(solution)/shard_map/all_to_all | solution.py:220
  16.4 25.0 %collective-permute-start.2 = (bf16[16,64,128]{2,1,0:T(8,128)(2,1)S(1)}, bf16[16,64,128]{2,1,0:T(8,128)(2,1)}, u32[]{:S(2)}, u32[]{:S(2)}) collective-permute-start(bf16[16,64,128]{2,1,0:T(8,128)(2,1)S(1)} %get-tuple-element.14), channel_id=1, source_target_pairs={{0,192},{64,0},{128,64},{192,128},{1,193},{65,1},{129,65},{193,129... | collective-permute-start | bytes 786440 | tf_op jit(solution)/shard_map/ppermute | solution.py:189
  19.0 23.9 %collective-permute-start.1 = (bf16[16,64,128]{2,1,0:T(8,128)(2,1)S(1)}, bf16[16,64,128]{2,1,0:T(8,128)(2,1)}, u32[]{:S(2)}, u32[]{:S(2)}) collective-permute-start(bf16[16,64,128]{2,1,0:T(8,128)(2,1)S(1)} %get-tuple-element.14), channel_id=1, source_target_pairs={{0,128},{64,192},{128,0},{192,64},{1,129},{65,193},{129,1},{193,65... | collective-permute-start | bytes 786440 | tf_op jit(solution)/shard_map/ppermute | solution.py:189
  19.6 28.8 %collective-permute-start = (bf16[16,64,128]{2,1,0:T(8,128)(2,1)S(1)}, bf16[16,64,128]{2,1,0:T(8,128)(2,1)}, u32[]{:S(2)}, u32[]{:S(2)}) collective-permute-start(bf16[16,64,128]{2,1,0:T(8,128)(2,1)S(1)} %get-tuple-element.14), channel_id=1, source_target_pairs={{0,64},{64,128},{128,192},{192,0},{1,65},{65,129},{129,193},{193,1... | collective-permute-start | bytes 786440 | tf_op jit(solution)/shard_map/ppermute | solution.py:189
  24.7 1.0 copy-start.4
  25.7 1.2 copy-start.3
  26.9 1.2 copy-start.5
  34.7 14.3 %collective-permute-start.6 = (bf16[4,8,48,256]{3,2,1,0:T(8,128)(2,1)}, bf16[4,8,48,256]{3,2,1,0:T(8,128)(2,1)S(1)}, u32[]{:S(2)}, u32[]{:S(2)}) collective-permute-start(bf16[4,8,48,256]{3,2,1,0:T(8,128)(2,1)} %get-tuple-element.16), channel_id=1, source_target_pairs={{0,32},{32,0},{1,33},{33,1},{2,34},{34,2},{3,35},{35,3},{4,36},{36... | collective-permute-start | bytes 2359304 | tf_op jit(solution)/shard_map/ppermute | solution.py:224
  49.8 7.7 %collective-permute-start.7 = (bf16[8,48,256]{2,1,0:T(8,128)(2,1)S(1)}, bf16[8,48,256]{2,1,0:T(8,128)(2,1)S(1)}, u32[]{:S(2)}, u32[]{:S(2)}) collective-permute-start(bf16[8,48,256]{2,1,0:T(8,128)(2,1)S(1)} %get-tuple-element.18), channel_id=1, source_target_pairs={{0,64},{64,128},{128,192},{192,0},{1,65},{65,129},{129,193},{193,1... | collective-permute-start | bytes 589832 | tf_op jit(solution)/shard_map/ppermute | solution.py:189
  50.4 10.1 %collective-permute-start.8 = (bf16[8,48,256]{2,1,0:T(8,128)(2,1)S(1)}, bf16[8,48,256]{2,1,0:T(8,128)(2,1)S(1)}, u32[]{:S(2)}, u32[]{:S(2)}) collective-permute-start(bf16[8,48,256]{2,1,0:T(8,128)(2,1)S(1)} %get-tuple-element.19), channel_id=1, source_target_pairs={{0,128},{64,192},{128,0},{192,64},{1,129},{65,193},{129,1},{193,65... | collective-permute-start | bytes 589832 | tf_op jit(solution)/shard_map/ppermute | solution.py:189
  52.1 9.6 %collective-permute-start.9 = (bf16[8,48,256]{2,1,0:T(8,128)(2,1)S(1)}, bf16[8,48,256]{2,1,0:T(8,128)(2,1)S(1)}, u32[]{:S(2)}, u32[]{:S(2)}) collective-permute-start(bf16[8,48,256]{2,1,0:T(8,128)(2,1)S(1)} %get-tuple-element.20), channel_id=1, source_target_pairs={{0,192},{64,0},{128,64},{192,128},{1,193},{65,1},{129,65},{193,129... | collective-permute-start | bytes 589832 | tf_op jit(solution)/shard_map/ppermute | solution.py:189
  54.1 60.9 %collective-permute-start.3 = (bf16[4,16,64,128]{3,2,1,0:T(8,128)(2,1)S(1)}, bf16[4,16,64,128]{3,2,1,0:T(8,128)(2,1)S(1)}, u32[]{:S(2)}, u32[]{:S(2)}) collective-permute-start(bf16[4,16,64,128]{3,2,1,0:T(8,128)(2,1)S(1)} %pad_maximum_fusion.own_o), channel_id=1, source_target_pairs={{0,32},{32,0},{1,33},{33,1},{2,34},{34,2},{3,35},{35,3},{4,36},{36... | collective-permute-start | bytes 3145736 | tf_op jit(solution)/shard_map/ppermute | solution.py:219
  61.8 6.9 %collective-permute-start.21 = (bf16[3,48,256]{2,1,0:T(8,128)(2,1)S(1)}, bf16[3,48,256]{2,1,0:T(8,128)(2,1)S(1)}, u32[]{:S(2)}, u32[]{:S(2)}) collective-permute-start(bf16[3,48,256]{2,1,0:T(8,128)(2,1)S(1)} %slice.47), channel_id=1, source_target_pairs={{0,4},{4,8},{8,12},{12,16},{16,20},{20,24},{24,28},{28,0},{1,5},{5... | collective-permute-start | bytes 221192 | tf_op jit(solution)/shard_map/ppermute | solution.py:189
  62.0 9.4 %collective-permute-start.25 = (bf16[3,48,256]{2,1,0:T(8,128)(2,1)S(1)}, bf16[3,48,256]{2,1,0:T(8,128)(2,1)S(1)}, u32[]{:S(2)}, u32[]{:S(2)}) collective-permute-start(bf16[3,48,256]{2,1,0:T(8,128)(2,1)S(1)} %slice.47), channel_id=1, source_target_pairs={{0,28},{4,0},{8,4},{12,8},{16,12},{20,16},{24,20},{28,24},{1,29},{... | collective-permute-start | bytes 221192 | tf_op jit(solution)/shard_map/ppermute | solution.py:189
  67.0 5.3 %collective-permute-start.11 = (bf16[5,48,256]{2,1,0:T(8,128)(2,1)S(1)}, bf16[5,48,256]{2,1,0:T(8,128)(2,1)S(1)}, u32[]{:S(2)}, u32[]{:S(2)}) collective-permute-start(bf16[5,48,256]{2,1,0:T(8,128)(2,1)S(1)} %get-tuple-element.22), channel_id=1, source_target_pairs={{0,2},{1,3},{2,0},{3,1},{4,6},{5,7},{6,4},{7,5},{8,10},{9,11},{10,... | collective-permute-start | bytes 368648 | tf_op jit(solution)/shard_map/ppermute | solution.py:189
  68.7 5.5 %collective-permute-start.10 = (bf16[5,48,256]{2,1,0:T(8,128)(2,1)S(1)}, bf16[5,48,256]{2,1,0:T(8,128)(2,1)S(1)}, u32[]{:S(2)}, u32[]{:S(2)}) collective-permute-start(bf16[5,48,256]{2,1,0:T(8,128)(2,1)S(1)} %get-tuple-element.22), channel_id=1, source_target_pairs={{0,1},{1,2},{2,3},{3,0},{4,5},{5,6},{6,7},{7,4},{8,9},{9,10},{10,1... | collective-permute-start | bytes 368648 | tf_op jit(solution)/shard_map/ppermute | solution.py:189
  68.7 5.5 %collective-permute-start.12 = (bf16[5,48,256]{2,1,0:T(8,128)(2,1)S(1)}, bf16[5,48,256]{2,1,0:T(8,128)(2,1)S(1)}, u32[]{:S(2)}, u32[]{:S(2)}) collective-permute-start(bf16[5,48,256]{2,1,0:T(8,128)(2,1)S(1)} %get-tuple-element.22), channel_id=1, source_target_pairs={{0,3},{1,0},{2,1},{3,2},{4,7},{5,4},{6,5},{7,6},{8,11},{9,8},{10,9... | collective-permute-start | bytes 368648 | tf_op jit(solution)/shard_map/ppermute | solution.py:189
  71.5 5.4 %collective-permute-start.22 = (bf16[3,48,256]{2,1,0:T(8,128)(2,1)S(1)}, bf16[3,48,256]{2,1,0:T(8,128)(2,1)S(1)}, u32[]{:S(2)}, u32[]{:S(2)}) collective-permute-start(bf16[3,48,256]{2,1,0:T(8,128)(2,1)S(1)} %collective-permute-done.21), channel_id=1, source_target_pairs={{0,4},{4,8},{8,12},{12,16},{16,20},{20,24},{24,28},{28,0},{1,5},{5... | collective-permute-start | bytes 221192 | tf_op jit(solution)/shard_map/ppermute | solution.py:189
  72.3 4.6 %collective-permute-start.26 = (bf16[3,48,256]{2,1,0:T(8,128)(2,1)S(1)}, bf16[3,48,256]{2,1,0:T(8,128)(2,1)S(1)}, u32[]{:S(2)}, u32[]{:S(2)}) collective-permute-start(bf16[3,48,256]{2,1,0:T(8,128)(2,1)S(1)} %collective-permute-done.25), channel_id=1, source_target_pairs={{0,28},{4,0},{8,4},{12,8},{16,12},{20,16},{24,20},{28,24},{1,29},{... | collective-permute-start | bytes 221192 | tf_op jit(solution)/shard_map/ppermute | solution.py:189
  74.3 49.5 %copy-start.1 = (s32[4096,1]{0,1:T(1,128)S(1)}, s32[4096,1]{0,1:T(1,128)}, u32[]{:S(2)}) copy-start(s32[4096,1]{0,1:T(1,128)} %param.11) | copy-start | bytes 49156
  74.3 49.5 %copy-start.2 = (s32[4096]{0:T(1024)S(1)}, s32[4096]{0:T(1024)}, u32[]{:S(2)}) copy-start(s32[4096]{0:T(1024)} %local.1) | copy-start | bytes 49156
  74.3 19.6 %collective-permute-start.17 = (bf16[4,5,48,256]{3,2,1,0:T(8,128)(2,1)S(1)}, bf16[4,5,48,256]{3,2,1,0:T(8,128)(2,1)S(1)}, u32[]{:S(2)}, u32[]{:S(2)}) collective-permute-start(bf16[4,5,48,256]{3,2,1,0:T(8,128)(2,1)S(1)} %pad_maximum_fusion.1), channel_id=1, source_target_pairs={{0,28},{4,0},{8,4},{12,8},{16,12},{20,16},{24,20},{28,24},{1,29},{... | collective-permute-start | bytes 1474568 | tf_op jit(solution)/shard_map/ppermute | solution.py:189
  76.9 17.1 %collective-permute-start.13 = (bf16[4,5,48,256]{3,2,1,0:T(8,128)(2,1)S(1)}, bf16[4,5,48,256]{3,2,1,0:T(8,128)(2,1)S(1)}, u32[]{:S(2)}, u32[]{:S(2)}) collective-permute-start(bf16[4,5,48,256]{3,2,1,0:T(8,128)(2,1)S(1)} %pad_maximum_fusion.1), channel_id=1, source_target_pairs={{0,4},{4,8},{8,12},{12,16},{16,20},{20,24},{24,28},{28,0},{1,5},{5... | collective-permute-start | bytes 1474568 | tf_op jit(solution)/shard_map/ppermute | solution.py:189
  76.9 12.6 %collective-permute-start.23 = (bf16[3,48,256]{2,1,0:T(8,128)(2,1)S(1)}, bf16[3,48,256]{2,1,0:T(8,128)(2,1)S(1)}, u32[]{:S(2)}, u32[]{:S(2)}) collective-permute-start(bf16[3,48,256]{2,1,0:T(8,128)(2,1)S(1)} %collective-permute-done.22), channel_id=1, source_target_pairs={{0,4},{4,8},{8,12},{12,16},{16,20},{20,24},{24,28},{28,0},{1,5},{5... | collective-permute-start | bytes 221192 | tf_op jit(solution)/shard_map/ppermute | solution.py:189
  76.9 17.0 %collective-permute-start.27 = (bf16[3,48,256]{2,1,0:T(8,128)(2,1)S(1)}, bf16[3,48,256]{2,1,0:T(8,128)(2,1)S(1)}, u32[]{:S(2)}, u32[]{:S(2)}) collective-permute-start(bf16[3,48,256]{2,1,0:T(8,128)(2,1)S(1)} %collective-permute-done.26), channel_id=1, source_target_pairs={{0,28},{4,0},{8,4},{12,8},{16,12},{20,16},{24,20},{28,24},{1,29},{... | collective-permute-start | bytes 221192 | tf_op jit(solution)/shard_map/ppermute | solution.py:189
  89.4 4.4 %collective-permute-start.24 = (bf16[3,48,256]{2,1,0:T(8,128)(2,1)S(1)}, bf16[3,48,256]{2,1,0:T(8,128)(2,1)S(1)}, u32[]{:S(2)}, u32[]{:S(2)}) collective-permute-start(bf16[3,48,256]{2,1,0:T(8,128)(2,1)S(1)} %collective-permute-done.23), channel_id=1, source_target_pairs={{0,4},{4,8},{8,12},{12,16},{16,20},{20,24},{24,28},{28,0},{1,5},{5... | collective-permute-start | bytes 221192 | tf_op jit(solution)/shard_map/ppermute | solution.py:189
  93.9 7.8 %collective-permute-start.18 = (bf16[4,5,48,256]{3,2,1,0:T(8,128)(2,1)S(1)}, bf16[4,5,48,256]{3,2,1,0:T(8,128)(2,1)S(1)}, u32[]{:S(2)}, u32[]{:S(2)}) collective-permute-start(bf16[4,5,48,256]{3,2,1,0:T(8,128)(2,1)S(1)} %collective-permute-done.17), channel_id=1, source_target_pairs={{0,28},{4,0},{8,4},{12,8},{16,12},{20,16},{24,20},{28,24},{1,29},{... | collective-permute-start | bytes 1474568 | tf_op jit(solution)/shard_map/ppermute | solution.py:189
  94.0 9.4 %collective-permute-start.14 = (bf16[4,5,48,256]{3,2,1,0:T(8,128)(2,1)S(1)}, bf16[4,5,48,256]{3,2,1,0:T(8,128)(2,1)S(1)}, u32[]{:S(2)}, u32[]{:S(2)}) collective-permute-start(bf16[4,5,48,256]{3,2,1,0:T(8,128)(2,1)S(1)} %collective-permute-done.13), channel_id=1, source_target_pairs={{0,4},{4,8},{8,12},{12,16},{16,20},{20,24},{24,28},{28,0},{1,5},{5... | collective-permute-start | bytes 1474568 | tf_op jit(solution)/shard_map/ppermute | solution.py:189
  95.5 9.1 %collective-permute-start.30 = (bf16[8,3,48,256]{3,2,1,0:T(8,128)(2,1)S(1)}, bf16[8,3,48,256]{3,2,1,0:T(8,128)(2,1)S(1)}, u32[]{:S(2)}, u32[]{:S(2)}) collective-permute-start(bf16[8,3,48,256]{3,2,1,0:T(8,128)(2,1)S(1)} %bitcast_dynamic-update-slice_fusion), channel_id=1, source_target_pairs={{0,3},{1,0},{2,1},{3,2},{4,7},{5,4},{6,5},{7,6},{8,11},{9,8},{10,9... | collective-permute-start | bytes 1769480 | tf_op jit(solution)/shard_map/ppermute | solution.py:189
  97.0 10.3 %collective-permute-start.28 = (bf16[8,3,48,256]{3,2,1,0:T(8,128)(2,1)S(1)}, bf16[8,3,48,256]{3,2,1,0:T(8,128)(2,1)S(1)}, u32[]{:S(2)}, u32[]{:S(2)}) collective-permute-start(bf16[8,3,48,256]{3,2,1,0:T(8,128)(2,1)S(1)} %bitcast_dynamic-update-slice_fusion), channel_id=1, source_target_pairs={{0,1},{1,2},{2,3},{3,0},{4,5},{5,6},{6,7},{7,4},{8,9},{9,10},{10,1... | collective-permute-start | bytes 1769480 | tf_op jit(solution)/shard_map/ppermute | solution.py:189
  101.7 11.5 %collective-permute-start.19 = (bf16[4,5,48,256]{3,2,1,0:T(8,128)(2,1)S(1)}, bf16[4,5,48,256]{3,2,1,0:T(8,128)(2,1)S(1)}, u32[]{:S(2)}, u32[]{:S(2)}) collective-permute-start(bf16[4,5,48,256]{3,2,1,0:T(8,128)(2,1)S(1)} %collective-permute-done.18), channel_id=1, source_target_pairs={{0,28},{4,0},{8,4},{12,8},{16,12},{20,16},{24,20},{28,24},{1,29},{... | collective-permute-start | bytes 1474568 | tf_op jit(solution)/shard_map/ppermute | solution.py:189
  103.4 11.0 %collective-permute-start.15 = (bf16[4,5,48,256]{3,2,1,0:T(8,128)(2,1)S(1)}, bf16[4,5,48,256]{3,2,1,0:T(8,128)(2,1)S(1)}, u32[]{:S(2)}, u32[]{:S(2)}) collective-permute-start(bf16[4,5,48,256]{3,2,1,0:T(8,128)(2,1)S(1)} %collective-permute-done.14), channel_id=1, source_target_pairs={{0,4},{4,8},{8,12},{12,16},{16,20},{20,24},{24,28},{28,0},{1,5},{5... | collective-permute-start | bytes 1474568 | tf_op jit(solution)/shard_map/ppermute | solution.py:189
  104.6 10.4 %collective-permute-start.31 = (bf16[4,3,48,256]{3,2,1,0:T(8,128)(2,1)S(1)}, bf16[4,3,48,256]{3,2,1,0:T(8,128)(2,1)S(1)}, u32[]{:S(2)}, u32[]{:S(2)}) collective-permute-start(bf16[4,3,48,256]{3,2,1,0:T(8,128)(2,1)S(1)} %slice.49), channel_id=1, source_target_pairs={{0,3},{1,0},{2,1},{3,2},{4,7},{5,4},{6,5},{7,6},{8,11},{9,8},{10,9... | collective-permute-start | bytes 884744 | tf_op jit(solution)/shard_map/ppermute | solution.py:189
  107.4 10.4 %collective-permute-start.29 = (bf16[4,3,48,256]{3,2,1,0:T(8,128)(2,1)S(1)}, bf16[4,3,48,256]{3,2,1,0:T(8,128)(2,1)S(1)}, u32[]{:S(2)}, u32[]{:S(2)}) collective-permute-start(bf16[4,3,48,256]{3,2,1,0:T(8,128)(2,1)S(1)} %slice.48), channel_id=1, source_target_pairs={{0,1},{1,2},{2,3},{3,0},{4,5},{5,6},{6,7},{7,4},{8,9},{9,10},{10,1... | collective-permute-start | bytes 884744 | tf_op jit(solution)/shard_map/ppermute | solution.py:189
  113.1 8.1 %collective-permute-start.20 = (bf16[2,5,48,256]{3,2,1,0:T(8,128)(2,1)S(1)}, bf16[2,5,48,256]{3,2,1,0:T(8,128)(2,1)S(1)}, u32[]{:S(2)}, u32[]{:S(2)}) collective-permute-start(bf16[2,5,48,256]{3,2,1,0:T(8,128)(2,1)S(1)} %slice.46), channel_id=1, source_target_pairs={{0,28},{4,0},{8,4},{12,8},{16,12},{20,16},{24,20},{28,24},{1,29},{... | collective-permute-start | bytes 737288 | tf_op jit(solution)/shard_map/ppermute | solution.py:189
  114.5 9.3 %collective-permute-start.16 = (bf16[2,5,48,256]{3,2,1,0:T(8,128)(2,1)S(1)}, bf16[2,5,48,256]{3,2,1,0:T(8,128)(2,1)S(1)}, u32[]{:S(2)}, u32[]{:S(2)}) collective-permute-start(bf16[2,5,48,256]{3,2,1,0:T(8,128)(2,1)S(1)} %slice.45), channel_id=1, source_target_pairs={{0,4},{4,8},{8,12},{12,16},{16,20},{20,24},{24,28},{28,0},{1,5},{5... | collective-permute-start | bytes 737288 | tf_op jit(solution)/shard_map/ppermute | solution.py:189

commit v5 on v4

--- a/solution.py
+++ b/solution.py
@@ -93,7 +93,7 @@
         in_specs=[SMEM] * 4 + [ANY] * 3,
         out_specs=(by_block, by_block),
         scratch_shapes=[pltpu.VMEM((24, 2, 128, 256), jnp.bfloat16), pltpu.SemaphoreType.DMA((3,))],
-        compiler_params=params(12),
+        compiler_params=params(56),
         cost_estimate=pl.CostEstimate(flops=1_600_000_000, bytes_accessed=9_000_000, transcendentals=0),
         name="products",
     )(place, pattern, live, weight, low, own, high)

time: 150 us -> 151 us (level)
  starting transfers between devices: 51.5 us -> 54 us
  local copies, waits for them, and re-layouts: 5.1 us -> 3.31 us
  other arithmetic: 2.69 us -> 0.91 us
    ppermute x28, starting transfers between devices: 32.4 us -> 35 us  [shifted(): lax.ppermute(value, axis, [(n, (n + by) % count) for n in range(count)])]
    unnamed x23 -> x17, local copies, waits for them, and re-layouts: 4.91 us -> 2.59 us
  transfers between devices with their start and end apart: 33 -> 33, of which waited for: 18 -> 18; matrix products, arithmetic and copies ran while one was open for 2% -> 1% of each run, Pallas kernels for 5% -> 6%
where the time goes in v5:
time: 151 us; the launch traced here: 150 us
  waiting for transfers between devices  55.7 us (37%)
  starting transfers between devices  54 us (36%)
  Pallas kernels  19.1 us (13%)
  blocking collectives  16.4 us (11%)
  local copies, waits for them, and re-layouts  3.31 us (2%)
    ppermute x28, waiting for transfers between devices, shifted(): lax.ppermute(value, axis, [(n, (n + by) % count) for n in range(count)])  51.3 us
    ppermute x28, starting transfers between devices, shifted(): lax.ppermute(value, axis, [(n, (n + by) % count) for n in range(count)])  35 us
    all_to_all x1, blocking collectives, local_program(): lax.all_to_all(sums, ('y', 'core'), 0, 0, tiled=True)  16.4 us
    pallas_call x1, Pallas kernels, applied_sums(): pl.pallas_call(apply_kernel, grid=(8,), out_shape=jax.ShapeDtypeStruct((8...  9.53 us
    pallas_call x1, Pallas kernels, products(): pl.pallas_call(product_kernel, grid=(8,), out_shape=(bf16(4, 8, 48, 256),...  7.55 us
    all_to_all x1, starting transfers between devices, local_program(): vals_q = lax.all_to_all(chunks, ('y', 'core'), 0, 0, tiled=True)  6.7 us
    ppermute x1, starting transfers between devices, local_program(): low = lax.ppermute(own, ('z', 'x'), [(n, n + 1) for n in range(31)])  5.57 us
    ppermute x1, starting transfers between devices, local_program(): got = lax.ppermute(theirs, 'core', swap)  3.94 us
  transfers between devices with their start and end apart: 33, of which 18 were waited for; matrix products, arithmetic and copies ran while one was open for 1% of the time, Pallas kernels for 6%

profile of v5, /device:TPU:1, one launch (start us, length us, event | category | flops | bytes accessed | tf_op | source)
XLA Modules:
  0.0 150.3 jit_solution(4892520752572386239)
XLA Ops:
  0.0 1.3 collective-permute-start.5
  1.3 5.6 %collective-permute-start.4 = (bf16[8,2,128,256]{3,2,1,0:T(8,128)(2,1)}, bf16[8,2,128,256]{3,2,1,0:T(8,128)(2,1)}, u32[]{:S(2)}, u32[]{:S(2)}) collective-permute-start(bf16[8,2,128,256]{3,2,1,0:T(8,128)(2,1)} %bitcast.76), channel_id=1, source_target_pairs={{0,1},{1,2},{2,3},{3,4},{4,5},{5,6},{6,7},{7,8},{8,9},{9,10},{10,1... | collective-permute-start | bytes 3145736 | tf_op jit(solution)/shard_map/ppermute | solution.py:214
  6.9 1.4 copy-done
  8.3 1.3 cut_values.1
  9.6 6.7 %all-to-all-start = ((bf16[8,16,48,128]{3,2,1,0:T(8,128)(2,1)}), bf16[8,16,48,128]{3,2,1,0:T(8,128)(2,1)S(1)}, u32[]{:S(2)}, u32[]{:S(2)}) async-start(bf16[8,16,48,128]{3,2,1,0:T(8,128)(2,1)} %get-tuple-element.13), calls=%async_computation | async-start | bytes 3145728 | tf_op jit(solution)/shard_map/all_to_all | solution.py:220
  16.3 2.6 %collective-permute-start.2 = (bf16[16,64,128]{2,1,0:T(8,128)(2,1)S(1)}, bf16[16,64,128]{2,1,0:T(8,128)(2,1)S(1)}, u32[]{:S(2)}, u32[]{:S(2)}) collective-permute-start(bf16[16,64,128]{2,1,0:T(8,128)(2,1)S(1)} %get-tuple-element.14), channel_id=1, source_target_pairs={{0,192},{64,0},{128,64},{192,128},{1,193},{65,1},{129,65},{193,129... | collective-permute-start | bytes 786440 | tf_op jit(solution)/shard_map/ppermute | solution.py:189
  18.9 0.5 collective-permute-start.1
  19.5 0.6 collective-permute-start
  20.7 0.6 stack.84.place
  21.3 3.5 %collective-permute-done.5.high = bf16[8,2,128,256]{3,2,1,0:T(8,128)(2,1)} collective-permute-done((bf16[8,2,128,256]{3,2,1,0:T(8,128)(2,1)}, bf16[8,2,128,256]{3,2,1,0:T(8,128)(2,1)}, u32[]{:S(2)}, u32[]{:S(2)}) %collective-permute-start.5) | collective-permute-done | bytes 1048608 | tf_op jit(solution)/shard_map/ppermute | solution.py:215
  24.8 0.9 collective-permute-done.4.low
  25.7 7.6 %products.1 = (bf16[4,8,48,256]{3,2,1,0:T(8,128)(2,1)}, bf16[4,8,48,256]{3,2,1,0:T(8,128)(2,1)}) custom-call(s32[5]{0:T(128)} %stack.84.place, s32[8,6]{1,0:T(8,128)} %pattern.1, s32[256]{0:T(256)} %live.1, f32[1]{0:T(128)S(6)} %copy.15.weight, bf16[8,2,128,256]{3,2,1,0:T(8,128)(2,1)} %collective-permute-done.4.low, bf16[8,2,128,256]{3,2,1,0:T(8,128)(2,1)} %bitcast.77, ...), custom_call_target="tpu_custom_call" | custom-call | flops 1600000000 | bytes 9000000 | tf_op jit(solution)/shard_map/products/pallas_call | solution.py:89
  33.3 3.9 %collective-permute-start.6 = (bf16[4,8,48,256]{3,2,1,0:T(8,128)(2,1)}, bf16[4,8,48,256]{3,2,1,0:T(8,128)(2,1)S(1)}, u32[]{:S(2)}, u32[]{:S(2)}) collective-permute-start(bf16[4,8,48,256]{3,2,1,0:T(8,128)(2,1)} %get-tuple-element.16), channel_id=1, source_target_pairs={{0,32},{32,0},{1,33},{33,1},{2,34},{34,2},{3,35},{35,3},{4,36},{36... | collective-permute-start | bytes 2359304 | tf_op jit(solution)/shard_map/ppermute | solution.py:224
  37.2 4.0 %collective-permute-done.2 = bf16[16,64,128]{2,1,0:T(8,128)(2,1)S(1)} collective-permute-done((bf16[16,64,128]{2,1,0:T(8,128)(2,1)S(1)}, bf16[16,64,128]{2,1,0:T(8,128)(2,1)S(1)}, u32[]{:S(2)}, u32[]{:S(2)}) %collective-permute-start.2) | collective-permute-done | bytes 262176 | tf_op jit(solution)/shard_map/ppermute | solution.py:189
  41.2 1.5 %collective-permute-done.1 = bf16[16,64,128]{2,1,0:T(8,128)(2,1)S(1)} collective-permute-done((bf16[16,64,128]{2,1,0:T(8,128)(2,1)S(1)}, bf16[16,64,128]{2,1,0:T(8,128)(2,1)S(1)}, u32[]{:S(2)}, u32[]{:S(2)}) %collective-permute-start.1) | collective-permute-done | bytes 262176 | tf_op jit(solution)/shard_map/ppermute | solution.py:189
  42.7 5.5 %collective-permute-done = bf16[16,64,128]{2,1,0:T(8,128)(2,1)S(1)} collective-permute-done((bf16[16,64,128]{2,1,0:T(8,128)(2,1)S(1)}, bf16[16,64,128]{2,1,0:T(8,128)(2,1)S(1)}, u32[]{:S(2)}, u32[]{:S(2)}) %collective-permute-start) | collective-permute-done | bytes 262176 | tf_op jit(solution)/shard_map/ppermute | solution.py:189
  48.2 1.1 copy-done.1
  49.3 0.7 pair_sums.1
  50.1 0.5 collective-permute-start.7
  50.6 1.8 %collective-permute-start.8 = (bf16[8,48,256]{2,1,0:T(8,128)(2,1)S(1)}, bf16[8,48,256]{2,1,0:T(8,128)(2,1)S(1)}, u32[]{:S(2)}, u32[]{:S(2)}) collective-permute-start(bf16[8,48,256]{2,1,0:T(8,128)(2,1)S(1)} %get-tuple-element.19), channel_id=1, source_target_pairs={{0,128},{64,192},{128,0},{192,64},{1,129},{65,193},{129,1},{193,65... | collective-permute-start | bytes 589832 | tf_op jit(solution)/shard_map/ppermute | solution.py:189
  52.4 0.7 collective-permute-start.9
  53.2 1.5 %collective-permute-start.3 = (bf16[4,16,64,128]{3,2,1,0:T(8,128)(2,1)S(1)}, bf16[4,16,64,128]{3,2,1,0:T(8,128)(2,1)S(1)}, u32[]{:S(2)}, u32[]{:S(2)}) collective-permute-start(bf16[4,16,64,128]{3,2,1,0:T(8,128)(2,1)S(1)} %pad_maximum_fusion.own_o), channel_id=1, source_target_pairs={{0,32},{32,0},{1,33},{33,1},{2,34},{34,2},{3,35},{35,3},{4,36},{36... | collective-permute-start | bytes 3145736 | tf_op jit(solution)/shard_map/ppermute | solution.py:219
  54.7 3.0 %collective-permute-done.7 = bf16[8,48,256]{2,1,0:T(8,128)(2,1)S(1)} collective-permute-done((bf16[8,48,256]{2,1,0:T(8,128)(2,1)S(1)}, bf16[8,48,256]{2,1,0:T(8,128)(2,1)S(1)}, u32[]{:S(2)}, u32[]{:S(2)}) %collective-permute-start.7) | collective-permute-done | bytes 196640 | tf_op jit(solution)/shard_map/ppermute | solution.py:189
  57.7 3.0 %collective-permute-done.8 = bf16[8,48,256]{2,1,0:T(8,128)(2,1)S(1)} collective-permute-done((bf16[8,48,256]{2,1,0:T(8,128)(2,1)S(1)}, bf16[8,48,256]{2,1,0:T(8,128)(2,1)S(1)}, u32[]{:S(2)}, u32[]{:S(2)}) %collective-permute-start.8) | collective-permute-done | bytes 196640 | tf_op jit(solution)/shard_map/ppermute | solution.py:189
  60.7 1.2 collective-permute-done.9
  62.3 4.9 %collective-permute-start.25 = (bf16[3,48,256]{2,1,0:T(8,128)(2,1)S(1)}, bf16[3,48,256]{2,1,0:T(8,128)(2,1)S(1)}, u32[]{:S(2)}, u32[]{:S(2)}) collective-permute-start(bf16[3,48,256]{2,1,0:T(8,128)(2,1)S(1)} %slice.47), channel_id=1, source_target_pairs={{0,28},{4,0},{8,4},{12,8},{16,12},{20,16},{24,20},{28,24},{1,29},{... | collective-permute-start | bytes 221192 | tf_op jit(solution)/shard_map/ppermute | solution.py:189
  67.2 2.6 %collective-permute-start.11 = (bf16[5,48,256]{2,1,0:T(8,128)(2,1)S(1)}, bf16[5,48,256]{2,1,0:T(8,128)(2,1)S(1)}, u32[]{:S(2)}, u32[]{:S(2)}) collective-permute-start(bf16[5,48,256]{2,1,0:T(8,128)(2,1)S(1)} %get-tuple-element.22), channel_id=1, source_target_pairs={{0,2},{1,3},{2,0},{3,1},{4,6},{5,7},{6,4},{7,5},{8,10},{9,11},{10,... | collective-permute-start | bytes 368648 | tf_op jit(solution)/shard_map/ppermute | solution.py:189
  69.9 2.7 %collective-permute-start.12 = (bf16[5,48,256]{2,1,0:T(8,128)(2,1)S(1)}, bf16[5,48,256]{2,1,0:T(8,128)(2,1)S(1)}, u32[]{:S(2)}, u32[]{:S(2)}) collective-permute-start(bf16[5,48,256]{2,1,0:T(8,128)(2,1)S(1)} %get-tuple-element.22), channel_id=1, source_target_pairs={{0,3},{1,0},{2,1},{3,2},{4,7},{5,4},{6,5},{7,6},{8,11},{9,8},{10,9... | collective-permute-start | bytes 368648 | tf_op jit(solution)/shard_map/ppermute | solution.py:189
  72.7 2.7 %collective-permute-start.26 = (bf16[3,48,256]{2,1,0:T(8,128)(2,1)S(1)}, bf16[3,48,256]{2,1,0:T(8,128)(2,1)S(1)}, u32[]{:S(2)}, u32[]{:S(2)}) collective-permute-start(bf16[3,48,256]{2,1,0:T(8,128)(2,1)S(1)} %collective-permute-done.25), channel_id=1, source_target_pairs={{0,28},{4,0},{8,4},{12,8},{16,12},{20,16},{24,20},{28,24},{1,29},{... | collective-permute-start | bytes 221192 | tf_op jit(solution)/shard_map/ppermute | solution.py:189
  75.4 0.7 collective-permute-done.10
  76.2 1.6 %collective-permute-start.17 = (bf16[4,5,48,256]{3,2,1,0:T(8,128)(2,1)S(1)}, bf16[4,5,48,256]{3,2,1,0:T(8,128)(2,1)S(1)}, u32[]{:S(2)}, u32[]{:S(2)}) collective-permute-start(bf16[4,5,48,256]{3,2,1,0:T(8,128)(2,1)S(1)} %pad_maximum_fusion.1), channel_id=1, source_target_pairs={{0,28},{4,0},{8,4},{12,8},{16,12},{20,16},{24,20},{28,24},{1,29},{... | collective-permute-start | bytes 1474568 | tf_op jit(solution)/shard_map/ppermute | solution.py:189
  78.0 2.6 %collective-permute-start.27 = (bf16[3,48,256]{2,1,0:T(8,128)(2,1)S(1)}, bf16[3,48,256]{2,1,0:T(8,128)(2,1)S(1)}, u32[]{:S(2)}, u32[]{:S(2)}) collective-permute-start(bf16[3,48,256]{2,1,0:T(8,128)(2,1)S(1)} %collective-permute-done.26), channel_id=1, source_target_pairs={{0,28},{4,0},{8,4},{12,8},{16,12},{20,16},{24,20},{28,24},{1,29},{... | collective-permute-start | bytes 221192 | tf_op jit(solution)/shard_map/ppermute | solution.py:189
  80.6 10.2 %collective-permute-done.23 = bf16[3,48,256]{2,1,0:T(8,128)(2,1)S(1)} collective-permute-done((bf16[3,48,256]{2,1,0:T(8,128)(2,1)S(1)}, bf16[3,48,256]{2,1,0:T(8,128)(2,1)S(1)}, u32[]{:S(2)}, u32[]{:S(2)}) %collective-permute-start.23) | collective-permute-done | bytes 73760 | tf_op jit(solution)/shard_map/ppermute | solution.py:189
  90.8 4.4 %collective-permute-done.24 = bf16[3,48,256]{2,1,0:T(8,128)(2,1)S(1)} collective-permute-done((bf16[3,48,256]{2,1,0:T(8,128)(2,1)S(1)}, bf16[3,48,256]{2,1,0:T(8,128)(2,1)S(1)}, u32[]{:S(2)}, u32[]{:S(2)}) %collective-permute-start.24) | collective-permute-done | bytes 73760 | tf_op jit(solution)/shard_map/ppermute | solution.py:189
  95.4 1.4 collective-permute-start.14
  96.8 2.6 %collective-permute-start.30 = (bf16[8,3,48,256]{3,2,1,0:T(8,128)(2,1)S(1)}, bf16[8,3,48,256]{3,2,1,0:T(8,128)(2,1)S(1)}, u32[]{:S(2)}, u32[]{:S(2)}) collective-permute-start(bf16[8,3,48,256]{3,2,1,0:T(8,128)(2,1)S(1)} %bitcast_dynamic-update-slice_fusion), channel_id=1, source_target_pairs={{0,3},{1,0},{2,1},{3,2},{4,7},{5,4},{6,5},{7,6},{8,11},{9,8},{10,9... | collective-permute-start | bytes 1769480 | tf_op jit(solution)/shard_map/ppermute | solution.py:189
  99.4 4.0 %collective-permute-done.18 = bf16[4,5,48,256]{3,2,1,0:T(8,128)(2,1)S(1)} collective-permute-done((bf16[4,5,48,256]{3,2,1,0:T(8,128)(2,1)S(1)}, bf16[4,5,48,256]{3,2,1,0:T(8,128)(2,1)S(1)}, u32[]{:S(2)}, u32[]{:S(2)}) %collective-permute-start.18) | collective-permute-done | bytes 491552 | tf_op jit(solution)/shard_map/ppermute | solution.py:189
  103.4 1.5 collective-permute-start.19
  104.9 1.6 %collective-permute-done.30 = bf16[8,3,48,256]{3,2,1,0:T(8,128)(2,1)S(1)} collective-permute-done((bf16[8,3,48,256]{3,2,1,0:T(8,128)(2,1)S(1)}, bf16[8,3,48,256]{3,2,1,0:T(8,128)(2,1)S(1)}, u32[]{:S(2)}, u32[]{:S(2)}) %collective-permute-start.30) | collective-permute-done | bytes 589856 | tf_op jit(solution)/shard_map/ppermute | solution.py:189
  106.5 3.2 %collective-permute-start.31 = (bf16[4,3,48,256]{3,2,1,0:T(8,128)(2,1)S(1)}, bf16[4,3,48,256]{3,2,1,0:T(8,128)(2,1)S(1)}, u32[]{:S(2)}, u32[]{:S(2)}) collective-permute-start(bf16[4,3,48,256]{3,2,1,0:T(8,128)(2,1)S(1)} %slice.49), channel_id=1, source_target_pairs={{0,3},{1,0},{2,1},{3,2},{4,7},{5,4},{6,5},{7,6},{8,11},{9,8},{10,9... | collective-permute-start | bytes 884744 | tf_op jit(solution)/shard_map/ppermute | solution.py:189
  109.9 4.0 %collective-permute-done.19 = bf16[4,5,48,256]{3,2,1,0:T(8,128)(2,1)S(1)} collective-permute-done((bf16[4,5,48,256]{3,2,1,0:T(8,128)(2,1)S(1)}, bf16[4,5,48,256]{3,2,1,0:T(8,128)(2,1)S(1)}, u32[]{:S(2)}, u32[]{:S(2)}) %collective-permute-start.19) | collective-permute-done | bytes 491552 | tf_op jit(solution)/shard_map/ppermute | solution.py:189
  113.9 1.3 collective-permute-start.20
  115.7 3.7 %collective-permute-done.29 = bf16[4,3,48,256]{3,2,1,0:T(8,128)(2,1)S(1)} collective-permute-done((bf16[4,3,48,256]{3,2,1,0:T(8,128)(2,1)S(1)}, bf16[4,3,48,256]{3,2,1,0:T(8,128)(2,1)S(1)}, u32[]{:S(2)}, u32[]{:S(2)}) %collective-permute-start.29) | collective-permute-done | bytes 294944 | tf_op jit(solution)/shard_map/ppermute | solution.py:189
  119.4 2.6 %collective-permute-done.20 = bf16[2,5,48,256]{3,2,1,0:T(8,128)(2,1)S(1)} collective-permute-done((bf16[2,5,48,256]{3,2,1,0:T(8,128)(2,1)S(1)}, bf16[2,5,48,256]{3,2,1,0:T(8,128)(2,1)S(1)}, u32[]{:S(2)}, u32[]{:S(2)}) %collective-permute-start.20) | collective-permute-done | bytes 245792 | tf_op jit(solution)/shard_map/ppermute | solution.py:189
  122.0 1.7 %collective-permute-done.16 = bf16[2,5,48,256]{3,2,1,0:T(8,128)(2,1)S(1)} collective-permute-done((bf16[2,5,48,256]{3,2,1,0:T(8,128)(2,1)S(1)}, bf16[2,5,48,256]{3,2,1,0:T(8,128)(2,1)S(1)}, u32[]{:S(2)}, u32[]{:S(2)}) %collective-permute-start.16) | collective-permute-done | bytes 245792 | tf_op jit(solution)/shard_map/ppermute | solution.py:189
  123.7 9.5 %applied_sums.1 = f32[8,4,128]{2,1,0:T(4,128)S(1)} custom-call(s32[5]{0:T(128)S(1)} %copy-done.4, s32[4096]{0:T(1024)S(1)} %bitcast.65, s32[4096]{0:T(1024)S(1)} %copy-done.3, bf16[8,16,48,128]{3,2,1,0:T(8,128)(2,1)S(1)} %all-to-all-done.vals_q, bf16[4,16,64,128]{3,2,1,0:T(8,128)(2,1)S(1)} %pad_maximum_fusion.own_o, ...), custom_call_target="tpu_custom_call" | custom-call | flops 400000000 | bytes 8000000 | tf_op jit(solution)/shard_map/applied_sums/pallas_call | solution.py:172
  133.2 16.4 %all_to_all.10 = f32[8,4,128]{2,1,0:T(4,128)S(1)} all-to-all(f32[8,4,128]{2,1,0:T(4,128)S(1)} %applied_sums.1), channel_id=1, replica_groups=mesh['y'=4,'core'=2,'z'=8,'x'=4] {'y','core'}, dimensions={0} | all-to-all | bytes 32768 | tf_op jit(solution)/shard_map/all_to_all | solution.py:245
  149.7 0.6 reduce_sum.9
  (55 shorter events, 1.6 us)
Async XLA Ops:
  0.0 24.8 %collective-permute-start.5 = (bf16[8,2,128,256]{3,2,1,0:T(8,128)(2,1)}, bf16[8,2,128,256]{3,2,1,0:T(8,128)(2,1)}, u32[]{:S(2)}, u32[]{:S(2)}) collective-permute-start(bf16[8,2,128,256]{3,2,1,0:T(8,128)(2,1)} %bitcast.75), channel_id=1, source_target_pairs={{1,0},{2,1},{3,2},{4,3},{5,4},{6,5},{7,6},{8,7},{9,8},{10,9},{11,1... | collective-permute-start | bytes 3145736 | tf_op jit(solution)/shard_map/ppermute | solution.py:215
  1.3 24.4 %collective-permute-start.4 = (bf16[8,2,128,256]{3,2,1,0:T(8,128)(2,1)}, bf16[8,2,128,256]{3,2,1,0:T(8,128)(2,1)}, u32[]{:S(2)}, u32[]{:S(2)}) collective-permute-start(bf16[8,2,128,256]{3,2,1,0:T(8,128)(2,1)} %bitcast.76), channel_id=1, source_target_pairs={{0,1},{1,2},{2,3},{3,4},{4,5},{5,6},{6,7},{7,8},{8,9},{9,10},{10,1... | collective-permute-start | bytes 3145736 | tf_op jit(solution)/shard_map/ppermute | solution.py:214
  6.9 1.4 copy-start
  9.6 38.6 %all-to-all-start = ((bf16[8,16,48,128]{3,2,1,0:T(8,128)(2,1)}), bf16[8,16,48,128]{3,2,1,0:T(8,128)(2,1)S(1)}, u32[]{:S(2)}, u32[]{:S(2)}) async-start(bf16[8,16,48,128]{3,2,1,0:T(8,128)(2,1)} %get-tuple-element.13), calls=%async_computation | async-start | bytes 3145728 | tf_op jit(solution)/shard_map/all_to_all | solution.py:220
  16.3 24.9 %collective-permute-start.2 = (bf16[16,64,128]{2,1,0:T(8,128)(2,1)S(1)}, bf16[16,64,128]{2,1,0:T(8,128)(2,1)S(1)}, u32[]{:S(2)}, u32[]{:S(2)}) collective-permute-start(bf16[16,64,128]{2,1,0:T(8,128)(2,1)S(1)} %get-tuple-element.14), channel_id=1, source_target_pairs={{0,192},{64,0},{128,64},{192,128},{1,193},{65,1},{129,65},{193,129... | collective-permute-start | bytes 786440 | tf_op jit(solution)/shard_map/ppermute | solution.py:189
  18.9 23.8 %collective-permute-start.1 = (bf16[16,64,128]{2,1,0:T(8,128)(2,1)S(1)}, bf16[16,64,128]{2,1,0:T(8,128)(2,1)S(1)}, u32[]{:S(2)}, u32[]{:S(2)}) collective-permute-start(bf16[16,64,128]{2,1,0:T(8,128)(2,1)S(1)} %get-tuple-element.14), channel_id=1, source_target_pairs={{0,128},{64,192},{128,0},{192,64},{1,129},{65,193},{129,1},{193,65... | collective-permute-start | bytes 786440 | tf_op jit(solution)/shard_map/ppermute | solution.py:189
  19.5 28.7 %collective-permute-start = (bf16[16,64,128]{2,1,0:T(8,128)(2,1)S(1)}, bf16[16,64,128]{2,1,0:T(8,128)(2,1)S(1)}, u32[]{:S(2)}, u32[]{:S(2)}) collective-permute-start(bf16[16,64,128]{2,1,0:T(8,128)(2,1)S(1)} %get-tuple-element.14), channel_id=1, source_target_pairs={{0,64},{64,128},{128,192},{192,0},{1,65},{65,129},{129,193},{193,1... | collective-permute-start | bytes 786440 | tf_op jit(solution)/shard_map/ppermute | solution.py:189
  21.3 26.9 %copy-start.4 = (s32[5]{0:T(128)S(1)}, s32[5]{0:T(128)}, u32[]{:S(2)}) copy-start(s32[5]{0:T(128)} %stack.84.place) | copy-start | bytes 64
  33.3 14.9 %collective-permute-start.6 = (bf16[4,8,48,256]{3,2,1,0:T(8,128)(2,1)}, bf16[4,8,48,256]{3,2,1,0:T(8,128)(2,1)S(1)}, u32[]{:S(2)}, u32[]{:S(2)}) collective-permute-start(bf16[4,8,48,256]{3,2,1,0:T(8,128)(2,1)} %get-tuple-element.16), channel_id=1, source_target_pairs={{0,32},{32,0},{1,33},{33,1},{2,34},{34,2},{3,35},{35,3},{4,36},{36... | collective-permute-start | bytes 2359304 | tf_op jit(solution)/shard_map/ppermute | solution.py:224
  48.2 1.1 copy-start.1
  50.1 7.7 %collective-permute-start.7 = (bf16[8,48,256]{2,1,0:T(8,128)(2,1)S(1)}, bf16[8,48,256]{2,1,0:T(8,128)(2,1)S(1)}, u32[]{:S(2)}, u32[]{:S(2)}) collective-permute-start(bf16[8,48,256]{2,1,0:T(8,128)(2,1)S(1)} %get-tuple-element.18), channel_id=1, source_target_pairs={{0,64},{64,128},{128,192},{192,0},{1,65},{65,129},{129,193},{193,1... | collective-permute-start | bytes 589832 | tf_op jit(solution)/shard_map/ppermute | solution.py:189
  50.6 10.1 %collective-permute-start.8 = (bf16[8,48,256]{2,1,0:T(8,128)(2,1)S(1)}, bf16[8,48,256]{2,1,0:T(8,128)(2,1)S(1)}, u32[]{:S(2)}, u32[]{:S(2)}) collective-permute-start(bf16[8,48,256]{2,1,0:T(8,128)(2,1)S(1)} %get-tuple-element.19), channel_id=1, source_target_pairs={{0,128},{64,192},{128,0},{192,64},{1,129},{65,193},{129,1},{193,65... | collective-permute-start | bytes 589832 | tf_op jit(solution)/shard_map/ppermute | solution.py:189
  52.4 9.6 %collective-permute-start.9 = (bf16[8,48,256]{2,1,0:T(8,128)(2,1)S(1)}, bf16[8,48,256]{2,1,0:T(8,128)(2,1)S(1)}, u32[]{:S(2)}, u32[]{:S(2)}) collective-permute-start(bf16[8,48,256]{2,1,0:T(8,128)(2,1)S(1)} %get-tuple-element.20), channel_id=1, source_target_pairs={{0,192},{64,0},{128,64},{192,128},{1,193},{65,1},{129,65},{193,129... | collective-permute-start | bytes 589832 | tf_op jit(solution)/shard_map/ppermute | solution.py:189
  53.2 62.3 %collective-permute-start.3 = (bf16[4,16,64,128]{3,2,1,0:T(8,128)(2,1)S(1)}, bf16[4,16,64,128]{3,2,1,0:T(8,128)(2,1)S(1)}, u32[]{:S(2)}, u32[]{:S(2)}) collective-permute-start(bf16[4,16,64,128]{3,2,1,0:T(8,128)(2,1)S(1)} %pad_maximum_fusion.own_o), channel_id=1, source_target_pairs={{0,32},{32,0},{1,33},{33,1},{2,34},{34,2},{3,35},{35,3},{4,36},{36... | collective-permute-start | bytes 3145736 | tf_op jit(solution)/shard_map/ppermute | solution.py:219
  62.0 7.8 %collective-permute-start.21 = (bf16[3,48,256]{2,1,0:T(8,128)(2,1)S(1)}, bf16[3,48,256]{2,1,0:T(8,128)(2,1)S(1)}, u32[]{:S(2)}, u32[]{:S(2)}) collective-permute-start(bf16[3,48,256]{2,1,0:T(8,128)(2,1)S(1)} %slice.47), channel_id=1, source_target_pairs={{0,4},{4,8},{8,12},{12,16},{16,20},{20,24},{24,28},{28,0},{1,5},{5... | collective-permute-start | bytes 221192 | tf_op jit(solution)/shard_map/ppermute | solution.py:189
  62.3 10.3 %collective-permute-start.25 = (bf16[3,48,256]{2,1,0:T(8,128)(2,1)S(1)}, bf16[3,48,256]{2,1,0:T(8,128)(2,1)S(1)}, u32[]{:S(2)}, u32[]{:S(2)}) collective-permute-start(bf16[3,48,256]{2,1,0:T(8,128)(2,1)S(1)} %slice.47), channel_id=1, source_target_pairs={{0,28},{4,0},{8,4},{12,8},{16,12},{20,16},{24,20},{28,24},{1,29},{... | collective-permute-start | bytes 221192 | tf_op jit(solution)/shard_map/ppermute | solution.py:189
  67.2 5.5 %collective-permute-start.11 = (bf16[5,48,256]{2,1,0:T(8,128)(2,1)S(1)}, bf16[5,48,256]{2,1,0:T(8,128)(2,1)S(1)}, u32[]{:S(2)}, u32[]{:S(2)}) collective-permute-start(bf16[5,48,256]{2,1,0:T(8,128)(2,1)S(1)} %get-tuple-element.22), channel_id=1, source_target_pairs={{0,2},{1,3},{2,0},{3,1},{4,6},{5,7},{6,4},{7,5},{8,10},{9,11},{10,... | collective-permute-start | bytes 368648 | tf_op jit(solution)/shard_map/ppermute | solution.py:189
  69.8 6.3 %collective-permute-start.10 = (bf16[5,48,256]{2,1,0:T(8,128)(2,1)S(1)}, bf16[5,48,256]{2,1,0:T(8,128)(2,1)S(1)}, u32[]{:S(2)}, u32[]{:S(2)}) collective-permute-start(bf16[5,48,256]{2,1,0:T(8,128)(2,1)S(1)} %get-tuple-element.22), channel_id=1, source_target_pairs={{0,1},{1,2},{2,3},{3,0},{4,5},{5,6},{6,7},{7,4},{8,9},{9,10},{10,1... | collective-permute-start | bytes 368648 | tf_op jit(solution)/shard_map/ppermute | solution.py:189
  69.9 6.2 %collective-permute-start.12 = (bf16[5,48,256]{2,1,0:T(8,128)(2,1)S(1)}, bf16[5,48,256]{2,1,0:T(8,128)(2,1)S(1)}, u32[]{:S(2)}, u32[]{:S(2)}) collective-permute-start(bf16[5,48,256]{2,1,0:T(8,128)(2,1)S(1)} %get-tuple-element.22), channel_id=1, source_target_pairs={{0,3},{1,0},{2,1},{3,2},{4,7},{5,4},{6,5},{7,6},{8,11},{9,8},{10,9... | collective-permute-start | bytes 368648 | tf_op jit(solution)/shard_map/ppermute | solution.py:189
  72.6 5.3 %collective-permute-start.22 = (bf16[3,48,256]{2,1,0:T(8,128)(2,1)S(1)}, bf16[3,48,256]{2,1,0:T(8,128)(2,1)S(1)}, u32[]{:S(2)}, u32[]{:S(2)}) collective-permute-start(bf16[3,48,256]{2,1,0:T(8,128)(2,1)S(1)} %collective-permute-done.21), channel_id=1, source_target_pairs={{0,4},{4,8},{8,12},{12,16},{16,20},{20,24},{24,28},{28,0},{1,5},{5... | collective-permute-start | bytes 221192 | tf_op jit(solution)/shard_map/ppermute | solution.py:189
  72.7 5.2 %collective-permute-start.26 = (bf16[3,48,256]{2,1,0:T(8,128)(2,1)S(1)}, bf16[3,48,256]{2,1,0:T(8,128)(2,1)S(1)}, u32[]{:S(2)}, u32[]{:S(2)}) collective-permute-start(bf16[3,48,256]{2,1,0:T(8,128)(2,1)S(1)} %collective-permute-done.25), channel_id=1, source_target_pairs={{0,28},{4,0},{8,4},{12,8},{16,12},{20,16},{24,20},{28,24},{1,29},{... | collective-permute-start | bytes 221192 | tf_op jit(solution)/shard_map/ppermute | solution.py:189
  76.2 47.5 %copy-start.2 = (s32[4096,1]{0,1:T(1,128)S(1)}, s32[4096,1]{0,1:T(1,128)}, u32[]{:S(2)}) copy-start(s32[4096,1]{0,1:T(1,128)} %param.11) | copy-start | bytes 49156
  76.2 47.5 %copy-start.3 = (s32[4096]{0:T(1024)S(1)}, s32[4096]{0:T(1024)}, u32[]{:S(2)}) copy-start(s32[4096]{0:T(1024)} %local.1) | copy-start | bytes 49156
  76.2 19.1 %collective-permute-start.17 = (bf16[4,5,48,256]{3,2,1,0:T(8,128)(2,1)S(1)}, bf16[4,5,48,256]{3,2,1,0:T(8,128)(2,1)S(1)}, u32[]{:S(2)}, u32[]{:S(2)}) collective-permute-start(bf16[4,5,48,256]{3,2,1,0:T(8,128)(2,1)S(1)} %pad_maximum_fusion.1), channel_id=1, source_target_pairs={{0,28},{4,0},{8,4},{12,8},{16,12},{20,16},{24,20},{28,24},{1,29},{... | collective-permute-start | bytes 1474568 | tf_op jit(solution)/shard_map/ppermute | solution.py:189
  77.8 17.5 %collective-permute-start.13 = (bf16[4,5,48,256]{3,2,1,0:T(8,128)(2,1)S(1)}, bf16[4,5,48,256]{3,2,1,0:T(8,128)(2,1)S(1)}, u32[]{:S(2)}, u32[]{:S(2)}) collective-permute-start(bf16[4,5,48,256]{3,2,1,0:T(8,128)(2,1)S(1)} %pad_maximum_fusion.1), channel_id=1, source_target_pairs={{0,4},{4,8},{8,12},{12,16},{16,20},{20,24},{24,28},{28,0},{1,5},{5... | collective-permute-start | bytes 1474568 | tf_op jit(solution)/shard_map/ppermute | solution.py:189
  77.9 12.9 %collective-permute-start.23 = (bf16[3,48,256]{2,1,0:T(8,128)(2,1)S(1)}, bf16[3,48,256]{2,1,0:T(8,128)(2,1)S(1)}, u32[]{:S(2)}, u32[]{:S(2)}) collective-permute-start(bf16[3,48,256]{2,1,0:T(8,128)(2,1)S(1)} %collective-permute-done.22), channel_id=1, source_target_pairs={{0,4},{4,8},{8,12},{12,16},{16,20},{20,24},{24,28},{28,0},{1,5},{5... | collective-permute-start | bytes 221192 | tf_op jit(solution)/shard_map/ppermute | solution.py:189
  78.0 17.3 %collective-permute-start.27 = (bf16[3,48,256]{2,1,0:T(8,128)(2,1)S(1)}, bf16[3,48,256]{2,1,0:T(8,128)(2,1)S(1)}, u32[]{:S(2)}, u32[]{:S(2)}) collective-permute-start(bf16[3,48,256]{2,1,0:T(8,128)(2,1)S(1)} %collective-permute-done.26), channel_id=1, source_target_pairs={{0,28},{4,0},{8,4},{12,8},{16,12},{20,16},{24,20},{28,24},{1,29},{... | collective-permute-start | bytes 221192 | tf_op jit(solution)/shard_map/ppermute | solution.py:189
  90.8 4.4 %collective-permute-start.24 = (bf16[3,48,256]{2,1,0:T(8,128)(2,1)S(1)}, bf16[3,48,256]{2,1,0:T(8,128)(2,1)S(1)}, u32[]{:S(2)}, u32[]{:S(2)}) collective-permute-start(bf16[3,48,256]{2,1,0:T(8,128)(2,1)S(1)} %collective-permute-done.23), channel_id=1, source_target_pairs={{0,4},{4,8},{8,12},{12,16},{16,20},{20,24},{24,28},{28,0},{1,5},{5... | collective-permute-start | bytes 221192 | tf_op jit(solution)/shard_map/ppermute | solution.py:189
  95.3 8.1 %collective-permute-start.18 = (bf16[4,5,48,256]{3,2,1,0:T(8,128)(2,1)S(1)}, bf16[4,5,48,256]{3,2,1,0:T(8,128)(2,1)S(1)}, u32[]{:S(2)}, u32[]{:S(2)}) collective-permute-start(bf16[4,5,48,256]{3,2,1,0:T(8,128)(2,1)S(1)} %collective-permute-done.17), channel_id=1, source_target_pairs={{0,28},{4,0},{8,4},{12,8},{16,12},{20,16},{24,20},{28,24},{1,29},{... | collective-permute-start | bytes 1474568 | tf_op jit(solution)/shard_map/ppermute | solution.py:189
  95.4 9.5 %collective-permute-start.14 = (bf16[4,5,48,256]{3,2,1,0:T(8,128)(2,1)S(1)}, bf16[4,5,48,256]{3,2,1,0:T(8,128)(2,1)S(1)}, u32[]{:S(2)}, u32[]{:S(2)}) collective-permute-start(bf16[4,5,48,256]{3,2,1,0:T(8,128)(2,1)S(1)} %collective-permute-done.13), channel_id=1, source_target_pairs={{0,4},{4,8},{8,12},{12,16},{16,20},{20,24},{24,28},{28,0},{1,5},{5... | collective-permute-start | bytes 1474568 | tf_op jit(solution)/shard_map/ppermute | solution.py:189
  96.8 9.7 %collective-permute-start.30 = (bf16[8,3,48,256]{3,2,1,0:T(8,128)(2,1)S(1)}, bf16[8,3,48,256]{3,2,1,0:T(8,128)(2,1)S(1)}, u32[]{:S(2)}, u32[]{:S(2)}) collective-permute-start(bf16[8,3,48,256]{3,2,1,0:T(8,128)(2,1)S(1)} %bitcast_dynamic-update-slice_fusion), channel_id=1, source_target_pairs={{0,3},{1,0},{2,1},{3,2},{4,7},{5,4},{6,5},{7,6},{8,11},{9,8},{10,9... | collective-permute-start | bytes 1769480 | tf_op jit(solution)/shard_map/ppermute | solution.py:189
  99.4 10.3 %collective-permute-start.28 = (bf16[8,3,48,256]{3,2,1,0:T(8,128)(2,1)S(1)}, bf16[8,3,48,256]{3,2,1,0:T(8,128)(2,1)S(1)}, u32[]{:S(2)}, u32[]{:S(2)}) collective-permute-start(bf16[8,3,48,256]{3,2,1,0:T(8,128)(2,1)S(1)} %bitcast_dynamic-update-slice_fusion), channel_id=1, source_target_pairs={{0,1},{1,2},{2,3},{3,0},{4,5},{5,6},{6,7},{7,4},{8,9},{9,10},{10,1... | collective-permute-start | bytes 1769480 | tf_op jit(solution)/shard_map/ppermute | solution.py:189
  103.4 10.5 %collective-permute-start.19 = (bf16[4,5,48,256]{3,2,1,0:T(8,128)(2,1)S(1)}, bf16[4,5,48,256]{3,2,1,0:T(8,128)(2,1)S(1)}, u32[]{:S(2)}, u32[]{:S(2)}) collective-permute-start(bf16[4,5,48,256]{3,2,1,0:T(8,128)(2,1)S(1)} %collective-permute-done.18), channel_id=1, source_target_pairs={{0,28},{4,0},{8,4},{12,8},{16,12},{20,16},{24,20},{28,24},{1,29},{... | collective-permute-start | bytes 1474568 | tf_op jit(solution)/shard_map/ppermute | solution.py:189
  104.9 10.3 %collective-permute-start.15 = (bf16[4,5,48,256]{3,2,1,0:T(8,128)(2,1)S(1)}, bf16[4,5,48,256]{3,2,1,0:T(8,128)(2,1)S(1)}, u32[]{:S(2)}, u32[]{:S(2)}) collective-permute-start(bf16[4,5,48,256]{3,2,1,0:T(8,128)(2,1)S(1)} %collective-permute-done.14), channel_id=1, source_target_pairs={{0,4},{4,8},{8,12},{12,16},{16,20},{20,24},{24,28},{28,0},{1,5},{5... | collective-permute-start | bytes 1474568 | tf_op jit(solution)/shard_map/ppermute | solution.py:189
  106.5 9.2 %collective-permute-start.31 = (bf16[4,3,48,256]{3,2,1,0:T(8,128)(2,1)S(1)}, bf16[4,3,48,256]{3,2,1,0:T(8,128)(2,1)S(1)}, u32[]{:S(2)}, u32[]{:S(2)}) collective-permute-start(bf16[4,3,48,256]{3,2,1,0:T(8,128)(2,1)S(1)} %slice.49), channel_id=1, source_target_pairs={{0,3},{1,0},{2,1},{3,2},{4,7},{5,4},{6,5},{7,6},{8,11},{9,8},{10,9... | collective-permute-start | bytes 884744 | tf_op jit(solution)/shard_map/ppermute | solution.py:189
  109.8 9.6 %collective-permute-start.29 = (bf16[4,3,48,256]{3,2,1,0:T(8,128)(2,1)S(1)}, bf16[4,3,48,256]{3,2,1,0:T(8,128)(2,1)S(1)}, u32[]{:S(2)}, u32[]{:S(2)}) collective-permute-start(bf16[4,3,48,256]{3,2,1,0:T(8,128)(2,1)S(1)} %slice.48), channel_id=1, source_target_pairs={{0,1},{1,2},{2,3},{3,0},{4,5},{5,6},{6,7},{7,4},{8,9},{9,10},{10,1... | collective-permute-start | bytes 884744 | tf_op jit(solution)/shard_map/ppermute | solution.py:189
  113.9 8.1 %collective-permute-start.20 = (bf16[2,5,48,256]{3,2,1,0:T(8,128)(2,1)S(1)}, bf16[2,5,48,256]{3,2,1,0:T(8,128)(2,1)S(1)}, u32[]{:S(2)}, u32[]{:S(2)}) collective-permute-start(bf16[2,5,48,256]{3,2,1,0:T(8,128)(2,1)S(1)} %slice.46), channel_id=1, source_target_pairs={{0,28},{4,0},{8,4},{12,8},{16,12},{20,16},{24,20},{28,24},{1,29},{... | collective-permute-start | bytes 737288 | tf_op jit(solution)/shard_map/ppermute | solution.py:189
  115.2 8.5 %collective-permute-start.16 = (bf16[2,5,48,256]{3,2,1,0:T(8,128)(2,1)S(1)}, bf16[2,5,48,256]{3,2,1,0:T(8,128)(2,1)S(1)}, u32[]{:S(2)}, u32[]{:S(2)}) collective-permute-start(bf16[2,5,48,256]{3,2,1,0:T(8,128)(2,1)S(1)} %slice.45), channel_id=1, source_target_pairs={{0,4},{4,8},{8,12},{12,16},{16,20},{20,24},{24,28},{28,0},{1,5},{5... | collective-permute-start | bytes 737288 | tf_op jit(solution)/shard_map/ppermute | solution.py:189
